TPU v7x, 32 devices: a whole 2x2x4 slice. The times are simulated.
32 devices in a mesh: fsdp: 4 (over z), ctx: 4 (over y, core), tp: 2 (over x).
Axes of the slice: x: 2, y: 2, z: 4, core: 2. Of those that a mesh axis runs over, the one named last changes fastest.
Arguments:
- block_input: bfloat16 [4, 1024, 1024], P('fsdp', 'ctx'), may hold values from -6 to 6
- input_gain: float32 [1024], replicated, may hold values from 0.5 to 1.5
- gate_proj: bfloat16 [1024, 2048], P('fsdp', 'tp'), may hold values from -0.1875 to 0.1875
- x_proj: bfloat16 [1024, 2048], P('fsdp', 'tp'), may hold values from -0.1875 to 0.1875
- bc_proj: bfloat16 [1024, 256], P('fsdp'), may hold values from -0.1875 to 0.1875
- dt_proj: bfloat16 [1024, 32], P('fsdp', 'tp'), may hold values from -0.1875 to 0.1875
- x_conv: float32 [4, 2048], P(None, 'tp'), may hold values from -3 to 3
- bc_conv: float32 [4, 256], replicated, may hold values from -3 to 3
- dt_bias: float32 [32], P('tp'), may hold values from -2 to 1
- a_log: float32 [32], P('tp'), may hold values from -11 to -2
- skip_gain: float32 [32], P('tp'), may hold values from 0.5 to 1.5
- gated_gain: float32 [2048], P('tp'), may hold values from 0.5 to 1.5
- out_proj: bfloat16 [2048, 1024], P('tp', 'fsdp'), may hold values from -0.125 to 0.125
- cotangent: bfloat16 [4, 1024, 1024], P('fsdp', 'ctx'), may hold values from -6 to 6
Outputs:
- block_output: bfloat16 [4, 1024, 1024], P('fsdp', 'ctx')
- input_grad: float32 [4, 1024, 1024], P('fsdp', 'ctx')
- grad_input_gain: float32 [1024], replicated
- grad_gate_proj: float32 [1024, 2048], P('fsdp', 'tp')
- grad_x_proj: float32 [1024, 2048], P('fsdp', 'tp')
- grad_bc_proj: float32 [1024, 256], P('fsdp')
- grad_dt_proj: float32 [1024, 32], P('fsdp', 'tp')
- grad_x_conv: float32 [4, 2048], P(None, 'tp')
- grad_bc_conv: float32 [4, 256], replicated
- grad_dt_bias: float32 [32], P('tp')
- grad_a_log: float32 [32], P('tp')
- grad_skip_gain: float32 [32], P('tp')
- grad_gated_gain: float32 [2048], P('tp')
- grad_out_proj: float32 [2048, 1024], P('tp', 'fsdp')
All inputs are finite; a program needn't handle non-finite values.
Results may differ from a plain program's by a relative error of at most 0.0098.
Values may be sent and summed in bfloat16 or wider, within the bound.
No kernel may reach another device: no remote copies, remote signals or barrier semaphores. Data moves between devices by JAX's collectives and lax.ppermute only.
A program may use at most 128 MiB of HBM per device.

v0:
```python
import jax
import jax.numpy as jnp
from jax import lax
from jax.sharding import PartitionSpec as P

EPSILON = 1e-05
FINE = lax.Precision.HIGHEST


def from_behind(block, axis, distance):
    devices = range(lax.axis_size(axis))
    route = [(i - distance, i) for i in devices if i - distance in devices]
    return lax.ppermute(block, axis, route)


def carried_in(part, axis, combine, identity, reverse):
    count = lax.axis_size(axis)
    place = lax.axis_index(axis)
    ahead = count - 1 - place if reverse else place
    gathered = jax.tree.map(lambda a: lax.all_gather(a, axis), part)
    state = jax.tree.map(lambda a, e: jnp.zeros_like(a) + jnp.asarray(e, a.dtype), part, identity)

    def one(lap, state):
        source = count - 1 - lap if reverse else lap
        return combine(
            state, jax.tree.map(lambda a: lax.dynamic_index_in_dim(a, source, 0, False), gathered)
        )

    return lax.fori_loop(0, ahead, one, state)


def combine_states(earlier, later):
    return (earlier[0] * later[0], earlier[1] * later[0][:, :, None, None] + later[1])


def silu_slope(values):
    sigmoid_value = jax.nn.sigmoid(values)
    return sigmoid_value * (1.0 + values * (1.0 - sigmoid_value))


def block_local(x_heads, b_rows, c_rows, step_size, log_decay):
    cumulative = jnp.cumsum(log_decay, axis=2)
    log_gaps = cumulative[:, :, :, None] - cumulative[:, :, None, :]
    length = log_decay.shape[2]
    causal = jnp.tril(jnp.ones((length, length), jnp.bool_))
    decays = jnp.where(causal, jnp.exp(jnp.where(causal, log_gaps, 0.0)), 0.0)
    scores = jnp.einsum("btn,bsn->bts", c_rows, b_rows, precision=FINE)
    weights = decays * scores[:, None, :, :] * step_size[:, :, None, :]
    within = jnp.einsum("bhts,bshp->bthp", weights, x_heads, precision=FINE)
    tail_decay = jnp.exp(cumulative[:, :, -1:] - cumulative) * step_size
    summary = jnp.einsum("bhs,bshp,bsn->bhpn", tail_decay, x_heads, b_rows, precision=FINE)
    return (within, summary, jnp.exp(cumulative[:, :, -1]))


def block_carry(c_rows, log_decay, state_in):
    cumulative = jnp.cumsum(log_decay, axis=2)
    carried = jnp.einsum("btn,bhpn->bthp", c_rows, state_in, precision=FINE)
    return jnp.exp(cumulative).transpose(0, 2, 1)[:, :, :, None] * carried


def back_product(grad_low, weight):
    return lax.dot_general(
        grad_low, weight, (((1,), (1,)), ((), ())), preferred_element_type=jnp.float32
    )


def on_device(
    block_input,
    input_gain,
    gate_proj,
    x_proj,
    bc_proj,
    dt_proj,
    x_conv,
    bc_conv,
    dt_bias,
    a_log,
    skip_gain,
    gated_gain,
    out_proj,
    cotangent,
):
    seqs_here, length, model_width = block_input.shape
    row_count = seqs_here * length
    inner_here = gate_proj.shape[1]
    heads_here = dt_proj.shape[1]
    head_size = inner_here // heads_here
    state_size = bc_proj.shape[1] // 2
    tap_count = x_conv.shape[0]
    full_inner = inner_here * lax.axis_size("tp")
    full_gate, full_x, full_bc, full_dt, full_out = (
        lax.all_gather(gate_proj, "fsdp", axis=0, tiled=True),
        lax.all_gather(x_proj, "fsdp", axis=0, tiled=True),
        lax.all_gather(bc_proj, "fsdp", axis=0, tiled=True),
        lax.all_gather(dt_proj, "fsdp", axis=0, tiled=True),
        lax.all_gather(out_proj, "fsdp", axis=1, tiled=True),
    )
    residual = block_input.astype(jnp.float32)
    in_scale = lax.rsqrt(jnp.mean(residual * residual, axis=-1, keepdims=True) + EPSILON)
    normed_low = (
        (residual * in_scale * input_gain).astype(jnp.bfloat16).reshape(row_count, model_width)
    )
    gate_input = jnp.dot(normed_low, full_gate, preferred_element_type=jnp.float32).reshape(
        seqs_here, length, inner_here
    )
    x_input = jnp.dot(normed_low, full_x, preferred_element_type=jnp.float32).reshape(
        seqs_here, length, inner_here
    )
    bc_input = jnp.dot(normed_low, full_bc, preferred_element_type=jnp.float32).reshape(
        seqs_here, length, 2 * state_size
    )
    dt_input = jnp.dot(normed_low, full_dt, preferred_element_type=jnp.float32).reshape(
        seqs_here, length, heads_here
    )
    conv_input = jnp.concatenate([x_input, bc_input], axis=-1)
    conv_taps = jnp.concatenate([x_conv, bc_conv], axis=-1)
    edge_rows = from_behind(conv_input[:, length - tap_count + 1 :, :], "ctx", 1)
    padded = jnp.concatenate([edge_rows, conv_input], axis=1)
    conv_out = jnp.zeros_like(conv_input)
    for offset in range(tap_count):
        conv_out = conv_out + conv_taps[offset] * padded[:, offset : offset + length, :]
    activated = jax.nn.silu(conv_out)
    x_heads = activated[:, :, :inner_here].reshape(seqs_here, length, heads_here, head_size)
    b_rows = activated[:, :, inner_here : inner_here + state_size]
    c_rows = activated[:, :, inner_here + state_size :]
    pre_step = dt_input.transpose(0, 2, 1) + dt_bias[None, :, None]
    step_size = jax.nn.softplus(pre_step)
    decay_rates = jnp.exp(a_log)[None, :, None]
    log_decay = -decay_rates * step_size
    (within, summary, total_decay), local_back = jax.vjp(
        block_local, x_heads, b_rows, c_rows, step_size, log_decay
    )
    identity = (jnp.ones_like(total_decay), jnp.zeros_like(summary))
    state_in = carried_in((total_decay, summary), "ctx", combine_states, identity, False)[1]
    carried, carry_back = jax.vjp(block_carry, c_rows, log_decay, state_in)
    mixed_heads = within + carried + skip_gain[None, None, :, None] * x_heads
    mixed_flat = mixed_heads.reshape(seqs_here, length, inner_here)
    gate_act = jax.nn.silu(gate_input)
    gated_rows = mixed_flat * gate_act
    square_sum = lax.psum(jnp.sum(gated_rows * gated_rows, axis=-1), "tp")
    out_scale = lax.rsqrt(square_sum / full_inner + EPSILON)[:, :, None]
    normed_out = (
        (gated_rows * out_scale * gated_gain).astype(jnp.bfloat16).reshape(row_count, inner_here)
    )
    branch_sum = lax.psum(jnp.dot(normed_out, full_out, preferred_element_type=jnp.float32), "tp")
    block_output = (residual + branch_sum.reshape(seqs_here, length, model_width)).astype(
        jnp.bfloat16
    )
    cot_rows = cotangent.reshape(row_count, model_width)
    grad_out_w = lax.dot_general(
        normed_out, cot_rows, (((0,), (0,)), ((), ())), preferred_element_type=jnp.float32
    )
    d_normed_low = back_product(cot_rows, full_out).astype(jnp.bfloat16)
    d_normed_out = d_normed_low.astype(jnp.float32).reshape(seqs_here, length, inner_here)
    grad_gated_gain = jnp.sum(d_normed_out * gated_rows * out_scale, axis=(0, 1))
    cross_sum = lax.psum(jnp.sum(d_normed_out * gated_gain * gated_rows, axis=-1), "tp")
    d_gated = (
        out_scale * gated_gain * d_normed_out
        - gated_rows * (out_scale**3 / full_inner) * cross_sum[:, :, None]
    )
    d_mixed = (d_gated * gate_act).reshape(seqs_here, length, heads_here, head_size)
    d_gate_low = (
        (d_gated * mixed_flat * silu_slope(gate_input))
        .astype(jnp.bfloat16)
        .reshape(row_count, inner_here)
    )
    grad_skip_gain = jnp.sum(d_mixed * x_heads, axis=(0, 1, 3))
    d_c_carry, d_decay_carry, state_grad = carry_back(d_mixed)
    later_grad = carried_in((total_decay, state_grad), "ctx", combine_states, identity, True)[1]
    d_total = jnp.sum(later_grad * state_in, axis=(2, 3))
    d_x_heads, d_b_rows, d_c_rows, d_step, d_log_decay = local_back((d_mixed, later_grad, d_total))
    d_x_heads = d_x_heads + skip_gain[None, None, :, None] * d_mixed
    d_c_rows = d_c_rows + d_c_carry
    d_log_decay = d_log_decay + d_decay_carry
    grad_a_log = jnp.sum(d_log_decay * log_decay, axis=(0, 2))
    d_pre = (d_step - decay_rates * d_log_decay) * jax.nn.sigmoid(pre_step)
    grad_dt_bias = jnp.sum(d_pre, axis=(0, 2))
    d_dt_low = d_pre.transpose(0, 2, 1).astype(jnp.bfloat16).reshape(row_count, heads_here)
    d_activated = jnp.concatenate(
        [d_x_heads.reshape(seqs_here, length, inner_here), d_b_rows, d_c_rows], axis=-1
    )
    d_conv_out = d_activated * silu_slope(conv_out)
    d_padded = jnp.zeros_like(padded)
    tap_grads = []
    for offset in range(tap_count):
        tap_grads.append(jnp.sum(d_conv_out * padded[:, offset : offset + length, :], axis=(0, 1)))
        d_padded = d_padded.at[:, offset : offset + length, :].add(conv_taps[offset] * d_conv_out)
    grad_taps = jnp.stack(tap_grads)
    edge_grad = from_behind(d_padded[:, : tap_count - 1, :], "ctx", -1)
    d_conv_input = d_padded[:, tap_count - 1 :, :] + jnp.pad(
        edge_grad, ((0, 0), (length - tap_count + 1, 0), (0, 0))
    )
    d_x_low = d_conv_input[:, :, :inner_here].astype(jnp.bfloat16).reshape(row_count, inner_here)
    partial_normed = (
        back_product(d_gate_low, full_gate)
        + back_product(d_x_low, full_x)
        + back_product(d_dt_low, full_dt)
    )
    summed_normed, summed_bc, grad_bc_conv = lax.psum(
        (
            partial_normed,
            d_conv_input[:, :, inner_here:].reshape(row_count, 2 * state_size),
            grad_taps[:, inner_here:],
        ),
        "tp",
    )
    d_bc_low = summed_bc.astype(jnp.bfloat16)
    d_normed = (summed_normed + back_product(d_bc_low, full_bc)).reshape(
        seqs_here, length, model_width
    )

    def weight_grad(grad_low):
        return lax.dot_general(
            normed_low, grad_low, (((0,), (0,)), ((), ())), preferred_element_type=jnp.float32
        )

    weight_grads = (
        weight_grad(d_gate_low),
        weight_grad(d_x_low),
        weight_grad(d_bc_low),
        weight_grad(d_dt_low),
        grad_out_w,
    )
    grad_input_gain = jnp.sum(d_normed * residual * in_scale, axis=(0, 1))
    d_scaled = d_normed * input_gain
    input_grad = (
        cotangent.astype(jnp.float32)
        + in_scale * d_scaled
        - residual
        * (in_scale**3 / model_width)
        * jnp.sum(d_scaled * residual, axis=-1, keepdims=True)
    )
    sectioned = (
        lax.psum_scatter(weight_grads[0], "fsdp", scatter_dimension=0, tiled=True),
        lax.psum_scatter(weight_grads[1], "fsdp", scatter_dimension=0, tiled=True),
        lax.psum_scatter(weight_grads[2], "fsdp", scatter_dimension=0, tiled=True),
        lax.psum_scatter(weight_grads[3], "fsdp", scatter_dimension=0, tiled=True),
        lax.psum_scatter(weight_grads[4], "fsdp", scatter_dimension=1, tiled=True),
    )
    owned_rows = (
        lax.psum_scatter(sectioned[0], "ctx", scatter_dimension=0, tiled=True),
        lax.psum_scatter(sectioned[1], "ctx", scatter_dimension=0, tiled=True),
        lax.psum_scatter(sectioned[2], "ctx", scatter_dimension=0, tiled=True),
        lax.psum_scatter(sectioned[3], "ctx", scatter_dimension=0, tiled=True),
        lax.psum_scatter(sectioned[4], "ctx", scatter_dimension=1, tiled=True),
    )
    grad_gate_proj, grad_x_proj, grad_bc_proj, grad_dt_proj, grad_out_proj = (
        lax.all_gather(owned_rows[0], "ctx", axis=0, tiled=True),
        lax.all_gather(owned_rows[1], "ctx", axis=0, tiled=True),
        lax.all_gather(owned_rows[2], "ctx", axis=0, tiled=True),
        lax.all_gather(owned_rows[3], "ctx", axis=0, tiled=True),
        lax.all_gather(owned_rows[4], "ctx", axis=1, tiled=True),
    )
    small_totals = lax.psum(
        (
            grad_input_gain,
            grad_taps[:, :inner_here],
            grad_bc_conv,
            grad_dt_bias,
            grad_a_log,
            grad_skip_gain,
            grad_gated_gain,
        ),
        ("fsdp", "ctx"),
    )
    return (
        block_output,
        input_grad,
        small_totals[0],
        grad_gate_proj,
        grad_x_proj,
        grad_bc_proj,
        grad_dt_proj,
        small_totals[1],
        small_totals[2],
        small_totals[3],
        small_totals[4],
        small_totals[5],
        small_totals[6],
        grad_out_proj,
    )


def solution(mesh):
    in_specs = (
        P("fsdp", "ctx", None),
        P(),
        P("fsdp", "tp"),
        P("fsdp", "tp"),
        P("fsdp", None),
        P("fsdp", "tp"),
        P(None, "tp"),
        P(),
        P("tp"),
        P("tp"),
        P("tp"),
        P("tp"),
        P("tp", "fsdp"),
        P("fsdp", "ctx", None),
    )
    out_specs = (
        P("fsdp", "ctx", None),
        P("fsdp", "ctx", None),
        P(),
        P("fsdp", "tp"),
        P("fsdp", "tp"),
        P("fsdp", None),
        P("fsdp", "tp"),
        P(None, "tp"),
        P(),
        P("tp"),
        P("tp"),
        P("tp"),
        P("tp"),
        P("tp", "fsdp"),
    )
    return jax.shard_map(
        on_device, mesh=mesh, in_specs=in_specs, out_specs=out_specs, check_vma=False
    )
```

profile of v0, /device:TPU:0, one launch (start us, length us, event | category | flops | bytes accessed | tf_op | source)
XLA Modules:
  0.0 786.5 jit_solution(12926951627118034505)
XLA Ops:
  8.0 15.0 %all_gather.50 = bf16[1024,16]{0,1:T(8,128)(2,1)S(1)} all-gather(bf16[256,16]{0,1:T(8,128)(2,1)} %param.31), channel_id=1, replica_groups=mesh['fsdp'=4,'ctx'=4,'tp'=2] {'fsdp'}, dimensions={0}, use_global_device_ids=true | all-gather | bytes 40960 | tf_op jit(solution)/shard_map/all_gather | solution.py:95
  29.3 22.7 %all_gather.49 = bf16[1024,256]{1,0:T(8,128)(2,1)S(1)} all-gather(bf16[256,256]{1,0:T(8,128)(2,1)S(1)} %copy-done.44), channel_id=1, replica_groups=mesh['fsdp'=4,'ctx'=4,'tp'=2] {'fsdp'}, dimensions={0}, use_global_device_ids=true | all-gather | bytes 655360 | tf_op jit(solution)/shard_map/all_gather | solution.py:94
  54.0 12.6 %all-gather.13.cloned.1.call-done = bf16[1024,1024]{1,0:T(8,128)(2,1)} async-done(((bf16[256,1024]{1,0:T(8,128)(2,1)}), bf16[1024,1024]{1,0:T(8,128)(2,1)}) %all-gather.13.cloned.1.call-update) | async-done | bytes 2097168 | tf_op jit(solution)/shard_map/all_gather | solution.py:93
  66.6 2.3 convolution_bitcast_fusion.1
  69.0 1.7 collective-permute-start
  71.7 1.8 fusion.40
  75.6 1.6 copy.193
  77.2 2.9 fusion.62
  83.0 7.0 all-gather
  91.1 2.6 copy.207
  94.4 2.1 fusion.92
  96.4 7.8 all-gather.25.cloned.1.call-done
  104.3 1.9 fusion.72
  106.3 6.0 fusion.36
  112.3 2.6 copy.205
  114.9 36.8 %all-gather.15.cloned.1.call-done = bf16[1024,1024]{1,0:T(8,128)(2,1)} async-done(((bf16[256,1024]{1,0:T(8,128)(2,1)}), bf16[1024,1024]{1,0:T(8,128)(2,1)}) %all-gather.15.cloned.1.call-update) | async-done | bytes 2097168 | tf_op jit(solution)/shard_map/all_gather | solution.py:92
  151.7 3.7 multiply_reduce_fusion.8
  155.4 4.9 psum.91
  160.3 37.8 %all-gather.17.cloned.1.call-done = bf16[1024,1024]{1,0:T(8,128)(2,1)} async-done(((bf16[1024,256]{1,0:T(8,128)(2,1)}), bf16[1024,1024]{1,0:T(8,128)(2,1)}) %all-gather.17.cloned.1.call-update) | async-done | bytes 2097168 | tf_op jit(solution)/shard_map/all_gather | solution.py:96
  198.2 4.0 fusion.49
  202.2 5.1 psum.93
  207.3 2.9 fusion.59
  212.4 2.6 copy.208
  215.0 3.0 fusion.88
  218.1 2.3 multiply_convert_fusion
  221.2 2.8 fusion.121
  224.0 3.9 fusion.68
  228.0 2.6 copy.211
  230.7 8.6 %fusion.8 = (f32[16,256]{1,0:T(8,128)}, f32[16,256]{1,0:T(8,128)}, f32[16,256]{1,0:T(8,128)}, f32[256,256]{1,0:T(8,128)S(1)}) fusion(f32[16,256]{1,0:T(8,128)S(1)} %copy-done.57, f32[256,256]{1,0:T(8,128)} %fusion.92, f32[16,256]{1,0:T(8,128)S(1)} %copy-done.59, pred[256,256]{1,0:T(8,128)(4,1)} %iota_compare_fusion, f32[16,64,256]{2,1,0:T(8,128)} %bitcast.308, ...), kind=kOutput, calls=%fused_computation.20 | convolution fusion | flops 820957184 | bytes 2768896 | tf_op jit(solution)/shard_map/transpose(jvp(bhts,bshp->bthp))/dot_general | solution.py:49
  240.7 1.8 convolution_bitcast_fusion.6
  243.9 6.0 while.31
  250.0 2.4 multiply_reduce_fusion.6
  252.5 4.9 fusion.30
  257.4 2.5 copy.216
  259.9 3.1 fusion.42
  263.1 2.6 multiply_reduce_fusion.5
  268.5 4.5 scatter-add.11
  273.0 2.6 slice_add_fusion.1
  275.5 4.4 scatter-add.14
  282.0 1.8 collective-permute-done.1
  283.8 1.5 fusion.39
  286.4 2.8 fusion.77
  292.9 2.5 reduce-window.26
  295.5 2.5 reduce-window.24
  300.2 12.9 %all-reduce.11 = (bf16[256,256]{1,0:T(8,128)(2,1)S(1)}, f32[4,256]{1,0:T(4,128)}) all-reduce(f32[256,256]{1,0:T(8,128)S(1)} %slice_bitcast_fusion, f32[4,256]{1,0:T(4,128)S(1)} %pad_maximum_fusion.2), channel_id=1, replica_groups=mesh['fsdp'=4,'ctx'=4,'tp'=2] {'tp'}, use_global_device_ids=true, to_apply=%region_24.25 | all-reduce | flops 66560 | bytes 401408 | tf_op jit(solution)/shard_map/psum | solution.py:199
  314.6 3.4 reduce-scatter.15.cloned.1.call-done
  318.0 79.6 %reduce-scatter.29.cloned.1.call-done = f32[1024,256]{1,0:T(8,128)} async-done(((f32[1024,1024]{1,0:T(8,128)}), f32[1024,256]{1,0:T(8,128)}) %reduce-scatter.29.cloned.1.call-update) | async-done | bytes 1048592 | tf_op jit(solution)/shard_map/reduce_scatter | solution.py:238
  397.7 2.5 copy.245
  400.3 77.0 %reduce-scatter.19.cloned.1.call-done = f32[256,1024]{1,0:T(8,128)} async-done(((f32[1024,1024]{1,0:T(8,128)}), f32[256,1024]{1,0:T(8,128)}) %reduce-scatter.19.cloned.1.call-update) | async-done | bytes 1048592 | tf_op jit(solution)/shard_map/reduce_scatter | solution.py:235
  477.3 3.5 convolution_bitcast_fusion
  483.2 16.5 %reduce-scatter.27.cloned.1.call-done = f32[256,16]{0,1:T(8,128)} async-done(((f32[1024,16]{0,1:T(8,128)}), f32[256,16]{0,1:T(8,128)}) %reduce-scatter.27.cloned.1.call-update) | async-done | bytes 16400 | tf_op jit(solution)/shard_map/reduce_scatter | solution.py:237
  502.6 25.2 %reduce-scatter.23.cloned.1.call-done = f32[256,256]{1,0:T(8,128)} async-done(((f32[1024,256]{1,0:T(8,128)}), f32[256,256]{1,0:T(8,128)}) %reduce-scatter.23.cloned.1.call-update) | async-done | bytes 262160 | tf_op jit(solution)/shard_map/reduce_scatter | solution.py:236
  527.9 26.2 %reduce-scatter.17.cloned.1.call-done = f32[64,1024]{1,0:T(8,128)} async-done(((f32[256,1024]{1,0:T(8,128)}), f32[64,1024]{1,0:T(8,128)}) %reduce-scatter.17.cloned.1.call-update) | async-done | bytes 262160 | tf_op jit(solution)/shard_map/reduce_scatter | solution.py:241
  554.1 27.2 %reduce-scatter.33.cloned.1.call-done = f32[64,1024]{1,0:T(8,128)} async-done(((f32[256,1024]{1,0:T(8,128)}), f32[64,1024]{1,0:T(8,128)}) %reduce-scatter.33.cloned.1.call-update) | async-done | bytes 262160
  581.4 27.6 %reduce-scatter.21.cloned.1.call-done = f32[64,1024]{1,0:T(8,128)} async-done(((f32[256,1024]{1,0:T(8,128)}), f32[64,1024]{1,0:T(8,128)}) %reduce-scatter.21.cloned.1.call-update) | async-done | bytes 262160 | tf_op jit(solution)/shard_map/reduce_scatter | solution.py:242
  609.3 22.1 %reduce-scatter.31.cloned.1.call-done = f32[64,16]{1,0:T(8,128)} async-done(((f32[256,16]{1,0:T(8,128)}), f32[64,16]{1,0:T(8,128)}) %reduce-scatter.31.cloned.1.call-update) | async-done | bytes 4112
  632.2 5.2 all-gather.3
  638.1 59.9 %all-reduce.10.cloned.1.call-done = (f32[1,256,1024]{2,1,0:T(8,128)}, f32[256,1024]{1,0:T(8,128)}) async-done(((f32[1,256,1024]{2,1,0:T(8,128)}, f32[256,1024]{1,0:T(8,128)}), (f32[1,256,1024]{2,1,0:T(8,128)}, f32[256,1024]{1,0:T(8,128)})) %all-reduce.10.cloned.1.call-update) | async-done | bytes 2097168 | tf_op jit(solution)/shard_map/psum | solution.py:145
  698.0 1.9 fusion.58
  699.9 62.2 %all-reduce.4 = (f32[1024]{0:T(1024)}, f32[4,1024]{1,0:T(4,128)}, f32[4,256]{1,0:T(4,128)}, f32[16]{0:T(128)}, f32[16]{0:T(128)}, /*index=5*/f32[16]{0:T(128)}, f32[1024]{0:T(1024)}) all-reduce(f32[1024]{0:T(1024)S(1)} %get-tuple-element.317, f32[4,1024]{1,0:T(4,128)S(1)} %slice.219, ...), channel_id=1, replica_groups=mesh['fsdp'=4,'ctx'=4,'tp'=2] {'fsdp','ctx'}, use_global_device_ids=true, to_apply=%region_27.28 | all-reduce | flops 7216 | bytes 57728 | tf_op jit(solution)/shard_map/psum | solution.py:254
  762.2 2.8 fusion.55
  764.9 7.0 all_gather.60
  772.0 2.6 copy.228
  774.6 1.6 all-gather.21.cloned.1.call-done
  (287 shorter events, 52.1 us)
Async XLA Ops:
  7.2 59.4 %all-gather.13.cloned.1.call-start = ((), (), s32[]{:S(2)}) async-start(), calls=%async_computation.10 | async-start | bytes 2621440 | tf_op jit(solution)/shard_map/all_gather | solution.py:93
  7.9 96.3 %all-gather.25.cloned.1.call-start = ((), (), s32[]{:S(2)}) async-start(), calls=%async_computation.24 | async-start | bytes 2621440 | tf_op jit(solution)/shard_map/all_gather | solution.py:20
  23.0 4.7 copy-start.42
  23.0 6.2 copy-start.64
  23.0 6.3 copy-start.67
  23.0 6.3 copy-start.44
  26.0 26.7 %copy-start.2 = (bf16[1,256,1024]{2,1,0:T(8,128)(2,1)S(1)}, bf16[1,256,1024]{2,1,0:T(8,128)(2,1)}, u32[]{:S(2)}) copy-start(bf16[1,256,1024]{2,1,0:T(8,128)(2,1)} %param.26) | copy-start | bytes 1572868
  26.1 26.7 %copy-start.37 = (f32[1024]{0:T(1024)S(1)}, f32[1024]{0:T(1024)}, u32[]{:S(2)}) copy-start(f32[1024]{0:T(1024)} %param.27) | copy-start | bytes 12292
  27.6 25.6 %copy-start.33 = (f32[1,16,256]{1,2,0:T(8,128)}, f32[1,16,256]{1,2,0:T(8,128)S(1)}, u32[]{:S(2)}) copy-start(f32[1,16,256]{1,2,0:T(8,128)S(1)} %get-tuple-element.380) | copy-start | bytes 49156
  27.6 25.6 %copy-start.29 = (f32[1,16,256]{1,2,0:T(8,128)}, f32[1,16,256]{1,2,0:T(8,128)S(1)}, u32[]{:S(2)}) copy-start(f32[1,16,256]{1,2,0:T(8,128)S(1)} %get-tuple-element.381) | copy-start | bytes 49156
  29.2 24.0 %copy-start.24 = (f32[1,16,256]{1,2,0:T(8,128)}, f32[1,16,256]{1,2,0:T(8,128)S(1)}, u32[]{:S(2)}) copy-start(f32[1,16,256]{1,2,0:T(8,128)S(1)} %get-tuple-element.365) | copy-start | bytes 49156
  53.2 18.5 %copy-start.21 = (f32[1,256,256]{2,1,0:T(8,128)}, f32[1,256,256]{2,1,0:T(8,128)S(1)}, u32[]{:S(2)}) copy-start(f32[1,256,256]{2,1,0:T(8,128)S(1)} %convolution_bitcast_fusion.3) | copy-start | bytes 786436
  53.2 15.7 %copy-start.65 = (f32[16]{0:T(128)}, f32[16]{0:T(128)S(1)}, u32[]{:S(2)}) copy-start(f32[16]{0:T(128)S(1)} %get-tuple-element.374) | copy-start | bytes 196
  69.0 2.6 collective-permute-start
  77.2 29.0 %copy-start.7 = (f32[1,256,1024]{1,2,0:T(8,128)}, f32[1,256,1024]{1,2,0:T(8,128)S(1)}, u32[]{:S(2)}) copy-start(f32[1,256,1024]{1,2,0:T(8,128)S(1)} %copy.193) | copy-start | bytes 3145732
  77.2 5.0 copy-start.36
  80.2 9.8 %copy-start.35 = (f32[256,16]{1,0:T(8,128)S(1)}, f32[256,16]{1,0:T(8,128)}, u32[]{:S(2)}) copy-start(f32[256,16]{1,0:T(8,128)} %get-tuple-element.364) | copy-start | bytes 49156
  80.2 71.5 %all-gather.15.cloned.1.call-start = ((), (), s32[]{:S(2)}) async-start(), calls=%async_computation.11 | async-start | bytes 2621440 | tf_op jit(solution)/shard_map/all_gather | solution.py:92
  80.9 117.2 %all-gather.17.cloned.1.call-start = ((), (), s32[]{:S(2)}) async-start(), calls=%async_computation.12 | async-start | bytes 2621440 | tf_op jit(solution)/shard_map/all_gather | solution.py:96
  81.5 162.4 %all-gather.27.cloned.1.call-start = ((), (), s32[]{:S(2)}) async-start(), calls=%async_computation.25 | async-start | bytes 2621440 | tf_op jit(solution)/shard_map/all_gather | solution.py:20
  104.2 8.1 %copy-start.73 = (f32[4,1,16]{2,1,0:T(1,128)}, f32[4,1,16]{2,1,0:T(1,128)S(1)}, u32[]{:S(2)}) copy-start(f32[4,1,16]{2,1,0:T(1,128)S(1)} %get-tuple-element.621) | copy-start | bytes 772
  106.2 6.1 copy-start.20
  114.9 83.2 %copy-start.45 = (f32[1024]{0:T(1024)S(1)}, f32[1024]{0:T(1024)}, u32[]{:S(2)}) copy-start(f32[1024]{0:T(1024)} %param.37) | copy-start | bytes 12292
  155.4 68.7 %copy-start.5 = (f32[256,1024]{1,0:T(8,128)}, f32[256,1024]{1,0:T(8,128)S(1)}, u32[]{:S(2)}) copy-start(f32[256,1024]{1,0:T(8,128)S(1)} %get-tuple-element.363) | copy-start | bytes 3145732
  207.3 4.0 copy-start.17
  218.0 99.9 %reduce-scatter.15.cloned.1.call-start = ((), (), s32[]{:S(2)}) async-start(), calls=%async_computation.13 | async-start | bytes 5242880 | tf_op jit(solution)/shard_map/reduce_scatter | solution.py:234
  224.0 173.7 %reduce-scatter.29.cloned.1.call-start = ((), (), s32[]{:S(2)}) async-start(), calls=%async_computation.22 | async-start | bytes 5242880 | tf_op jit(solution)/shard_map/reduce_scatter | solution.py:238
  228.0 249.2 %reduce-scatter.19.cloned.1.call-start = ((), (), s32[]{:S(2)}) async-start(), calls=%async_computation.16 | async-start | bytes 5242880 | tf_op jit(solution)/shard_map/reduce_scatter | solution.py:235
  230.7 10.1 %copy-start.13 = (f32[256,1024]{0,1:T(8,128)S(1)}, f32[256,1024]{0,1:T(8,128)}, u32[]{:S(2)}) copy-start(f32[256,1024]{0,1:T(8,128)} %copy.208) | copy-start | bytes 3145732
  259.9 3.2 copy-start.4
  259.9 3.2 copy-start.22
  268.5 4.5 copy-start.1
  280.7 3.1 collective-permute-start.1
  289.2 3.1 copy-start.25
  289.2 3.1 copy-start.30
  289.3 210.5 %reduce-scatter.27.cloned.1.call-start = ((), (), s32[]{:S(2)}) async-start(), calls=%async_computation.21 | async-start | bytes 81920 | tf_op jit(solution)/shard_map/reduce_scatter | solution.py:237
  292.5 6.0 copy-start.34
  292.5 6.0 copy-start.74
  292.9 7.2 copy-start.11
  299.1 15.4 %copy-start.40 = (bf16[1,16,256]{1,2,0:T(8,128)(2,1)}, bf16[1,16,256]{1,2,0:T(8,128)(2,1)S(1)}, u32[]{:S(2)}) copy-start(bf16[1,16,256]{1,2,0:T(8,128)(2,1)S(1)} %get-tuple-element.358) | copy-start | bytes 24580
  300.0 227.8 %reduce-scatter.23.cloned.1.call-start = ((), (), s32[]{:S(2)}) async-start(), calls=%async_computation.19 | async-start | bytes 1310720 | tf_op jit(solution)/shard_map/reduce_scatter | solution.py:236
  314.5 239.5 %reduce-scatter.17.cloned.1.call-start = ((), (), s32[]{:S(2)}) async-start(), calls=%async_computation.14 | async-start | bytes 1310720 | tf_op jit(solution)/shard_map/reduce_scatter | solution.py:241
  318.0 263.3 %reduce-scatter.33.cloned.1.call-start = ((), (), s32[]{:S(2)}) async-start(), calls=%async_computation.27 | async-start | bytes 1310720
  400.2 77.1 %copy-start.6 = (f32[256,1024]{1,0:T(8,128)S(1)}, f32[256,1024]{1,0:T(8,128)}, u32[]{:S(2)}) copy-start(f32[256,1024]{1,0:T(8,128)} %copy-done.5) | copy-start | bytes 3145732
  400.2 208.7 %reduce-scatter.21.cloned.1.call-start = ((), (), s32[]{:S(2)}) async-start(), calls=%async_computation.17 | async-start | bytes 1310720 | tf_op jit(solution)/shard_map/reduce_scatter | solution.py:242
  477.2 3.6 copy-start.16
  477.3 154.1 %reduce-scatter.31.cloned.1.call-start = ((), (), s32[]{:S(2)}) async-start(), calls=%async_computation.26 | async-start | bytes 163840
  477.3 3.5 copy-start.23
  482.4 18.9 %copy-start.41 = (bf16[1,16,256]{1,2,0:T(8,128)(2,1)S(1)}, bf16[1,16,256]{1,2,0:T(8,128)(2,1)}, u32[]{:S(2)}) copy-start(bf16[1,16,256]{1,2,0:T(8,128)(2,1)} %copy-done.40) | copy-start | bytes 24580
  482.4 18.9 %copy-start.43 = (bf16[1024,16]{0,1:T(8,128)(2,1)S(1)}, bf16[1024,16]{0,1:T(8,128)(2,1)}, u32[]{:S(2)}) copy-start(bf16[1024,16]{0,1:T(8,128)(2,1)} %copy-done.42) | copy-start | bytes 98308
  501.2 196.8 %all-reduce.10.cloned.1.call-start = ((), (), s32[]{:S(2)}) async-start(), calls=%async_computation.28 | async-start | bytes 4194304 | tf_op jit(solution)/shard_map/psum | solution.py:145
  502.5 106.5 %copy-start.56 = (f32[1024]{0:T(1024)S(1)}, f32[1024]{0:T(1024)}, u32[]{:S(2)}) copy-start(f32[1024]{0:T(1024)} %get-tuple-element.355) | copy-start | bytes 12292
  502.5 106.7 %copy-start.49 = (f32[1,1280]{1,0:T(1,128)S(1)}, f32[1,1280]{1,0:T(1,128)}, u32[]{:S(2)}) copy-start(f32[1,1280]{1,0:T(1,128)} %copy-done.48) | copy-start | bytes 15364
  502.5 106.7 %copy-start.51 = (f32[1,1280]{1,0:T(1,128)S(1)}, f32[1,1280]{1,0:T(1,128)}, u32[]{:S(2)}) copy-start(f32[1,1280]{1,0:T(1,128)} %copy-done.50) | copy-start | bytes 15364
  502.5 106.7 %copy-start.53 = (f32[1,1280]{1,0:T(1,128)S(1)}, f32[1,1280]{1,0:T(1,128)}, u32[]{:S(2)}) copy-start(f32[1,1280]{1,0:T(1,128)} %copy-done.52) | copy-start | bytes 15364
  502.5 106.7 %copy-start.55 = (f32[1,1280]{1,0:T(1,128)S(1)}, f32[1,1280]{1,0:T(1,128)}, u32[]{:S(2)}) copy-start(f32[1,1280]{1,0:T(1,128)} %copy-done.54) | copy-start | bytes 15364
  502.5 195.5 %copy-start.27 = (bf16[1024,256]{1,0:T(8,128)(2,1)S(1)}, bf16[1024,256]{1,0:T(8,128)(2,1)}, u32[]{:S(2)}) copy-start(bf16[1024,256]{1,0:T(8,128)(2,1)} %copy-done.26) | copy-start | bytes 1572868
  502.6 262.4 %reduce-scatter.25.cloned.1.call-start = ((), (), s32[]{:S(2)}) async-start(), calls=%async_computation.20 | async-start | bytes 327680 | tf_op jit(solution)/shard_map/reduce_scatter | solution.py:243
  527.8 244.2 %all-gather.19.cloned.1.call-start = ((), (), s32[]{:S(2)}) async-start(), calls=%async_computation.15 | async-start | bytes 1310720 | tf_op jit(solution)/shard_map/all_gather | solution.py:248
  554.1 217.9 %all-gather.23.cloned.1.call-start = ((), (), s32[]{:S(2)}) async-start(), calls=%async_computation.23 | async-start | bytes 1310720 | tf_op jit(solution)/shard_map/all_gather | solution.py:252
  581.4 194.9 %all-gather.21.cloned.1.call-start = ((), (), s32[]{:S(2)}) async-start(), calls=%async_computation.18 | async-start | bytes 1310720 | tf_op jit(solution)/shard_map/all_gather | solution.py:249
  698.0 64.1 %copy-start.28 = (bf16[1,256,1024]{2,1,0:T(8,128)(2,1)S(1)}, bf16[1,256,1024]{2,1,0:T(8,128)(2,1)}, u32[]{:S(2)}) copy-start(bf16[1,256,1024]{2,1,0:T(8,128)(2,1)} %param.39) | copy-start | bytes 1572868
  698.0 64.1 %copy-start.70 = (f32[256]{0:T(256)S(1)}, f32[256]{0:T(256)}, u32[]{:S(2)}) copy-start(f32[256]{0:T(256)} %get-tuple-element.376) | copy-start | bytes 3076
  772.0 4.3 copy-start.31
  (34 other events, 68.7 us)
Sparse Core Ops, SparseCore 0:
  9.6 56.9 all-gather.12
  80.3 23.7 all-gather.24
  105.7 45.9 all-gather.14
  153.1 44.9 all-gather.16
  218.1 20.8 all-gather.26
  241.2 76.7 reduce-scatter.14
  320.4 77.2 reduce-scatter.28
  399.9 77.2 reduce-scatter.18
  480.1 19.5 reduce-scatter.26
  502.4 25.3 reduce-scatter.22
  530.5 23.5 reduce-scatter.16
  556.4 24.8 reduce-scatter.32
  584.0 24.8 reduce-scatter.20
  611.8 19.5 reduce-scatter.30
  634.9 63.0 all-reduce.9
  700.3 20.0 reduce-scatter.24
  721.9 16.9 all-gather.18
  740.4 16.7 all-gather.22
  758.8 17.4 all-gather.20
where the time goes:
time: 796 us; the launch traced here: 786 us
  waiting for transfers between devices  466 us (59%)
  blocking collectives  142 us (18%)
  matrix products  71.4 us (9%)
  local copies, waits for them, and re-layouts  50.8 us (6%)
  other arithmetic  36.6 us (5%)
  between operations  15.5 us (2%)
    reduce_scatter x1, waiting for transfers between devices, on_device(): lax.psum_scatter(weight_grads[4], 'fsdp', scatter_dimension=1, tiled=True)  79.6 us
    reduce_scatter x1, waiting for transfers between devices, on_device(): lax.psum_scatter(weight_grads[1], 'fsdp', scatter_dimension=0, tiled=True)  77 us
    psum x1, blocking collectives, on_device(): lax.psum((grad_input_gain, grad_taps[:, :inner_here], grad_bc_conv, grad_...  62.2 us
    psum x1, waiting for transfers between devices, on_device(): lax.psum(jnp.dot(normed_out, full_out, preferred_element_type=jnp.float32...  59.9 us
    unnamed x21, waiting for transfers between devices  51.5 us
    all_gather x1, waiting for transfers between devices, on_device(): lax.all_gather(out_proj, 'fsdp', axis=1, tiled=True)  37.8 us
    all_gather x1, waiting for transfers between devices, on_device(): lax.all_gather(gate_proj, 'fsdp', axis=0, tiled=True)  36.8 us
    reduce_scatter x1, waiting for transfers between devices, on_device(): lax.psum_scatter(sectioned[1], 'ctx', scatter_dimension=0, tiled=True)  27.6 us
  transfers between devices with their start and end apart: 21, of which 17 were waited for; matrix products, arithmetic and copies ran while one was open for 16% of the time, Pallas kernels for 0%

commit v1 on v0

v1 whole, which is shorter than its diff:
```python
import jax
import jax.numpy as jnp
from jax import lax
from jax.experimental import pallas as pl
from jax.experimental.pallas import tpu as pltpu
from jax.sharding import PartitionSpec as P

EPSILON = 1e-05
FINE = lax.Precision.HIGHEST
F32 = jnp.float32
LOW = jnp.bfloat16
HALO = 16
LANES = 128
NEVER = -1e30


def swap(block, axis, bits):
    count = lax.axis_size(axis)
    return lax.ppermute(block, axis, [(i, i ^ bits) for i in range(count)])


def bits_of(axis):
    return [1 << b for b in range(lax.axis_size(axis).bit_length() - 1)]


def spread(block, axis):
    pieces = {0: block}
    for bit in reversed(bits_of(axis)):
        pieces.update({k ^ bit: swap(v, axis, bit) for k, v in list(pieces.items())})
    return [pieces[k] for k in range(len(pieces))]


def after(value, *earlier):
    return lax.optimization_barrier((value, *earlier))[0]


def launch(body, outs, place, *args, scratch=(), mib=40, flops=0):
    moved = sum(a.size * a.dtype.itemsize for a in args)
    return pl.pallas_call(
        body,
        out_shape=[jax.ShapeDtypeStruct(s, d) for s, d in outs],
        in_specs=[pl.BlockSpec(memory_space=pltpu.SMEM)]
        + [pl.BlockSpec(memory_space=pltpu.VMEM)] * len(args),
        out_specs=[pl.BlockSpec(memory_space=pltpu.VMEM)] * len(outs),
        scratch_shapes=[pltpu.VMEM(s, d) for s, d in scratch],
        compiler_params=pltpu.CompilerParams(vmem_limit_bytes=mib << 20),
        cost_estimate=pl.CostEstimate(flops=flops, bytes_accessed=moved, transcendentals=0),
    )(place, *args)


def aligned(start, count):
    return pl.ds(pl.multiple_of(start, count), count)


def mm(a, b, dims=((1,), (0,))):
    return lax.dot_general(
        a.astype(LOW), b.astype(LOW), (dims, ((), ())), preferred_element_type=F32
    )


NT = ((1,), (1,))
TN = ((0,), (0,))


def fine(a, b):
    return lax.dot_general(
        a, b, (((1,), (0,)), ((), ())), precision=FINE, preferred_element_type=F32
    )


def split_mm(a, b):
    high = a.astype(LOW)
    return mm(high, b) + mm(a - high.astype(F32), b)


def sigmoid(v):
    return 1.0 / (1.0 + jnp.exp(-v))


def silu_slope(v, s):
    return s * (1.0 + v * (1.0 - s))


def iota(shape, dim):
    return lax.broadcasted_iota(jnp.int32, shape, dim)


def pair_wide(v, i, per):
    rows = v.shape[0]
    first = iota((rows, LANES), 1) < LANES // per
    return jnp.where(first, v[:, per * i : per * i + 1], v[:, per * i + 1 : per * i + 2])


def head_of_unit(units, size):
    return iota((units, LANES), 0) // size == iota((units, LANES), 1)


def as_column(row, units, size):
    return jnp.sum(jnp.where(head_of_unit(units, size), row[0:1], 0.0), axis=1, keepdims=True)


def pack_body(place, rows, xp, bcp, dtp, gp, op, first, gate_q, out_q, halo, dt_wide):
    part, inner = gate_q.shape
    here = aligned(place[1] * part, part)
    heads = dtp.shape[1]
    blank = jnp.zeros((dtp.shape[0], LANES - heads), LOW)
    dt_wide[...] = jnp.concatenate([dtp[...], blank], axis=1)
    states = bcp.shape[1]
    first[:, :inner] = xp[here, :]
    first[:, inner : inner + states] = bcp[here, :]
    first[:, inner + states :] = dt_wide[here, :]
    gate_q[...] = gp[here, :]
    out_q[...] = op[aligned(place[1] * out_q.shape[0], out_q.shape[0]), :]
    halo[...] = rows[rows.shape[0] - HALO :, :]


def norm_rows(v, gain):
    v = v.astype(F32)
    return v * lax.rsqrt(jnp.mean(v * v, axis=-1, keepdims=True) + EPSILON) * gain


def norm_body(place, rows, halo, gain, normed):
    normed[:HALO] = norm_rows(halo[...], gain[...]).astype(LOW)
    for at in range(0, rows.shape[0], 64):
        normed[HALO + at : HALO + at + 64] = norm_rows(rows[at : at + 64], gain[...]).astype(LOW)


def front_body(fsdp, ctx, taps, heads, size):
    def body(place, normed, xp, bcp, dtp, *rest):
        parts = rest[:ctx]
        x_conv, bc_conv, dt_bias, a_log = rest[ctx : ctx + 4]
        w_all, proj, conv_out, act, within, state, scalars, w_x = rest[ctx + 4 :]
        z, c = place[0], place[1]
        shard, inner = xp.shape
        both = inner + bcp.shape[1]
        half_bc = bcp.shape[1] // 2
        own = aligned(z * shard, shard)
        w_all[own, :inner] = xp[...]
        w_all[own, inner:both] = bcp[...]
        w_all[own, both:] = dtp[...]
        n = shard // ctx
        for j in range(ctx):
            for k in range(1, fsdp):
                w_all[aligned((z ^ k) * shard + (c ^ j) * n, n), :] = parts[j][k - 1]
        proj[...] = jnp.dot(normed[...], w_all[...], preferred_element_type=F32)
        length = conv_out.shape[0]
        start = HALO - taps + 1
        for at in range(0, both, LANES):
            cols = slice(at, at + LANES)
            if at < inner:
                tap = x_conv[:, cols]
            else:
                tap = bc_conv[:, at - inner : at - inner + LANES]
            total = tap[0:1] * proj[start : start + length, cols]
            for k in range(1, taps):
                total = total + tap[k : k + 1] * proj[start + k : start + k + length, cols]
            conv_out[:, cols] = total
            act[:, cols] = total * sigmoid(total)
        pre = proj[HALO:, both:] + dt_bias[...]
        step = jnp.maximum(pre, 0.0) + jnp.log1p(jnp.exp(-jnp.abs(pre)))
        log_decay = -jnp.exp(a_log[...]) * step
        lower = iota((length, length), 0) >= iota((length, length), 1)
        cum = fine(jnp.where(lower, 1.0, 0.0), log_decay)
        cum_t = cum.T
        scalars[0] = step
        scalars[1] = cum
        scalars[2] = jnp.exp(cum)
        tail = jnp.exp(cum[length - 1 :] - cum)
        scalars[3] = tail
        b_low = act[:, inner : inner + half_bc].astype(LOW)
        c_low = act[:, inner + half_bc :].astype(LOW)
        scores = mm(c_low, b_low, NT)
        half = length // 2
        per = LANES // size
        first = iota((half, LANES), 1) < size
        for i in range(heads // per):
            cols = slice(LANES * i, LANES * i + LANES)
            stepped = act[:, cols] * pair_wide(step, i, per)
            w_x[:, cols] = (stepped * pair_wide(tail, i, per)).astype(LOW)
            low = stepped.astype(LOW)
            tops, bottoms = [], []
            for h in range(per * i, per * i + per):
                gaps = cum[:half, h : h + 1] - cum_t[h : h + 1, :half]
                top = jnp.exp(jnp.where(lower[:half, :half], gaps, NEVER)) * scores[:half, :half]
                gaps = cum[half:, h : h + 1] - cum_t[h : h + 1, :]
                bottom = jnp.exp(jnp.where(lower[half:], gaps, NEVER)) * scores[half:]
                tops.append(mm(top, low[:half]))
                bottoms.append(mm(bottom, low))
            within[:half, cols] = jnp.where(first, tops[0], tops[1])
            within[half:, cols] = jnp.where(first, bottoms[0], bottoms[1])
        state[...] = mm(w_x[...], b_low, TN).astype(LOW)

    return body


def merge(before, keep, other, decay, other_decay, size):
    units = keep.shape[0]
    earlier = other * as_column(decay, units, size) + keep
    later = keep * as_column(other_decay, units, size) + other
    return jnp.where(before, earlier, later)


def scan_body(bit, reverse, size, first):
    def body(place, state, other, decay, other_decay, *rest):
        if first:
            total, total_decay, prefix, prefix_decay = rest
        else:
            old, old_decay, total, total_decay, prefix, prefix_decay = rest
        before = ((place[1] & bit) != 0) != reverse
        mine, theirs = state[...].astype(F32), other[...].astype(F32)
        total[...] = merge(before, mine, theirs, decay[...], other_decay[...], size).astype(LOW)
        total_decay[...] = decay[...] * other_decay[...]
        if first:
            prefix[...] = jnp.where(before, theirs, 0.0).astype(LOW)
            prefix_decay[...] = jnp.where(before, other_decay[...], 1.0)
        else:
            units = state.shape[0]
            kept = old[...].astype(F32)
            grown = theirs * as_column(old_decay[...], units, size) + kept
            prefix[...] = jnp.where(before, grown, kept).astype(LOW)
            prefix_decay[...] = jnp.where(before, old_decay[...] * other_decay[...], old_decay[...])

    return body


def run_scan(place, state, decay, reverse, size):
    bits = bits_of("ctx")
    kept = ()
    for bit in bits[:-1]:
        other, other_decay = swap(state, "ctx", bit), swap(decay, "ctx", bit)
        outs = [(state.shape, LOW), (decay.shape, F32)] * 2
        state, decay, *kept = launch(
            scan_body(bit, reverse, size, not kept),
            outs,
            place,
            state,
            other,
            decay,
            other_decay,
            *kept,
            mib=16,
        )
    return swap(state, "ctx", bits[-1]), kept[0], kept[1]


def last_prefix(before, other, kept, kept_decay, size):
    kept_f = kept[...].astype(F32)
    grown = other[...].astype(F32) * as_column(kept_decay[0:1], kept.shape[0], size) + kept_f
    return jnp.where(before, grown, kept_f)


def gate_body(fsdp, ctx):
    def body(place, normed, cot, gp, op, *rest):
        g_parts, o_parts = rest[:ctx], rest[ctx : 2 * ctx]
        gate_in, d_normed_out, w_gate, w_out = rest[2 * ctx :]
        z, c = place[0], place[1]
        shard = gp.shape[0]
        w_gate[aligned(z * shard, shard), :] = gp[...]
        span = op.shape[1]
        w_out[:, aligned(z * span, span)] = op[...]
        n, m = shard // ctx, op.shape[0] // ctx
        for j in range(ctx):
            for k in range(1, fsdp):
                w_gate[aligned((z ^ k) * shard + (c ^ j) * n, n), :] = g_parts[j][k - 1]
                w_out[aligned((c ^ j) * m, m), aligned((z ^ k) * span, span)] = o_parts[j][k - 1]
        gate_in[...] = jnp.dot(normed[HALO:], w_gate[...], preferred_element_type=F32)
        d_normed_out[...] = mm(cot[...], w_out[...], NT).astype(LOW)

    return body


def mix_body(bit, size):
    def body(
        place, other, kept, kept_decay, act, within, scalars, gate_in, d_no, skip, gain,
        state_in, swept, sums,
    ):
        before = (place[1] & bit) != 0
        state_in[...] = last_prefix(before, other, kept, kept_decay, size).astype(LOW)
        length, inner = within.shape
        half_bc = (act.shape[1] - inner) // 2
        c_low = act[:, inner + half_bc :].astype(LOW)
        grow = scalars[2]
        per = LANES // size
        squares = jnp.zeros((length, LANES), F32)
        crosses = jnp.zeros((length, LANES), F32)
        for i in range(inner // LANES):
            cols = slice(LANES * i, LANES * i + LANES)
            carried = mm(c_low, state_in[cols, :], NT)
            flow = within[:, cols] + pair_wide(grow, i, per) * carried
            swept[:, cols] = flow
            mixed = flow + skip[:, cols] * act[:, cols]
            gate = gate_in[:, cols]
            gated = mixed * gate * sigmoid(gate)
            squares = squares + gated * gated
            crosses = crosses + d_no[:, cols].astype(F32) * gain[:, cols] * gated
        lane = iota((length, LANES), 1)
        pair = jnp.where(
            lane == 0,
            jnp.sum(squares, axis=1, keepdims=True),
            jnp.where(lane == 1, jnp.sum(crosses, axis=1, keepdims=True), 0.0),
        )
        sums[...] = pair.T[:8]

    return body


def turn_body(size, full_inner):
    def body(
        place, mine, theirs, act, swept, scalars, gate_in, d_no, skip, gain,
        normed_out, d_gate, d_mixed, d_scaled, state_grad, rows_out,
    ):
        length, inner = swept.shape
        half_bc = (act.shape[1] - inner) // 2
        both = (mine[...] + theirs[...]).T
        scale = lax.rsqrt(both[:, 0:1] / full_inner + EPSILON)
        cross = scale * scale * scale / full_inner * both[:, 1:2]
        grow = scalars[2]
        per = LANES // size
        rows_out[...] = jnp.zeros(rows_out.shape, F32)
        for i in range(inner // LANES):
            cols = slice(LANES * i, LANES * i + LANES)
            x_act = act[:, cols]
            mixed = swept[:, cols] + skip[:, cols] * x_act
            gate = gate_in[:, cols]
            s = sigmoid(gate)
            gated = mixed * gate * s
            grad = d_no[:, cols].astype(F32)
            scaled = gated * scale
            normed_out[:, cols] = (scaled * gain[:, cols]).astype(LOW)
            rows_out[0:1, cols] = jnp.sum(grad * scaled, axis=0, keepdims=True)
            d_gated = scale * gain[:, cols] * grad - gated * cross
            d_gate[:, cols] = (d_gated * mixed * silu_slope(gate, s)).astype(LOW)
            dm = d_gated * gate * s
            d_mixed[:, cols] = dm
            rows_out[1:2, cols] = jnp.sum(dm * x_act, axis=0, keepdims=True)
            d_scaled[:, cols] = (dm * pair_wide(grow, i, per)).astype(LOW)
        c_low = act[:, inner + half_bc :].astype(LOW)
        state_grad[...] = mm(d_scaled[...], c_low, TN).astype(LOW)

    return body


def deal_body(ctx):
    def body(place, d_gate, normed_out, *rest):
        sends, stage = rest[:ctx], rest[ctx]
        w = sends[0].shape[2]
        for q in range(ctx):
            stage[q, 0] = d_gate[:, q * w : q * w + w]
            stage[q, 1] = normed_out[:, q * w : q * w + w]
        for k in range(ctx):
            sends[k][...] = stage[place[1] ^ k]

    return body


def local_body(heads, size):
    def body(place, d_mixed, act, scalars, rows, normed_out, w_out, back, pair_t, half_out, branch):
        length, inner = d_mixed.shape
        half_bc = (act.shape[1] - inner) // 2
        out = jnp.dot(normed_out[...], w_out[...], preferred_element_type=F32)
        branch[...] = out.astype(LOW)
        half_out[...] = rows[...].astype(F32) + out
        step, cum = scalars[0], scalars[1]
        cum_t = cum.T
        upper = iota((length, length), 0) <= iota((length, length), 1)
        b_low = act[:, inner : inner + half_bc].astype(LOW)
        c_low = act[:, inner + half_bc :].astype(LOW)
        scores = mm(b_low, c_low, NT)
        half = length // 2
        per = LANES // size
        first = iota((length, LANES), 1) < size
        pair_t[...] = jnp.zeros(pair_t.shape, F32)
        for i in range(heads // per):
            cols = slice(LANES * i, LANES * i + LANES)
            stepped = act[:, cols] * pair_wide(step, i, per)
            grad = d_mixed[:, cols].astype(LOW)
            tops, bottoms = [], []
            for h in range(per * i, per * i + per):
                mask = first if h == per * i else jnp.logical_not(first)
                mine = jnp.where(mask, stepped, 0.0).astype(LOW)
                gaps = cum_t[h : h + 1, :] - cum[:half, h : h + 1]
                top = jnp.exp(jnp.where(upper[:half], gaps, NEVER))
                gaps = cum_t[h : h + 1, half:] - cum[half:, h : h + 1]
                bottom = jnp.exp(jnp.where(upper[half:, half:], gaps, NEVER))
                pair_t[:half] += top * mm(mine[:half], grad, NT)
                pair_t[half:, half:] += bottom * mm(mine[half:], grad[half:], NT)
                tops.append(mm(top * scores[:half], grad))
                bottoms.append(mm(bottom * scores[half:, half:], grad[half:]))
            back[:half, cols] = jnp.where(first[:half], tops[0], tops[1])
            back[half:, cols] = jnp.where(first[:half], bottoms[0], bottoms[1])

    return body


def rear_body(bit, ctx, taps, heads, size):
    def body(
        place, other, kept, kept_decay, back, pair_t, act, conv_out, proj, scalars, swept, d_mixed,
        d_scaled, state_in, skip, skip_rows, x_conv, bc_conv, dt_bias, a_log, *rest,
    ):
        d_first, small = rest[:2]
        sends = rest[2 : 2 + ctx]
        spaced, tails, dots, sweeps, stage = rest[2 + ctx :]
        length, inner = back.shape
        both = act.shape[1]
        half_bc = (both - inner) // 2
        before = (place[1] & bit) == 0
        later_f = last_prefix(before, other, kept, kept_decay, size)
        later = later_f.astype(LOW)
        step, cum, tail = scalars[0], scalars[1], scalars[3]
        b_low = act[:, inner : inner + half_bc].astype(LOW)
        c_low = act[:, inner + half_bc :].astype(LOW)
        per = LANES // size
        ones_at = jnp.where(head_of_unit(inner, size), 1.0, 0.0)
        small[...] = jnp.zeros(small.shape, F32)
        spaced[:HALO] = jnp.zeros((HALO, both), F32)
        spaced[HALO + length :] = jnp.zeros((HALO, both), F32)
        last_rows = []
        for i in range(inner // LANES):
            cols = slice(LANES * i, LANES * i + LANES)
            x_act = act[:, cols]
            wide_step = pair_wide(step, i, per)
            stepped = x_act * wide_step
            wide_tail = pair_wide(tail, i, per)
            tails[:, cols] = (stepped * wide_tail).astype(LOW)
            extra = wide_tail * mm(b_low, later[cols, :], NT)
            last_rows.append(jnp.sum(stepped * extra, axis=0, keepdims=True))
            whole = back[:, cols] + extra
            grad = d_mixed[:, cols]
            dots[:, cols] = x_act * whole
            sweeps[:, cols] = grad * swept[:, cols]
            v = conv_out[:, cols]
            spaced[HALO : HALO + length, cols] = (
                wide_step * whole + skip[:, cols] * grad
            ) * silu_slope(v, sigmoid(v))
        pair = pair_t[...]
        d_b = mm(pair, c_low) + mm(tails[...], later)
        d_c = mm(pair, b_low, TN) + mm(d_scaled[...], state_in[...])
        for at, d in ((inner, d_b), (inner + half_bc, d_c)):
            v = conv_out[:, at : at + half_bc]
            spaced[HALO : HALO + length, at : at + half_bc] = d * silu_slope(v, sigmoid(v))
        start = HALO - taps + 1
        for at in range(0, both, LANES):
            cols = slice(at, at + LANES)
            if at < inner:
                tap = x_conv[:, cols]
            else:
                tap = bc_conv[:, at - inner : at - inner + LANES]
            grad = spaced[HALO : HALO + length, cols]
            total = tap[0:1] * spaced[taps - 1 : taps - 1 + HALO + length, cols]
            for k in range(1, taps):
                lead = taps - 1 - k
                total = total + tap[k : k + 1] * spaced[lead : lead + HALO + length, cols]
            d_first[:, cols] = total.astype(LOW)
            for k in range(taps):
                found = jnp.sum(
                    grad * proj[start + k : start + k + length, cols], axis=0, keepdims=True
                )
                if at < inner:
                    small[2 + k : 3 + k, cols] = found
                else:
                    put = k * (both - inner) + at - inner
                    small[1:2, put : put + LANES] = found
        d_step = split_mm(dots[...], ones_at)
        row_sum = split_mm(sweeps[...], ones_at)
        cross = jnp.sum(later_f * state_in[...].astype(F32), axis=1, keepdims=True)
        decay_grad = jnp.sum(jnp.where(ones_at > 0, cross, 0.0), axis=0, keepdims=True)
        tail_row = split_mm(
            jnp.broadcast_to(jnp.concatenate(last_rows, axis=1), (8, inner)), ones_at
        )[0:1]
        ends = tail_row + jnp.exp(cum[length - 1 :]) * decay_grad
        upper = jnp.where(iota((length, length), 0) <= iota((length, length), 1), 1.0, 0.0)
        d_log = fine(upper, row_sum - step * d_step) + ends
        rates = jnp.exp(a_log[...])
        pre = proj[HALO:, both:] + dt_bias[...]
        d_pre = (d_step - rates * d_log) * sigmoid(pre)
        d_pre = jnp.where(iota(d_pre.shape, 1) < heads, d_pre, 0.0)
        d_first[:HALO, both:] = jnp.zeros((HALO, LANES), LOW)
        d_first[HALO:, both:] = d_pre.astype(LOW)
        w = inner // ctx
        blank = 2 * LANES - LANES
        rest_width = both - inner + LANES + blank
        r = rest_width // ctx
        narrow = jnp.concatenate(
            [d_first[:, inner:], jnp.zeros((HALO + length, blank), LOW)], axis=1
        )
        for q in range(ctx):
            stage[q, :, :w] = d_first[:, q * w : q * w + w]
            stage[q, :, w:] = narrow[:, q * r : q * r + r]
        for k in range(ctx):
            sends[k][...] = stage[place[1] ^ k]
        small[6:7] = skip_rows[0:1]
        small[7:8, :LANES] = jnp.sum(d_pre, axis=0, keepdims=True)
        small[7:8, LANES : 2 * LANES] = jnp.sum(
            d_log * (-rates * step), axis=0, keepdims=True
        )
        small[7:8, 2 * LANES : 3 * LANES] = split_mm(
            jnp.broadcast_to(skip_rows[1:2], (8, inner)), ones_at
        )[0:1]

    return body


def down_body(place, d_first, d_gate, w_first, w_gate, rows, halo, small, own, send, edge, tally):
    grad = mm(d_first[...], w_first[...], NT)
    body = grad[HALO:] + mm(d_gate[...], w_gate[...], NT)
    own[...] = body
    send[...] = body.astype(LOW)
    edge[...] = grad[:HALO].astype(LOW)
    tally[...] = small[...]
    total = jnp.sum(grad[:HALO] * norm_rows(halo[...], 1.0), axis=0, keepdims=True)
    for at in range(0, rows.shape[0], 64):
        total = total + jnp.sum(
            body[at : at + 64] * norm_rows(rows[at : at + 64], 1.0), axis=0, keepdims=True
        )
    tally[0:1] = total


def weights_body(fsdp, ctx, stacked):
    def body(place, *rest):
        pieces, normeds = rest[:ctx], rest[ctx : 2 * ctx]
        rest = rest[2 * ctx :]
        cots = rest[: ctx if stacked else 0]
        own, *sends, part = rest[len(cots) :]
        for j in range(2 if stacked else 1):
            total = None
            for k in range(ctx):
                if stacked:
                    big = cots[k][...] if j else normeds[k][HALO:]
                    term = mm(pieces[k][j], big, TN)
                else:
                    term = mm(pieces[k][...], normeds[k][...], TN)
                total = term if total is None else total + term
            part[j] = total
        span = own.shape[2]
        own[...] = part[:, :, aligned(place[0] * span, span)]
        for k in range(1, fsdp):
            sends[k - 1][...] = part[:, :, aligned((place[0] ^ k) * span, span)].astype(LOW)

    return body


def close_body(ctx, inner, states, heads):
    def body(place, *rest):
        pairs, firsts, peers = rest[:ctx], rest[ctx : 2 * ctx], rest[2 * ctx : 3 * ctx]
        grad_gate, grad_out, grad_x, grad_bc, grad_dt, g_stage, x_stage, r_stage = rest[3 * ctx :]
        c = place[1]
        w = pairs[0].shape[1]
        r = peers[0].shape[1]
        for k in range(ctx):
            q = c ^ k
            g_stage[q] = pairs[k][0].astype(F32)
            grad_out[aligned(q * w, w), :] = pairs[k][1].astype(F32)
            x_stage[q] = firsts[k][0, :w].astype(F32)
            mine = firsts[k][0, w:].astype(F32)
            r_stage[0, aligned(q * r, r), :] = mine
            r_stage[1, aligned(q * r, r), :] = mine + peers[k][0].astype(F32)
        for q in range(ctx):
            grad_gate[:, q * w : q * w + w] = g_stage[q].T
            grad_x[:, q * w : q * w + w] = x_stage[q].T
        grad_bc[...] = r_stage[1, :states].T
        grad_dt[...] = r_stage[0, states : states + LANES].T[:, :heads]

    return body


def finish_body(place, own, peer, edge, edge_peer, rows, cot, gain, out):
    length, width = rows.shape
    extra = edge[...].astype(F32) + edge_peer[...].astype(F32)
    for at in range(0, length, 64):
        v = rows[at : at + 64].astype(F32)
        grad = own[at : at + 64] + peer[at : at + 64].astype(F32)
        if at + 64 == length:
            grad = grad + jnp.concatenate([jnp.zeros((64 - HALO, width), F32), extra])
        scale = lax.rsqrt(jnp.mean(v * v, axis=-1, keepdims=True) + EPSILON)
        d = grad * gain[...]
        inner = jnp.sum(d * v, axis=-1, keepdims=True)
        out[at : at + 64] = (
            cot[at : at + 64].astype(F32)
            + scale * d
            - v * (scale * scale * scale / width * inner)
        )


def on_device(
    block_input,
    input_gain,
    gate_proj,
    x_proj,
    bc_proj,
    dt_proj,
    x_conv,
    bc_conv,
    dt_bias,
    a_log,
    skip_gain,
    gated_gain,
    out_proj,
    cotangent,
):
    length, width = block_input.shape[1:]
    shard, inner = gate_proj.shape
    heads = dt_proj.shape[1]
    size = inner // heads
    states = bc_proj.shape[1]
    half_bc = states // 2
    taps = x_conv.shape[0]
    both = inner + states
    full_inner = inner * lax.axis_size("tp")
    ctx, fsdp = lax.axis_size("ctx"), lax.axis_size("fsdp")
    place = jnp.stack([lax.axis_index(a) for a in ("fsdp", "ctx", "tp")]).astype(jnp.int32)
    rows, cot = block_input[0], cotangent[0]
    ext = HALO + length
    last_bit = bits_of("ctx")[-1]

    first_q, gate_q, out_q, edge_rows, dt_wide = launch(
        pack_body,
        [
            ((shard // ctx, both + LANES), LOW),
            ((shard // ctx, inner), LOW),
            ((inner // ctx, out_proj.shape[1]), LOW),
            ((HALO, width), LOW),
            ((shard, LANES), LOW),
        ],
        place,
        rows,
        x_proj,
        bc_proj,
        dt_proj,
        gate_proj,
        out_proj,
        mib=16,
    )
    halo = lax.ppermute(edge_rows, "ctx", [(i, i + 1) for i in range(ctx - 1)])
    gain = input_gain[None]
    [normed] = launch(norm_body, [((ext, width), LOW)], place, rows, halo, gain, mib=16)

    def across(block):
        return [swap(block, "fsdp", k) for k in range(1, fsdp)]

    first_far = jnp.stack(across(first_q))
    first_parts = spread(first_far, "ctx")
    gate_q, out_q = after((gate_q, out_q), first_far)
    gate_far, out_far = jnp.stack(across(gate_q)), jnp.stack(across(out_q))
    gate_far, out_far = after((gate_far, out_far), first_parts[1])
    gate_parts, out_parts = spread(gate_far, "ctx"), spread(out_far, "ctx")
    late = after((normed, cot), gate_parts[-1])
    normed_all = [normed] + spread(late[0], "ctx")[1:]
    cot_all = [cot] + spread(late[1], "ctx")[1:]

    pad_heads = ((0, 0), (0, LANES - heads))
    bias_row = jnp.pad(dt_bias[None], pad_heads)
    a_row = jnp.pad(a_log[None], pad_heads)
    skip_row = jnp.repeat(skip_gain, size)[None]
    gained = gated_gain[None]
    w_first, proj, conv_out, act, within, state, scalars = launch(
        front_body(fsdp, ctx, taps, heads, size),
        [
            ((width, both + LANES), LOW),
            ((ext, both + LANES), F32),
            ((length, both), F32),
            ((length, both), F32),
            ((length, inner), F32),
            ((inner, half_bc), LOW),
            ((4, length, LANES), F32),
        ],
        place,
        normed,
        x_proj,
        bc_proj,
        dt_wide,
        *first_parts,
        x_conv,
        bc_conv,
        bias_row,
        a_row,
        scratch=[((length, inner), LOW)],
        flops=2 * ext * width * (both + LANES),
    )
    decay = scalars[2, length - 8 :][7:8] * jnp.ones((8, 1), F32)
    other, kept, kept_decay = run_scan(place, state, decay, False, size)
    gate_in, d_no, w_gate, w_out = launch(
        gate_body(fsdp, ctx),
        [
            ((length, inner), F32),
            ((length, inner), LOW),
            ((width, inner), LOW),
            ((inner, width), LOW),
        ],
        place,
        normed,
        cot,
        gate_proj,
        out_proj,
        *gate_parts,
        *out_parts,
        flops=4 * length * width * inner,
    )
    state_in, swept, sums = launch(
        mix_body(last_bit, size),
        [((inner, half_bc), LOW), ((length, inner), F32), ((8, length), F32)],
        place,
        other,
        kept,
        kept_decay,
        act,
        within,
        scalars,
        gate_in,
        d_no,
        skip_row,
        gained,
        flops=2 * length * inner * half_bc,
    )
    others = swap(sums, "tp", 1)
    normed_out, d_gate, d_mixed, d_scaled, state_grad, skip_rows = launch(
        turn_body(size, full_inner),
        [
            ((length, inner), LOW),
            ((length, inner), LOW),
            ((length, inner), F32),
            ((length, inner), LOW),
            ((inner, half_bc), LOW),
            ((8, inner), F32),
        ],
        place,
        sums,
        others,
        act,
        swept,
        scalars,
        gate_in,
        d_no,
        skip_row,
        gained,
        flops=2 * length * inner * half_bc,
    )
    other, kept, kept_decay = run_scan(place, state_grad, decay, True, size)

    w = inner // ctx
    sends = launch(
        deal_body(ctx),
        [((2, length, w), LOW)] * ctx,
        place,
        d_gate,
        normed_out,
        scratch=[((ctx, 2, length, w), LOW)],
        mib=16,
    )
    back, pair_t, half_out, branch = launch(
        local_body(heads, size),
        [
            ((length, inner), F32),
            ((length, length), F32),
            ((length, width), F32),
            ((length, width), LOW),
        ],
        place,
        d_mixed,
        act,
        scalars,
        rows,
        normed_out,
        w_out,
        flops=2 * length * width * inner,
    )
    block_output = (half_out + swap(branch, "tp", 1).astype(F32)).astype(LOW)[None]
    pieces = [sends[0]] + [swap(sends[k], "ctx", k) for k in range(1, ctx)]

    r = 4 * LANES // ctx
    d_first, small, *first_sends = launch(
        rear_body(last_bit, ctx, taps, heads, size),
        [((ext, both + LANES), LOW), ((8, inner), F32)] + [((ext, w + r), LOW)] * ctx,
        place,
        other,
        kept,
        kept_decay,
        back,
        pair_t,
        act,
        conv_out,
        proj,
        scalars,
        swept,
        d_mixed,
        d_scaled,
        state_in,
        skip_row,
        skip_rows,
        x_conv,
        bc_conv,
        bias_row,
        a_row,
        scratch=[
            ((ext + HALO, both), F32),
            ((length, inner), LOW),
            ((length, inner), F32),
            ((length, inner), F32),
            ((ctx, ext, w + r), LOW),
        ],
        flops=2 * length * inner * half_bc * 4,
    )
    first_pieces = [first_sends[0]] + [swap(first_sends[k], "ctx", k) for k in range(1, ctx)]
    own_grad, send_grad, edge, tally = launch(
        down_body,
        [((length, width), F32), ((length, width), LOW), ((HALO, width), LOW), ((8, width), F32)],
        place,
        d_first,
        d_gate,
        w_first,
        w_gate,
        rows,
        halo,
        small,
        flops=2 * ext * width * (both + LANES + inner),
    )
    back_one = [(i + 1, i) for i in range(ctx - 1)]
    edge_in = lax.ppermute(edge, "ctx", back_one)
    edge_peer = swap(edge_in, "tp", 1)
    [input_grad] = launch(
        finish_body,
        [((length, width), F32)],
        place,
        own_grad,
        swap(send_grad, "tp", 1),
        edge_in,
        edge_peer,
        rows,
        cot,
        gain,
        mib=24,
    )

    def reduce_parts(count, columns, *args, stacked):
        span = width // fsdp
        own, *outs = launch(
            weights_body(fsdp, ctx, stacked),
            [((count, columns, span), F32)] + [((count, columns, span), LOW)] * (fsdp - 1),
            place,
            *args,
            scratch=[((count, columns, width), F32)],
            flops=2 * count * columns * width * length * ctx,
        )
        for k in range(1, fsdp):
            own = own + swap(outs[k - 1], "fsdp", k).astype(F32)
        return own.astype(LOW)

    pair_own = reduce_parts(2, w, *pieces, *normed_all, *cot_all, stacked=True)
    pair_all = [pair_own] + [swap(pair_own, "ctx", k) for k in range(1, ctx)]
    first_own = reduce_parts(1, w + r, *first_pieces, *normed_all, stacked=False)
    first_all = [first_own] + [swap(first_own, "ctx", k) for k in range(1, ctx)]
    peer_own = swap(first_own[:, w:], "tp", 1)
    peer_all = [peer_own] + [swap(peer_own, "ctx", k) for k in range(1, ctx)]
    grad_gate, grad_out, grad_x, grad_bc, grad_dt = launch(
        close_body(ctx, inner, states, heads),
        [
            ((shard, inner), F32),
            ((inner, out_proj.shape[1]), F32),
            ((shard, inner), F32),
            ((shard, states), F32),
            ((shard, heads), F32),
        ],
        place,
        *pair_all,
        *first_all,
        *peer_all,
        scratch=[((ctx, w, shard), F32), ((ctx, w, shard), F32), ((2, r * ctx, shard), F32)],
        mib=24,
    )

    shared = (jnp.arange(8) < 2)[:, None]
    tally = tally + jnp.where(shared, swap(tally, "tp", 1), 0.0)
    for axis in ("ctx", "fsdp"):
        for bit in bits_of(axis):
            tally = tally + swap(tally, axis, bit)
    return (
        block_output,
        input_grad[None],
        tally[0],
        grad_gate,
        grad_x,
        grad_bc,
        grad_dt,
        tally[2 : 2 + taps],
        tally[1].reshape(taps, states),
        tally[7, :heads],
        tally[7, LANES : LANES + heads],
        tally[7, 2 * LANES : 2 * LANES + heads],
        tally[6],
        grad_out,
    )


def solution(mesh):
    rows = P("fsdp", "ctx", None)
    both = P("fsdp", "tp")
    head = P("tp")
    in_specs = (
        rows,
        P(),
        both,
        both,
        P("fsdp", None),
        both,
        P(None, "tp"),
        P(),
        head,
        head,
        head,
        head,
        P("tp", "fsdp"),
        rows,
    )
    out_specs = (
        rows,
        rows,
        P(),
        both,
        both,
        P("fsdp", None),
        both,
        P(None, "tp"),
        P(),
        head,
        head,
        head,
        head,
        P("tp", "fsdp"),
    )
    return jax.shard_map(
        on_device, mesh=mesh, in_specs=in_specs, out_specs=out_specs, check_vma=False
    )
```

time: 796 us -> 250 us (0.31); the launches traced: 786 us -> 250 us
  waiting for transfers between devices: 466 us -> 104 us
  blocking collectives: 142 us -> 0 us
  starting transfers between devices: 3.78 us -> 83.5 us
  matrix products: 71.4 us -> 0 us
  Pallas kernels: 0 us -> 38.8 us
  other arithmetic: 36.6 us -> 3.02 us
  local copies, waits for them, and re-layouts: 50.8 us -> 18.9 us
  between operations: 15.5 us -> 1.17 us
    reduce_scatter x8 -> x0, waiting for transfers between devices: 255 us -> none  [the longest x1 79.6 us: on_device(): lax.psum_scatter(weight_grads[4], 'fsdp', scatter_dimension=1, tiled=True)]
    ppermute x2 -> x62, waiting for transfers between devices: 2.49 us -> 104 us  [the longest x60 104 us: swap(): return lax.ppermute(block, axis, [(i, i ^ bits) for i in range(count)])]
    all_gather x8 -> x0, waiting for transfers between devices: 96.7 us -> none  [the longest x1 37.8 us: on_device(): lax.all_gather(out_proj, 'fsdp', axis=1, tiled=True)]
    psum x4 -> x0, blocking collectives: 85.1 us -> none  [the longest x1 62.2 us: on_device(): lax.psum((grad_input_gain, grad_taps[:, :inner_here], grad_bc_conv, grad_...]
    ppermute x2 -> x62, starting transfers between devices: 3.02 us -> 83.5 us  [the longest x60 80.6 us: swap(): return lax.ppermute(block, axis, [(i, i ^ bits) for i in range(count)])]
    dot_general x27 -> x0, matrix products: 71.4 us -> none  [the longest x3 19.4 us: block_local(): within = jnp.einsum('bhts,bshp->bthp', weights, x_heads, precision=FINE)]
    psum x1 -> x0, waiting for transfers between devices: 59.9 us -> none  [on_device(): lax.psum(jnp.dot(normed_out, full_out, preferred_element_type=jnp.float32...]
    all_gather x5 -> x0, blocking collectives: 57 us -> none  [the longest x1 22.7 us: on_device(): lax.all_gather(bc_proj, 'fsdp', axis=0, tiled=True)]
  transfers between devices with their start and end apart: 21 -> 62, of which waited for: 17 -> 25; matrix products, arithmetic and copies ran while one was open for 16% -> 2% of each run, Pallas kernels for 0% -> 12%
where the time goes in v1:
time: 250 us
  waiting for transfers between devices  104 us (42%)
  starting transfers between devices  83.5 us (33%)
  Pallas kernels  38.8 us (16%)
  local copies, waits for them, and re-layouts  18.9 us (8%)
  other arithmetic  3.02 us (1%)
    ppermute x60, waiting for transfers between devices, swap(): return lax.ppermute(block, axis, [(i, i ^ bits) for i in range(count)])  104 us
    ppermute x60, starting transfers between devices, swap(): return lax.ppermute(block, axis, [(i, i ^ bits) for i in range(count)])  80.6 us
    pallas_call x16, Pallas kernels, launch(): pl.pallas_call(body, out_shape=[jax.ShapeDtypeStruct(s, d) for s, d in ou...  38.8 us
    unnamed x68, local copies, waits for them, and re-layouts  15.6 us
  transfers between devices with their start and end apart: 62, of which 25 were waited for; matrix products, arithmetic and copies ran while one was open for 2% of the time, Pallas kernels for 12%

profile of v1, /device:TPU:0, one launch (start us, length us, event | category | flops | bytes accessed | tf_op | source)
XLA Modules:
  0.0 249.7 jit_solution(14618441102306119763)
XLA Ops:
  1.5 1.0 copy-done
  2.6 1.0 copy-done.5
  7.3 5.1 %collective-permute-start.3 = (bf16[64,1408]{1,0:T(8,128)(2,1)S(1)}, bf16[64,1408]{1,0:T(8,128)(2,1)S(1)}, u32[]{:S(2)}, u32[]{:S(2)}) collective-permute-start(bf16[64,1408]{1,0:T(8,128)(2,1)S(1)} %get-tuple-element.84), channel_id=1, source_target_pairs={{0,24},{8,16},{16,8},{24,0},{1,25},{9,17},{17,9},{25,1},{2,26},{10... | collective-permute-start | bytes 540680 | tf_op jit(solution)/shard_map/ppermute | solution.py:19
  13.0 4.9 %collective-permute-done.3 = bf16[64,1408]{1,0:T(8,128)(2,1)S(1)} collective-permute-done((bf16[64,1408]{1,0:T(8,128)(2,1)S(1)}, bf16[64,1408]{1,0:T(8,128)(2,1)S(1)}, u32[]{:S(2)}, u32[]{:S(2)}) %collective-permute-start.3) | collective-permute-done | bytes 180256 | tf_op jit(solution)/shard_map/ppermute | solution.py:19
  17.9 9.8 %collective-permute-done.2 = bf16[64,1408]{1,0:T(8,128)(2,1)S(1)} collective-permute-done((bf16[64,1408]{1,0:T(8,128)(2,1)S(1)}, bf16[64,1408]{1,0:T(8,128)(2,1)S(1)}, u32[]{:S(2)}, u32[]{:S(2)}) %collective-permute-start.2) | collective-permute-done | bytes 180256 | tf_op jit(solution)/shard_map/ppermute | solution.py:19
  27.8 1.6 collective-permute-start.5
  29.3 11.8 %collective-permute-done.5.rest_2_ = bf16[3,64,1408]{2,1,0:T(8,128)(2,1)S(1)} collective-permute-done((bf16[3,64,1408]{2,1,0:T(8,128)(2,1)S(1)}, bf16[3,64,1408]{2,1,0:T(8,128)(2,1)S(1)}, u32[]{:S(2)}, u32[]{:S(2)}) %collective-permute-start.5) | collective-permute-done | bytes 540704 | tf_op jit(solution)/shard_map/ppermute | solution.py:19
  41.1 2.3 collective-permute-start.12
  43.4 2.1 collective-permute-start.10
  45.5 3.8 %collective-permute-done.12 = bf16[64,1024]{1,0:T(8,128)(2,1)S(1)} collective-permute-done((bf16[64,1024]{1,0:T(8,128)(2,1)S(1)}, bf16[64,1024]{1,0:T(8,128)(2,1)S(1)}, u32[]{:S(2)}, u32[]{:S(2)}) %collective-permute-start.12) | collective-permute-done | bytes 131104 | tf_op jit(solution)/shard_map/ppermute | solution.py:19
  49.4 2.3 collective-permute-start.15
  51.7 3.3 %collective-permute-done.11 = bf16[64,1024]{1,0:T(8,128)(2,1)S(1)} collective-permute-done((bf16[64,1024]{1,0:T(8,128)(2,1)S(1)}, bf16[64,1024]{1,0:T(8,128)(2,1)S(1)}, u32[]{:S(2)}, u32[]{:S(2)}) %collective-permute-start.11) | collective-permute-done | bytes 131104 | tf_op jit(solution)/shard_map/ppermute | solution.py:19
  55.0 2.9 %collective-permute-start.13 = (bf16[256,256]{1,0:T(8,128)(2,1)S(1)}, bf16[256,256]{1,0:T(8,128)(2,1)S(1)}, u32[]{:S(2)}, u32[]{:S(2)}) collective-permute-start(bf16[256,256]{1,0:T(8,128)(2,1)S(1)} %get-tuple-element.95), channel_id=1, source_target_pairs={{0,8},{8,0},{16,24},{24,16},{1,9},{9,1},{17,25},{25,17},{2,10},{10... | collective-permute-start | bytes 393224 | tf_op jit(solution)/shard_map/ppermute | solution.py:19
  58.6 7.1 %collective-permute-done.14 = bf16[256,256]{1,0:T(8,128)(2,1)S(1)} collective-permute-done((bf16[256,256]{1,0:T(8,128)(2,1)S(1)}, bf16[256,256]{1,0:T(8,128)(2,1)S(1)}, u32[]{:S(2)}, u32[]{:S(2)}) %collective-permute-start.14) | collective-permute-done | bytes 131104 | tf_op jit(solution)/shard_map/ppermute | solution.py:19
  66.6 1.5 collective-permute-start.17
  68.6 1.4 collective-permute-start
  71.7 4.6 %shard_map.247 = (bf16[1024,1408]{1,0:T(8,128)(2,1)S(1)}, f32[272,1408]{1,0:T(8,128)S(1)}, f32[256,1280]{1,0:T(8,128)S(1)}, f32[256,1280]{1,0:T(8,128)S(1)}, f32...) custom-call(s32[3]{0:T(128)S(1)} %pad_add_fusion.place, ...), custom_call_target="tpu_custom_call" | custom-call | flops 784334848 | bytes 3462144 | tf_op jit(solution)/shard_map/pallas_call | solution.py:39
  76.3 1.5 copy-done.3
  77.9 1.2 copy-done.11
  79.0 1.1 copy-done.13
  81.1 14.4 %collective-permute-start.7 = (bf16[1024,128]{1,0:T(8,128)(2,1)S(1)}, bf16[1024,128]{1,0:T(8,128)(2,1)S(1)}, u32[]{:S(2)}, u32[]{:S(2)}) collective-permute-start(bf16[1024,128]{1,0:T(8,128)(2,1)S(1)} %get-tuple-element.85.state), channel_id=1, source_target_pairs={{0,2},{2,0},{4,6},{6,4},{1,3},{3,1},{5,7},{7,5},{8,10},{10,8},{12,... | collective-permute-start | bytes 786440 | tf_op jit(solution)/shard_map/ppermute | solution.py:19
  97.0 1.6 shard_map.248
  99.3 2.5 %collective-permute-start.9 = (bf16[1024,128]{1,0:T(8,128)(2,1)}, bf16[1024,128]{1,0:T(8,128)(2,1)}, u32[]{:S(2)}, u32[]{:S(2)}) collective-permute-start(bf16[1024,128]{1,0:T(8,128)(2,1)} %get-tuple-element.87), channel_id=1, source_target_pairs={{0,4},{2,6},{4,0},{6,2},{1,5},{3,7},{5,1},{7,3},{8,12},{10,14},{12... | collective-permute-start | bytes 786440 | tf_op jit(solution)/shard_map/ppermute | solution.py:19
  103.1 3.5 %shard_map.249 = (f32[256,1024]{1,0:T(8,128)S(1)}, bf16[256,1024]{1,0:T(8,128)(2,1)S(1)}, bf16[1024,1024]{1,0:T(8,128)(2,1)S(1)}, bf16[1024,1024]{1,0:T(8,128)(2,1)S(1)}) custom-call(s32[3]{0:T(128)S(1)} %pad_add_fusion.place, bf16[272,1024]{1,0:T(8,128)(2,1)S(1)} %shard_map.246.normed.rest_4_, bf16[256,1024]{1,0:T(8,128)(2,1)S(1)} %bitcast.36, ...), custom_call_target="tpu_custom_call" | custom-call | flops 1073741824 | bytes 5275648 | tf_op jit(solution)/shard_map/pallas_call | solution.py:39
  106.7 2.3 collective-permute-done.9.other
  109.0 2.2 shard_map.250
  111.2 1.5 collective-permute-start.22
  112.7 2.2 collective-permute-done.22.theirs
  114.9 2.3 shard_map.251
  117.8 1.7 collective-permute-start.38
  119.6 1.4 shard_map.253
  123.7 3.1 %shard_map.252 = (f32[256,1024]{1,0:T(8,128)S(1)}, f32[256,256]{1,0:T(8,128)S(1)}, f32[256,1024]{1,0:T(8,128)S(1)}, bf16[256,1024]{1,0:T(8,128)(2,1)S(1)}) custom-call(s32[3]{0:T(128)S(1)} %pad_add_fusion.place, f32[256,1024]{1,0:T(8,128)S(1)} %get-tuple-element.102.d_mixed, f32[256,1280]{1,0:T(8,128)S(1)} %get-tuple-element.90.act, ...), custom_call_target="tpu_custom_call" | custom-call | flops 536870912 | bytes 6029312 | tf_op jit(solution)/shard_map/pallas_call | solution.py:39
  126.8 12.1 %collective-permute-done.25.other = bf16[1024,128]{1,0:T(8,128)(2,1)S(1)} collective-permute-done((bf16[1024,128]{1,0:T(8,128)(2,1)S(1)}, bf16[1024,128]{1,0:T(8,128)(2,1)S(1)}, u32[]{:S(2)}, u32[]{:S(2)}) %collective-permute-start.25) | collective-permute-done | bytes 262176 | tf_op jit(solution)/shard_map/ppermute | solution.py:19
  138.9 5.8 %shard_map.254 = (bf16[272,1408]{1,0:T(8,128)(2,1)S(1)}, f32[8,1024]{1,0:T(8,128)S(1)}, bf16[272,384]{1,0:T(8,128)(2,1)S(1)}, bf16[272,384]{1,0:T(8,128)(2,1)S(1...) custom-call(s32[3]{0:T(128)S(1)} %pad_add_fusion.place, ...), custom_call_target="tpu_custom_call" | custom-call | flops 268435456 | bytes 9458688 | tf_op jit(solution)/shard_map/pallas_call | solution.py:39
  144.8 2.2 shard_map.255
  147.0 1.6 collective-permute-start.29
  149.3 1.7 collective-permute-done.29
  151.0 1.7 collective-permute-start.50
  152.9 1.2 collective-permute-done.30
  154.6 3.6 %collective-permute-done.31 = f32[8,1024]{1,0:T(8,128)S(1)} collective-permute-done((f32[8,1024]{1,0:T(8,128)S(1)}, f32[8,1024]{1,0:T(8,128)S(1)}, u32[]{:S(2)}, u32[]{:S(2)}) %collective-permute-start.31) | collective-permute-done | bytes 32800 | tf_op jit(solution)/shard_map/ppermute | solution.py:19
  158.2 1.7 collective-permute-start.35
  159.9 1.4 collective-permute-start.36
  161.3 4.1 %collective-permute-done.51.rest_3_ = bf16[272,384]{1,0:T(8,128)(2,1)S(1)} collective-permute-done((bf16[272,384]{1,0:T(8,128)(2,1)S(1)}, bf16[272,384]{1,0:T(8,128)(2,1)S(1)}, u32[]{:S(2)}, u32[]{:S(2)}) %collective-permute-start.51) | collective-permute-done | bytes 208928 | tf_op jit(solution)/shard_map/ppermute | solution.py:19
  165.5 1.5 collective-permute-start.23
  167.0 2.5 shard_map.259
  169.5 2.0 collective-permute-done.35.rest_2_
  171.5 2.3 collective-permute-start.54
  173.8 2.9 %collective-permute-done.36.rest_3_ = bf16[2,256,256]{2,1,0:T(8,128)(2,1)S(1)} collective-permute-done((bf16[2,256,256]{2,1,0:T(8,128)(2,1)S(1)}, bf16[2,256,256]{2,1,0:T(8,128)(2,1)S(1)}, u32[]{:S(2)}, u32[]{:S(2)}) %collective-permute-start.36) | collective-permute-done | bytes 262176 | tf_op jit(solution)/shard_map/ppermute | solution.py:19
  176.7 2.9 %collective-permute-start.52 = (bf16[1,384,256]{2,1,0:T(8,128)(2,1)S(1)}, bf16[1,384,256]{2,1,0:T(8,128)(2,1)S(1)}, u32[]{:S(2)}, u32[]{:S(2)}) collective-permute-start(bf16[1,384,256]{2,1,0:T(8,128)(2,1)S(1)} %get-tuple-element.142), channel_id=1, source_target_pairs={{0,8},{8,0},{16,24},{24,16},{1,9},{9,1},{17,25},{25,17},{2,10},{10... | collective-permute-start | bytes 589832 | tf_op jit(solution)/shard_map/ppermute | solution.py:19
  179.6 1.6 collective-permute-start.26
  181.1 2.0 shard_map.258
  183.1 1.5 collective-permute-start.27
  184.6 5.4 %collective-permute-done.53 = bf16[1,384,256]{2,1,0:T(8,128)(2,1)S(1)} collective-permute-done((bf16[1,384,256]{2,1,0:T(8,128)(2,1)S(1)}, bf16[1,384,256]{2,1,0:T(8,128)(2,1)S(1)}, u32[]{:S(2)}, u32[]{:S(2)}) %collective-permute-start.53) | collective-permute-done | bytes 196640 | tf_op jit(solution)/shard_map/ppermute | solution.py:19
  190.2 2.2 collective-permute-start.45
  192.5 2.1 collective-permute-start.44
  195.2 11.9 %collective-permute-start.58 = (bf16[1,128,256]{2,1,0:T(8,128)(2,1)S(1)}, bf16[1,128,256]{2,1,0:T(8,128)(2,1)S(1)}, u32[]{:S(2)}, u32[]{:S(2)}) collective-permute-start(bf16[1,128,256]{2,1,0:T(8,128)(2,1)S(1)} %slice.40), channel_id=1, source_target_pairs={{0,1},{1,0},{2,3},{3,2},{4,5},{5,4},{6,7},{7,6},{8,9},{9,8},{10,11... | collective-permute-start | bytes 196616 | tf_op jit(solution)/shard_map/ppermute | solution.py:19
  208.2 8.8 %collective-permute-done.44 = bf16[2,256,256]{2,1,0:T(8,128)(2,1)S(1)} collective-permute-done((bf16[2,256,256]{2,1,0:T(8,128)(2,1)S(1)}, bf16[2,256,256]{2,1,0:T(8,128)(2,1)S(1)}, u32[]{:S(2)}, u32[]{:S(2)}) %collective-permute-start.44) | collective-permute-done | bytes 262176 | tf_op jit(solution)/shard_map/ppermute | solution.py:19
  217.5 1.1 collective-permute-start.60
  224.7 10.3 %collective-permute-done.61.rest_11_ = bf16[1,128,256]{2,1,0:T(8,128)(2,1)} collective-permute-done((bf16[1,128,256]{2,1,0:T(8,128)(2,1)S(1)}, bf16[1,128,256]{2,1,0:T(8,128)(2,1)}, u32[]{:S(2)}, u32[]{:S(2)}) %collective-permute-start.61) | collective-permute-done | bytes 65568 | tf_op jit(solution)/shard_map/ppermute | solution.py:19
  236.6 1.2 slice_bitcast_fusion
  238.9 2.0 shard_map.256
  240.9 1.9 collective-permute-done.56.rest_6_
  242.8 2.8 %collective-permute-done.57.rest_7_ = bf16[1,384,256]{2,1,0:T(8,128)(2,1)S(1)} collective-permute-done((bf16[1,384,256]{2,1,0:T(8,128)(2,1)S(1)}, bf16[1,384,256]{2,1,0:T(8,128)(2,1)S(1)}, u32[]{:S(2)}, u32[]{:S(2)}) %collective-permute-start.57) | collective-permute-done | bytes 196640 | tf_op jit(solution)/shard_map/ppermute | solution.py:19
  245.6 3.4 %shard_map.260 = (f32[256,1024]{1,0:T(8,128)}, f32[1024,256]{1,0:T(8,128)}, f32[256,1024]{1,0:T(8,128)}, f32[256,256]{1,0:T(8,128)}, f32[256,16]{1,0:T(8,128)S(1)}) custom-call(s32[3]{0:T(128)S(1)} %pad_add_fusion.place, bf16[2,256,256]{2,1,0:T(8,128)(2,1)S(1)} %add_convert_fusion.1.rest_0_, bf16[2,256,256]{2,1,0:T(8,128)(2,1)S(1)} %collective-permute-done.46.rest_1_, ...), custom_call_target="tpu_custom_call" | custom-call | bytes 2097152 | tf_op jit(solution)/shard_map/pallas_call | solution.py:39
  (168 shorter events, 29.9 us)
Async XLA Ops:
  7.2 64.4 %copy-start.6 = (bf16[256,1024]{1,0:T(8,128)(2,1)S(1)}, bf16[256,1024]{1,0:T(8,128)(2,1)}, u32[]{:S(2)}) copy-start(bf16[256,1024]{1,0:T(8,128)(2,1)} %xp.3) | copy-start | bytes 1572868
  7.2 64.4 %copy-start.20 = (bf16[256,256]{1,0:T(8,128)(2,1)S(1)}, bf16[256,256]{1,0:T(8,128)(2,1)}, u32[]{:S(2)}) copy-start(bf16[256,256]{1,0:T(8,128)(2,1)} %bcp.3) | copy-start | bytes 393220
  7.3 10.6 %collective-permute-start.3 = (bf16[64,1408]{1,0:T(8,128)(2,1)S(1)}, bf16[64,1408]{1,0:T(8,128)(2,1)S(1)}, u32[]{:S(2)}, u32[]{:S(2)}) collective-permute-start(bf16[64,1408]{1,0:T(8,128)(2,1)S(1)} %get-tuple-element.84), channel_id=1, source_target_pairs={{0,24},{8,16},{16,8},{24,0},{1,25},{9,17},{17,9},{25,1},{2,26},{10... | collective-permute-start | bytes 540680 | tf_op jit(solution)/shard_map/ppermute | solution.py:19
  12.4 15.3 %collective-permute-start.2 = (bf16[64,1408]{1,0:T(8,128)(2,1)S(1)}, bf16[64,1408]{1,0:T(8,128)(2,1)S(1)}, u32[]{:S(2)}, u32[]{:S(2)}) collective-permute-start(bf16[64,1408]{1,0:T(8,128)(2,1)S(1)} %get-tuple-element.84), channel_id=1, source_target_pairs={{0,16},{8,24},{16,0},{24,8},{1,17},{9,25},{17,1},{25,9},{2,18},{10... | collective-permute-start | bytes 540680 | tf_op jit(solution)/shard_map/ppermute | solution.py:19
  12.4 15.3 %collective-permute-start.1 = (bf16[64,1408]{1,0:T(8,128)(2,1)S(1)}, bf16[64,1408]{1,0:T(8,128)(2,1)S(1)}, u32[]{:S(2)}, u32[]{:S(2)}) collective-permute-start(bf16[64,1408]{1,0:T(8,128)(2,1)S(1)} %get-tuple-element.84), channel_id=1, source_target_pairs={{0,8},{8,0},{16,24},{24,16},{1,9},{9,1},{17,25},{25,17},{2,10},{10... | collective-permute-start | bytes 540680 | tf_op jit(solution)/shard_map/ppermute | solution.py:19
  27.8 13.4 %collective-permute-start.5 = (bf16[3,64,1408]{2,1,0:T(8,128)(2,1)S(1)}, bf16[3,64,1408]{2,1,0:T(8,128)(2,1)S(1)}, u32[]{:S(2)}, u32[]{:S(2)}) collective-permute-start(bf16[3,64,1408]{2,1,0:T(8,128)(2,1)S(1)} %pad_maximum_fusion.rest_0_), channel_id=1, source_target_pairs={{0,4},{2,6},{4,0},{6,2},{1,5},{3,7},{5,1},{7,3},{8,12},{10,14},{12... | collective-permute-start | bytes 1622024 | tf_op jit(solution)/shard_map/ppermute | solution.py:19
  29.3 37.2 %collective-permute-start.4 = (bf16[3,64,1408]{2,1,0:T(8,128)(2,1)S(1)}, bf16[3,64,1408]{2,1,0:T(8,128)(2,1)S(1)}, u32[]{:S(2)}, u32[]{:S(2)}) collective-permute-start(bf16[3,64,1408]{2,1,0:T(8,128)(2,1)S(1)} %pad_maximum_fusion.rest_0_), channel_id=1, source_target_pairs={{0,2},{2,0},{4,6},{6,4},{1,3},{3,1},{5,7},{7,5},{8,10},{10,8},{12,... | collective-permute-start | bytes 1622024 | tf_op jit(solution)/shard_map/ppermute | solution.py:19
  41.1 30.5 %collective-permute-start.6 = (bf16[3,64,1408]{2,1,0:T(8,128)(2,1)S(1)}, bf16[3,64,1408]{2,1,0:T(8,128)(2,1)S(1)}, u32[]{:S(2)}, u32[]{:S(2)}) collective-permute-start(bf16[3,64,1408]{2,1,0:T(8,128)(2,1)S(1)} %collective-permute-done.5.rest_2_), channel_id=1, source_target_pairs={{0,2},{2,0},{4,6},{6,4},{1,3},{3,1},{5,7},{7,5},{8,10},{10,8},{12,... | collective-permute-start | bytes 1622024 | tf_op jit(solution)/shard_map/ppermute | solution.py:19
  41.1 8.2 %collective-permute-start.12 = (bf16[64,1024]{1,0:T(8,128)(2,1)S(1)}, bf16[64,1024]{1,0:T(8,128)(2,1)S(1)}, u32[]{:S(2)}, u32[]{:S(2)}) collective-permute-start(bf16[64,1024]{1,0:T(8,128)(2,1)S(1)} %get-tuple-element.94), channel_id=1, source_target_pairs={{0,24},{8,16},{16,8},{24,0},{1,25},{9,17},{17,9},{25,1},{2,26},{10... | collective-permute-start | bytes 393224 | tf_op jit(solution)/shard_map/ppermute | solution.py:19
  43.4 11.5 %collective-permute-start.11 = (bf16[64,1024]{1,0:T(8,128)(2,1)S(1)}, bf16[64,1024]{1,0:T(8,128)(2,1)S(1)}, u32[]{:S(2)}, u32[]{:S(2)}) collective-permute-start(bf16[64,1024]{1,0:T(8,128)(2,1)S(1)} %get-tuple-element.94), channel_id=1, source_target_pairs={{0,16},{8,24},{16,0},{24,8},{1,17},{9,25},{17,1},{25,9},{2,18},{10... | collective-permute-start | bytes 393224 | tf_op jit(solution)/shard_map/ppermute | solution.py:19
  43.4 11.5 %collective-permute-start.10 = (bf16[64,1024]{1,0:T(8,128)(2,1)S(1)}, bf16[64,1024]{1,0:T(8,128)(2,1)S(1)}, u32[]{:S(2)}, u32[]{:S(2)}) collective-permute-start(bf16[64,1024]{1,0:T(8,128)(2,1)S(1)} %get-tuple-element.94), channel_id=1, source_target_pairs={{0,8},{8,0},{16,24},{24,16},{1,9},{9,1},{17,25},{25,17},{2,10},{10... | collective-permute-start | bytes 393224 | tf_op jit(solution)/shard_map/ppermute | solution.py:19
  49.4 9.2 %collective-permute-start.15 = (bf16[256,256]{1,0:T(8,128)(2,1)S(1)}, bf16[256,256]{1,0:T(8,128)(2,1)S(1)}, u32[]{:S(2)}, u32[]{:S(2)}) collective-permute-start(bf16[256,256]{1,0:T(8,128)(2,1)S(1)} %get-tuple-element.95), channel_id=1, source_target_pairs={{0,24},{8,16},{16,8},{24,0},{1,25},{9,17},{17,9},{25,1},{2,26},{10... | collective-permute-start | bytes 393224 | tf_op jit(solution)/shard_map/ppermute | solution.py:19
  55.0 10.8 %collective-permute-start.14 = (bf16[256,256]{1,0:T(8,128)(2,1)S(1)}, bf16[256,256]{1,0:T(8,128)(2,1)S(1)}, u32[]{:S(2)}, u32[]{:S(2)}) collective-permute-start(bf16[256,256]{1,0:T(8,128)(2,1)S(1)} %get-tuple-element.95), channel_id=1, source_target_pairs={{0,16},{8,24},{16,0},{24,8},{1,17},{9,25},{17,1},{25,9},{2,18},{10... | collective-permute-start | bytes 393224 | tf_op jit(solution)/shard_map/ppermute | solution.py:19
  55.0 10.8 %collective-permute-start.13 = (bf16[256,256]{1,0:T(8,128)(2,1)S(1)}, bf16[256,256]{1,0:T(8,128)(2,1)S(1)}, u32[]{:S(2)}, u32[]{:S(2)}) collective-permute-start(bf16[256,256]{1,0:T(8,128)(2,1)S(1)} %get-tuple-element.95), channel_id=1, source_target_pairs={{0,8},{8,0},{16,24},{24,16},{1,9},{9,1},{17,25},{25,17},{2,10},{10... | collective-permute-start | bytes 393224 | tf_op jit(solution)/shard_map/ppermute | solution.py:19
  66.6 29.4 %collective-permute-start.17 = (bf16[3,64,1024]{2,1,0:T(8,128)(2,1)}, bf16[3,64,1024]{2,1,0:T(8,128)(2,1)}, u32[]{:S(2)}, u32[]{:S(2)}) collective-permute-start(bf16[3,64,1024]{2,1,0:T(8,128)(2,1)} %pad_maximum_fusion.1.rest_0_), channel_id=1, source_target_pairs={{0,4},{2,6},{4,0},{6,2},{1,5},{3,7},{5,1},{7,3},{8,12},{10,14},{12... | collective-permute-start | bytes 1179656 | tf_op jit(solution)/shard_map/ppermute | solution.py:19
  68.1 28.0 %collective-permute-start.20 = (bf16[3,256,256]{2,1,0:T(8,128)(2,1)}, bf16[3,256,256]{2,1,0:T(8,128)(2,1)}, u32[]{:S(2)}, u32[]{:S(2)}) collective-permute-start(bf16[3,256,256]{2,1,0:T(8,128)(2,1)} %pad_maximum_fusion.2.rest_4_), channel_id=1, source_target_pairs={{0,4},{2,6},{4,0},{6,2},{1,5},{3,7},{5,1},{7,3},{8,12},{10,14},{12... | collective-permute-start | bytes 1179656 | tf_op jit(solution)/shard_map/ppermute | solution.py:19
  68.6 2.2 collective-permute-start
  81.1 15.9 %collective-permute-start.7 = (bf16[1024,128]{1,0:T(8,128)(2,1)S(1)}, bf16[1024,128]{1,0:T(8,128)(2,1)S(1)}, u32[]{:S(2)}, u32[]{:S(2)}) collective-permute-start(bf16[1024,128]{1,0:T(8,128)(2,1)S(1)} %get-tuple-element.85.state), channel_id=1, source_target_pairs={{0,2},{2,0},{4,6},{6,4},{1,3},{3,1},{5,7},{7,5},{8,10},{10,8},{12,... | collective-permute-start | bytes 786440 | tf_op jit(solution)/shard_map/ppermute | solution.py:19
  95.5 1.2 collective-permute-start.8
  95.6 6.5 %collective-permute-start.16 = (bf16[3,64,1024]{2,1,0:T(8,128)(2,1)}, bf16[3,64,1024]{2,1,0:T(8,128)(2,1)}, u32[]{:S(2)}, u32[]{:S(2)}) collective-permute-start(bf16[3,64,1024]{2,1,0:T(8,128)(2,1)} %pad_maximum_fusion.1.rest_0_), channel_id=1, source_target_pairs={{0,2},{2,0},{4,6},{6,4},{1,3},{3,1},{5,7},{7,5},{8,10},{10,8},{12,... | collective-permute-start | bytes 1179656 | tf_op jit(solution)/shard_map/ppermute | solution.py:19
  96.0 6.0 %collective-permute-start.19 = (bf16[3,256,256]{2,1,0:T(8,128)(2,1)}, bf16[3,256,256]{2,1,0:T(8,128)(2,1)}, u32[]{:S(2)}, u32[]{:S(2)}) collective-permute-start(bf16[3,256,256]{2,1,0:T(8,128)(2,1)} %pad_maximum_fusion.2.rest_4_), channel_id=1, source_target_pairs={{0,2},{2,0},{4,6},{6,4},{1,3},{3,1},{5,7},{7,5},{8,10},{10,8},{12,... | collective-permute-start | bytes 1179656 | tf_op jit(solution)/shard_map/ppermute | solution.py:19
  96.1 6.0 %collective-permute-start.18 = (bf16[3,64,1024]{2,1,0:T(8,128)(2,1)}, bf16[3,64,1024]{2,1,0:T(8,128)(2,1)}, u32[]{:S(2)}, u32[]{:S(2)}) collective-permute-start(bf16[3,64,1024]{2,1,0:T(8,128)(2,1)} %collective-permute-done.17.rest_2_), channel_id=1, source_target_pairs={{0,2},{2,0},{4,6},{6,4},{1,3},{3,1},{5,7},{7,5},{8,10},{10,8},{12,... | collective-permute-start | bytes 1179656 | tf_op jit(solution)/shard_map/ppermute | solution.py:19
  96.7 5.4 %collective-permute-start.21 = (bf16[3,256,256]{2,1,0:T(8,128)(2,1)}, bf16[3,256,256]{2,1,0:T(8,128)(2,1)}, u32[]{:S(2)}, u32[]{:S(2)}) collective-permute-start(bf16[3,256,256]{2,1,0:T(8,128)(2,1)} %collective-permute-done.20.rest_6_), channel_id=1, source_target_pairs={{0,2},{2,0},{4,6},{6,4},{1,3},{3,1},{5,7},{7,5},{8,10},{10,8},{12,... | collective-permute-start | bytes 1179656 | tf_op jit(solution)/shard_map/ppermute | solution.py:19
  99.3 9.7 %collective-permute-start.9 = (bf16[1024,128]{1,0:T(8,128)(2,1)}, bf16[1024,128]{1,0:T(8,128)(2,1)}, u32[]{:S(2)}, u32[]{:S(2)}) collective-permute-start(bf16[1024,128]{1,0:T(8,128)(2,1)} %get-tuple-element.87), channel_id=1, source_target_pairs={{0,4},{2,6},{4,0},{6,2},{1,5},{3,7},{5,1},{7,3},{8,12},{10,14},{12... | collective-permute-start | bytes 786440 | tf_op jit(solution)/shard_map/ppermute | solution.py:19
  111.2 3.7 %collective-permute-start.22 = (f32[8,256]{1,0:T(8,128)S(1)}, f32[8,256]{1,0:T(8,128)S(1)}, u32[]{:S(2)}, u32[]{:S(2)}) collective-permute-start(f32[8,256]{1,0:T(8,128)S(1)} %get-tuple-element.100.mine), channel_id=1, source_target_pairs={{0,1},{1,0},{2,3},{3,2},{4,5},{5,4},{6,7},{7,6},{8,9},{9,8},{10,11... | collective-permute-start | bytes 24584 | tf_op jit(solution)/shard_map/ppermute | solution.py:19
  117.2 2.3 collective-permute-start.24
  117.3 29.7 %collective-permute-start.40 = (bf16[256,1024]{1,0:T(8,128)(2,1)S(1)}, bf16[256,1024]{1,0:T(8,128)(2,1)S(1)}, u32[]{:S(2)}, u32[]{:S(2)}) collective-permute-start(bf16[256,1024]{1,0:T(8,128)(2,1)S(1)} %bitcast.37), channel_id=1, source_target_pairs={{0,2},{2,0},{4,6},{6,4},{1,3},{3,1},{5,7},{7,5},{8,10},{10,8},{12,... | collective-permute-start | bytes 1572872 | tf_op jit(solution)/shard_map/ppermute | solution.py:19
  117.8 30.8 %collective-permute-start.38 = (bf16[272,1024]{1,0:T(8,128)(2,1)S(1)}, bf16[272,1024]{1,0:T(8,128)(2,1)S(1)}, u32[]{:S(2)}, u32[]{:S(2)}) collective-permute-start(bf16[272,1024]{1,0:T(8,128)(2,1)S(1)} %shard_map.246.normed.rest_4_), channel_id=1, source_target_pairs={{0,4},{2,6},{4,0},{6,2},{1,5},{3,7},{5,1},{7,3},{8,12},{10,14},{12... | collective-permute-start | bytes 1671176 | tf_op jit(solution)/shard_map/ppermute | solution.py:19
  121.0 17.9 %collective-permute-start.25 = (bf16[1024,128]{1,0:T(8,128)(2,1)S(1)}, bf16[1024,128]{1,0:T(8,128)(2,1)S(1)}, u32[]{:S(2)}, u32[]{:S(2)}) collective-permute-start(bf16[1024,128]{1,0:T(8,128)(2,1)S(1)} %get-tuple-element.108), channel_id=1, source_target_pairs={{0,4},{2,6},{4,0},{6,2},{1,5},{3,7},{5,1},{7,3},{8,12},{10,14},{12... | collective-permute-start | bytes 786440 | tf_op jit(solution)/shard_map/ppermute | solution.py:19
  122.0 27.3 %collective-permute-start.41 = (bf16[256,1024]{1,0:T(8,128)(2,1)S(1)}, bf16[256,1024]{1,0:T(8,128)(2,1)S(1)}, u32[]{:S(2)}, u32[]{:S(2)}) collective-permute-start(bf16[256,1024]{1,0:T(8,128)(2,1)S(1)} %bitcast.38), channel_id=1, source_target_pairs={{0,4},{2,6},{4,0},{6,2},{1,5},{3,7},{5,1},{7,3},{8,12},{10,14},{12... | collective-permute-start | bytes 1572872 | tf_op jit(solution)/shard_map/ppermute | solution.py:19
  123.0 31.2 %collective-permute-start.37 = (bf16[272,1024]{1,0:T(8,128)(2,1)S(1)}, bf16[272,1024]{1,0:T(8,128)(2,1)S(1)}, u32[]{:S(2)}, u32[]{:S(2)}) collective-permute-start(bf16[272,1024]{1,0:T(8,128)(2,1)S(1)} %shard_map.246.normed.rest_4_), channel_id=1, source_target_pairs={{0,2},{2,0},{4,6},{6,4},{1,3},{3,1},{5,7},{7,5},{8,10},{10,8},{12,... | collective-permute-start | bytes 1671176 | tf_op jit(solution)/shard_map/ppermute | solution.py:19
  138.9 13.9 %collective-permute-start.34 = (bf16[2,256,256]{2,1,0:T(8,128)(2,1)S(1)}, bf16[2,256,256]{2,1,0:T(8,128)(2,1)S(1)}, u32[]{:S(2)}, u32[]{:S(2)}) collective-permute-start(bf16[2,256,256]{2,1,0:T(8,128)(2,1)S(1)} %get-tuple-element.128), channel_id=1, source_target_pairs={{0,2},{2,0},{4,6},{6,4},{1,3},{3,1},{5,7},{7,5},{8,10},{10,8},{12,... | collective-permute-start | bytes 786440 | tf_op jit(solution)/shard_map/ppermute | solution.py:19
  147.0 4.0 %collective-permute-start.29 = (f32[8,1024]{1,0:T(8,128)S(1)}, f32[8,1024]{1,0:T(8,128)S(1)}, u32[]{:S(2)}, u32[]{:S(2)}) collective-permute-start(f32[8,1024]{1,0:T(8,128)S(1)} %get-tuple-element.126), channel_id=1, source_target_pairs={{0,1},{1,0},{2,3},{3,2},{4,5},{5,4},{6,7},{7,6},{8,9},{9,8},{10,11... | collective-permute-start | bytes 98312 | tf_op jit(solution)/shard_map/ppermute | solution.py:19
  148.6 18.4 %collective-permute-start.39 = (bf16[272,1024]{1,0:T(8,128)(2,1)S(1)}, bf16[272,1024]{1,0:T(8,128)(2,1)S(1)}, u32[]{:S(2)}, u32[]{:S(2)}) collective-permute-start(bf16[272,1024]{1,0:T(8,128)(2,1)S(1)} %collective-permute-done.38.rest_6_), channel_id=1, source_target_pairs={{0,2},{2,0},{4,6},{6,4},{1,3},{3,1},{5,7},{7,5},{8,10},{10,8},{12,... | collective-permute-start | bytes 1671176 | tf_op jit(solution)/shard_map/ppermute | solution.py:19
  149.3 8.9 %collective-permute-start.49 = (bf16[272,384]{1,0:T(8,128)(2,1)S(1)}, bf16[272,384]{1,0:T(8,128)(2,1)S(1)}, u32[]{:S(2)}, u32[]{:S(2)}) collective-permute-start(bf16[272,384]{1,0:T(8,128)(2,1)S(1)} %get-tuple-element.138), channel_id=1, source_target_pairs={{0,2},{2,0},{4,6},{6,4},{1,3},{3,1},{5,7},{7,5},{8,10},{10,8},{12,... | collective-permute-start | bytes 626696 | tf_op jit(solution)/shard_map/ppermute | solution.py:19
  151.0 8.9 %collective-permute-start.50 = (bf16[272,384]{1,0:T(8,128)(2,1)S(1)}, bf16[272,384]{1,0:T(8,128)(2,1)S(1)}, u32[]{:S(2)}, u32[]{:S(2)}) collective-permute-start(bf16[272,384]{1,0:T(8,128)(2,1)S(1)} %get-tuple-element.139), channel_id=1, source_target_pairs={{0,4},{2,6},{4,0},{6,2},{1,5},{3,7},{5,1},{7,3},{8,12},{10,14},{12... | collective-permute-start | bytes 626696 | tf_op jit(solution)/shard_map/ppermute | solution.py:19
  152.8 1.2 collective-permute-start.30
  154.0 25.5 %collective-permute-start.42 = (bf16[256,1024]{1,0:T(8,128)(2,1)S(1)}, bf16[256,1024]{1,0:T(8,128)(2,1)S(1)}, u32[]{:S(2)}, u32[]{:S(2)}) collective-permute-start(bf16[256,1024]{1,0:T(8,128)(2,1)S(1)} %collective-permute-done.41.rest_10_), channel_id=1, source_target_pairs={{0,2},{2,0},{4,6},{6,4},{1,3},{3,1},{5,7},{7,5},{8,10},{10,8},{12,... | collective-permute-start | bytes 1572872 | tf_op jit(solution)/shard_map/ppermute | solution.py:19
  154.2 4.0 %collective-permute-start.31 = (f32[8,1024]{1,0:T(8,128)S(1)}, f32[8,1024]{1,0:T(8,128)S(1)}, u32[]{:S(2)}, u32[]{:S(2)}) collective-permute-start(f32[8,1024]{1,0:T(8,128)S(1)} %add.42), channel_id=1, source_target_pairs={{0,4},{2,6},{4,0},{6,2},{1,5},{3,7},{5,1},{7,3},{8,12},{10,14},{12... | collective-permute-start | bytes 98312 | tf_op jit(solution)/shard_map/ppermute | solution.py:19
  158.2 7.3 %collective-permute-start.51 = (bf16[272,384]{1,0:T(8,128)(2,1)S(1)}, bf16[272,384]{1,0:T(8,128)(2,1)S(1)}, u32[]{:S(2)}, u32[]{:S(2)}) collective-permute-start(bf16[272,384]{1,0:T(8,128)(2,1)S(1)} %get-tuple-element.140), channel_id=1, source_target_pairs={{0,6},{2,4},{4,2},{6,0},{1,7},{3,5},{5,3},{7,1},{8,14},{10,12},{12... | collective-permute-start | bytes 626696 | tf_op jit(solution)/shard_map/ppermute | solution.py:19
  158.2 13.3 %collective-permute-start.35 = (bf16[2,256,256]{2,1,0:T(8,128)(2,1)S(1)}, bf16[2,256,256]{2,1,0:T(8,128)(2,1)S(1)}, u32[]{:S(2)}, u32[]{:S(2)}) collective-permute-start(bf16[2,256,256]{2,1,0:T(8,128)(2,1)S(1)} %get-tuple-element.129), channel_id=1, source_target_pairs={{0,4},{2,6},{4,0},{6,2},{1,5},{3,7},{5,1},{7,3},{8,12},{10,14},{12... | collective-permute-start | bytes 786440 | tf_op jit(solution)/shard_map/ppermute | solution.py:19
  159.9 16.8 %collective-permute-start.36 = (bf16[2,256,256]{2,1,0:T(8,128)(2,1)S(1)}, bf16[2,256,256]{2,1,0:T(8,128)(2,1)S(1)}, u32[]{:S(2)}, u32[]{:S(2)}) collective-permute-start(bf16[2,256,256]{2,1,0:T(8,128)(2,1)S(1)} %get-tuple-element.130), channel_id=1, source_target_pairs={{0,6},{2,4},{4,2},{6,0},{1,7},{3,5},{5,3},{7,1},{8,14},{10,12},{12... | collective-permute-start | bytes 786440 | tf_op jit(solution)/shard_map/ppermute | solution.py:19
  165.5 27.0 %collective-permute-start.23 = (bf16[256,1024]{1,0:T(8,128)(2,1)S(1)}, bf16[256,1024]{1,0:T(8,128)(2,1)S(1)}, u32[]{:S(2)}, u32[]{:S(2)}) collective-permute-start(bf16[256,1024]{1,0:T(8,128)(2,1)S(1)} %get-tuple-element.106), channel_id=1, source_target_pairs={{0,1},{1,0},{2,3},{3,2},{4,5},{5,4},{6,7},{7,6},{8,9},{9,8},{10,11... | collective-permute-start | bytes 1572872 | tf_op jit(solution)/shard_map/ppermute | solution.py:19
  167.0 9.7 %collective-permute-start.32 = (f32[8,1024]{1,0:T(8,128)S(1)}, f32[8,1024]{1,0:T(8,128)S(1)}, u32[]{:S(2)}, u32[]{:S(2)}) collective-permute-start(f32[8,1024]{1,0:T(8,128)S(1)} %add.43), channel_id=1, source_target_pairs={{0,8},{8,0},{16,24},{24,16},{1,9},{9,1},{17,25},{25,17},{2,10},{10... | collective-permute-start | bytes 98312 | tf_op jit(solution)/shard_map/ppermute | solution.py:19
  171.5 11.6 %collective-permute-start.54 = (bf16[1,384,256]{2,1,0:T(8,128)(2,1)S(1)}, bf16[1,384,256]{2,1,0:T(8,128)(2,1)S(1)}, u32[]{:S(2)}, u32[]{:S(2)}) collective-permute-start(bf16[1,384,256]{2,1,0:T(8,128)(2,1)S(1)} %get-tuple-element.144), channel_id=1, source_target_pairs={{0,24},{8,16},{16,8},{24,0},{1,25},{9,17},{17,9},{25,1},{2,26},{10... | collective-permute-start | bytes 589832 | tf_op jit(solution)/shard_map/ppermute | solution.py:19
  176.7 13.4 %collective-permute-start.53 = (bf16[1,384,256]{2,1,0:T(8,128)(2,1)S(1)}, bf16[1,384,256]{2,1,0:T(8,128)(2,1)S(1)}, u32[]{:S(2)}, u32[]{:S(2)}) collective-permute-start(bf16[1,384,256]{2,1,0:T(8,128)(2,1)S(1)} %get-tuple-element.143), channel_id=1, source_target_pairs={{0,16},{8,24},{16,0},{24,8},{1,17},{9,25},{17,1},{25,9},{2,18},{10... | collective-permute-start | bytes 589832 | tf_op jit(solution)/shard_map/ppermute | solution.py:19
  176.7 13.5 %collective-permute-start.52 = (bf16[1,384,256]{2,1,0:T(8,128)(2,1)S(1)}, bf16[1,384,256]{2,1,0:T(8,128)(2,1)S(1)}, u32[]{:S(2)}, u32[]{:S(2)}) collective-permute-start(bf16[1,384,256]{2,1,0:T(8,128)(2,1)S(1)} %get-tuple-element.142), channel_id=1, source_target_pairs={{0,8},{8,0},{16,24},{24,16},{1,9},{9,1},{17,25},{25,17},{2,10},{10... | collective-permute-start | bytes 589832 | tf_op jit(solution)/shard_map/ppermute | solution.py:19
  179.6 39.2 %collective-permute-start.26 = (bf16[256,1024]{1,0:T(8,128)(2,1)S(1)}, bf16[256,1024]{1,0:T(8,128)(2,1)S(1)}, u32[]{:S(2)}, u32[]{:S(2)}) collective-permute-start(bf16[256,1024]{1,0:T(8,128)(2,1)S(1)} %get-tuple-element.124), channel_id=1, source_target_pairs={{0,1},{1,0},{2,3},{3,2},{4,5},{5,4},{6,7},{7,6},{8,9},{9,8},{10,11... | collective-permute-start | bytes 1572872 | tf_op jit(solution)/shard_map/ppermute | solution.py:19
  183.1 11.5 %collective-permute-start.27 = (bf16[16,1024]{1,0:T(8,128)(2,1)S(1)}, bf16[16,1024]{1,0:T(8,128)(2,1)S(1)}, u32[]{:S(2)}, u32[]{:S(2)}) collective-permute-start(bf16[16,1024]{1,0:T(8,128)(2,1)S(1)} %get-tuple-element.125), channel_id=1, source_target_pairs={{2,0},{4,2},{6,4},{3,1},{5,3},{7,5},{10,8},{12,10},{14,12},{11,9},... | collective-permute-start | bytes 98312 | tf_op jit(solution)/shard_map/ppermute | solution.py:817
  190.1 5.2 %collective-permute-start.33 = (f32[8,1024]{1,0:T(8,128)S(1)}, f32[8,1024]{1,0:T(8,128)S(1)}, u32[]{:S(2)}, u32[]{:S(2)}) collective-permute-start(f32[8,1024]{1,0:T(8,128)S(1)} %add.44), channel_id=1, source_target_pairs={{0,16},{8,24},{16,0},{24,8},{1,17},{9,25},{17,1},{25,9},{2,18},{10... | collective-permute-start | bytes 98312 | tf_op jit(solution)/shard_map/ppermute | solution.py:19
  190.2 17.9 %collective-permute-start.45 = (bf16[2,256,256]{2,1,0:T(8,128)(2,1)S(1)}, bf16[2,256,256]{2,1,0:T(8,128)(2,1)S(1)}, u32[]{:S(2)}, u32[]{:S(2)}) collective-permute-start(bf16[2,256,256]{2,1,0:T(8,128)(2,1)S(1)} %get-tuple-element.136), channel_id=1, source_target_pairs={{0,24},{8,16},{16,8},{24,0},{1,25},{9,17},{17,9},{25,1},{2,26},{10... | collective-permute-start | bytes 786440 | tf_op jit(solution)/shard_map/ppermute | solution.py:19
  192.5 24.5 %collective-permute-start.44 = (bf16[2,256,256]{2,1,0:T(8,128)(2,1)S(1)}, bf16[2,256,256]{2,1,0:T(8,128)(2,1)S(1)}, u32[]{:S(2)}, u32[]{:S(2)}) collective-permute-start(bf16[2,256,256]{2,1,0:T(8,128)(2,1)S(1)} %get-tuple-element.135), channel_id=1, source_target_pairs={{0,16},{8,24},{16,0},{24,8},{1,17},{9,25},{17,1},{25,9},{2,18},{10... | collective-permute-start | bytes 786440 | tf_op jit(solution)/shard_map/ppermute | solution.py:19
  194.6 22.9 %collective-permute-start.43 = (bf16[2,256,256]{2,1,0:T(8,128)(2,1)S(1)}, bf16[2,256,256]{2,1,0:T(8,128)(2,1)S(1)}, u32[]{:S(2)}, u32[]{:S(2)}) collective-permute-start(bf16[2,256,256]{2,1,0:T(8,128)(2,1)S(1)} %get-tuple-element.134), channel_id=1, source_target_pairs={{0,8},{8,0},{16,24},{24,16},{1,9},{9,1},{17,25},{25,17},{2,10},{10... | collective-permute-start | bytes 786440 | tf_op jit(solution)/shard_map/ppermute | solution.py:19
  195.2 21.7 %collective-permute-start.58 = (bf16[1,128,256]{2,1,0:T(8,128)(2,1)S(1)}, bf16[1,128,256]{2,1,0:T(8,128)(2,1)S(1)}, u32[]{:S(2)}, u32[]{:S(2)}) collective-permute-start(bf16[1,128,256]{2,1,0:T(8,128)(2,1)S(1)} %slice.40), channel_id=1, source_target_pairs={{0,1},{1,0},{2,3},{3,2},{4,5},{5,4},{6,7},{7,6},{8,9},{9,8},{10,11... | collective-permute-start | bytes 196616 | tf_op jit(solution)/shard_map/ppermute | solution.py:19
  208.1 10.6 %collective-permute-start.28 = (bf16[16,1024]{1,0:T(8,128)(2,1)S(1)}, bf16[16,1024]{1,0:T(8,128)(2,1)S(1)}, u32[]{:S(2)}, u32[]{:S(2)}) collective-permute-start(bf16[16,1024]{1,0:T(8,128)(2,1)S(1)} %collective-permute-done.27.edge), channel_id=1, source_target_pairs={{0,1},{1,0},{2,3},{3,2},{4,5},{5,4},{6,7},{7,6},{8,9},{9,8},{10,11... | collective-permute-start | bytes 98312 | tf_op jit(solution)/shard_map/ppermute | solution.py:19
  217.0 19.0 %collective-permute-start.55 = (bf16[1,384,256]{2,1,0:T(8,128)(2,1)S(1)}, bf16[1,384,256]{2,1,0:T(8,128)(2,1)}, u32[]{:S(2)}, u32[]{:S(2)}) collective-permute-start(bf16[1,384,256]{2,1,0:T(8,128)(2,1)S(1)} %add_convert_fusion.2.rest_4_), channel_id=1, source_target_pairs={{0,2},{2,0},{4,6},{6,4},{1,3},{3,1},{5,7},{7,5},{8,10},{10,8},{12,... | collective-permute-start | bytes 589832 | tf_op jit(solution)/shard_map/ppermute | solution.py:19
  217.0 3.6 %collective-permute-start.59 = (bf16[1,128,256]{2,1,0:T(8,128)(2,1)S(1)}, bf16[1,128,256]{2,1,0:T(8,128)(2,1)S(1)}, u32[]{:S(2)}, u32[]{:S(2)}) collective-permute-start(bf16[1,128,256]{2,1,0:T(8,128)(2,1)S(1)} %collective-permute-done.58.rest_8_), channel_id=1, source_target_pairs={{0,2},{2,0},{4,6},{6,4},{1,3},{3,1},{5,7},{7,5},{8,10},{10,8},{12,... | collective-permute-start | bytes 196616 | tf_op jit(solution)/shard_map/ppermute | solution.py:19
  217.5 4.3 %collective-permute-start.60 = (bf16[1,128,256]{2,1,0:T(8,128)(2,1)S(1)}, bf16[1,128,256]{2,1,0:T(8,128)(2,1)S(1)}, u32[]{:S(2)}, u32[]{:S(2)}) collective-permute-start(bf16[1,128,256]{2,1,0:T(8,128)(2,1)S(1)} %collective-permute-done.58.rest_8_), channel_id=1, source_target_pairs={{0,4},{2,6},{4,0},{6,2},{1,5},{3,7},{5,1},{7,3},{8,12},{10,14},{12... | collective-permute-start | bytes 196616 | tf_op jit(solution)/shard_map/ppermute | solution.py:19
  218.7 26.8 %collective-permute-start.46 = (bf16[2,256,256]{2,1,0:T(8,128)(2,1)S(1)}, bf16[2,256,256]{2,1,0:T(8,128)(2,1)S(1)}, u32[]{:S(2)}, u32[]{:S(2)}) collective-permute-start(bf16[2,256,256]{2,1,0:T(8,128)(2,1)S(1)} %add_convert_fusion.1.rest_0_), channel_id=1, source_target_pairs={{0,2},{2,0},{4,6},{6,4},{1,3},{3,1},{5,7},{7,5},{8,10},{10,8},{12,... | collective-permute-start | bytes 786440 | tf_op jit(solution)/shard_map/ppermute | solution.py:19
  219.6 26.0 %collective-permute-start.47 = (bf16[2,256,256]{2,1,0:T(8,128)(2,1)S(1)}, bf16[2,256,256]{2,1,0:T(8,128)(2,1)S(1)}, u32[]{:S(2)}, u32[]{:S(2)}) collective-permute-start(bf16[2,256,256]{2,1,0:T(8,128)(2,1)S(1)} %add_convert_fusion.1.rest_0_), channel_id=1, source_target_pairs={{0,4},{2,6},{4,0},{6,2},{1,5},{3,7},{5,1},{7,3},{8,12},{10,14},{12... | collective-permute-start | bytes 786440 | tf_op jit(solution)/shard_map/ppermute | solution.py:19
  220.5 25.0 %collective-permute-start.48 = (bf16[2,256,256]{2,1,0:T(8,128)(2,1)S(1)}, bf16[2,256,256]{2,1,0:T(8,128)(2,1)S(1)}, u32[]{:S(2)}, u32[]{:S(2)}) collective-permute-start(bf16[2,256,256]{2,1,0:T(8,128)(2,1)S(1)} %add_convert_fusion.1.rest_0_), channel_id=1, source_target_pairs={{0,6},{2,4},{4,2},{6,0},{1,7},{3,5},{5,3},{7,1},{8,14},{10,12},{12... | collective-permute-start | bytes 786440 | tf_op jit(solution)/shard_map/ppermute | solution.py:19
  222.4 12.7 %collective-permute-start.61 = (bf16[1,128,256]{2,1,0:T(8,128)(2,1)S(1)}, bf16[1,128,256]{2,1,0:T(8,128)(2,1)}, u32[]{:S(2)}, u32[]{:S(2)}) collective-permute-start(bf16[1,128,256]{2,1,0:T(8,128)(2,1)S(1)} %collective-permute-done.58.rest_8_), channel_id=1, source_target_pairs={{0,6},{2,4},{4,2},{6,0},{1,7},{3,5},{5,3},{7,1},{8,14},{10,12},{12... | collective-permute-start | bytes 196616 | tf_op jit(solution)/shard_map/ppermute | solution.py:19
  235.0 7.7 %collective-permute-start.56 = (bf16[1,384,256]{2,1,0:T(8,128)(2,1)S(1)}, bf16[1,384,256]{2,1,0:T(8,128)(2,1)S(1)}, u32[]{:S(2)}, u32[]{:S(2)}) collective-permute-start(bf16[1,384,256]{2,1,0:T(8,128)(2,1)S(1)} %add_convert_fusion.2.rest_4_), channel_id=1, source_target_pairs={{0,4},{2,6},{4,0},{6,2},{1,5},{3,7},{5,1},{7,3},{8,12},{10,14},{12... | collective-permute-start | bytes 589832 | tf_op jit(solution)/shard_map/ppermute | solution.py:19
  236.0 9.6 %collective-permute-start.57 = (bf16[1,384,256]{2,1,0:T(8,128)(2,1)S(1)}, bf16[1,384,256]{2,1,0:T(8,128)(2,1)S(1)}, u32[]{:S(2)}, u32[]{:S(2)}) collective-permute-start(bf16[1,384,256]{2,1,0:T(8,128)(2,1)S(1)} %add_convert_fusion.2.rest_4_), channel_id=1, source_target_pairs={{0,6},{2,4},{4,2},{6,0},{1,7},{3,5},{5,3},{7,1},{8,14},{10,12},{12... | collective-permute-start | bytes 589832 | tf_op jit(solution)/shard_map/ppermute | solution.py:19
  (31 other events, 509.8 us)

commit v2 on v1

--- a/solution.py
+++ b/solution.py
@@ -30,22 +30,43 @@
     return [pieces[k] for k in range(len(pieces))]
 
 
-def after(value, *earlier):
-    return lax.optimization_barrier((value, *earlier))[0]
-
-
-def launch(body, outs, place, *args, scratch=(), mib=40, flops=0):
-    moved = sum(a.size * a.dtype.itemsize for a in args)
+def across_tp(far):
+    pairs = {k: [v, swap(v, "tp", 1)] for k, v in far.items()}
+    pairs.update({k ^ 1: [swap(h, "ctx", 1) for h in v] for k, v in list(pairs.items())})
+    return [h for k in range(2, len(pairs) + 2) for h in pairs[k]]
+
+
+def far_halves(half):
+    far = {0: half}
+    for bit in reversed(bits_of("ctx")[1:]):
+        far.update({k ^ bit: swap(v, "ctx", bit) for k, v in list(far.items())})
+    return {k: v for k, v in far.items() if k}
+
+
+def launch(body, outs, place, *args, scratch=(), mib=24, deps=(), hbm=(), far=()):
+    count = len(args)
+
+    def run(place_ref, *refs):
+        body(place_ref, *refs[:count], *refs[count + len(deps) :])
+
     return pl.pallas_call(
-        body,
+        run,
         out_shape=[jax.ShapeDtypeStruct(s, d) for s, d in outs],
         in_specs=[pl.BlockSpec(memory_space=pltpu.SMEM)]
-        + [pl.BlockSpec(memory_space=pltpu.VMEM)] * len(args),
-        out_specs=[pl.BlockSpec(memory_space=pltpu.VMEM)] * len(outs),
-        scratch_shapes=[pltpu.VMEM(s, d) for s, d in scratch],
+        + [
+            pl.BlockSpec(memory_space=pltpu.HBM if i in hbm else pltpu.VMEM) for i in range(count)
+        ]
+        + [pl.BlockSpec(memory_space=pl.ANY)] * len(deps),
+        out_specs=[
+            pl.BlockSpec(memory_space=pltpu.HBM if i in far else pltpu.VMEM)
+            for i in range(len(outs))
+        ],
+        scratch_shapes=[
+            pltpu.SemaphoreType.DMA(s) if d is None else pltpu.VMEM(s, d) for s, d in scratch
+        ],
         compiler_params=pltpu.CompilerParams(vmem_limit_bytes=mib << 20),
-        cost_estimate=pl.CostEstimate(flops=flops, bytes_accessed=moved, transcendentals=0),
-    )(place, *args)
+        cost_estimate=pl.CostEstimate(flops=1, bytes_accessed=1, transcendentals=0),
+    )(place, *args, *deps)
 
 
 def aligned(start, count):
@@ -99,19 +120,39 @@
     return jnp.sum(jnp.where(head_of_unit(units, size), row[0:1], 0.0), axis=1, keepdims=True)
 
 
-def pack_body(place, rows, xp, bcp, dtp, gp, op, first, gate_q, out_q, halo, dt_wide):
-    part, inner = gate_q.shape
-    here = aligned(place[1] * part, part)
-    heads = dtp.shape[1]
-    blank = jnp.zeros((dtp.shape[0], LANES - heads), LOW)
-    dt_wide[...] = jnp.concatenate([dtp[...], blank], axis=1)
-    states = bcp.shape[1]
-    first[:, :inner] = xp[here, :]
-    first[:, inner : inner + states] = bcp[here, :]
-    first[:, inner + states :] = dt_wide[here, :]
-    gate_q[...] = gp[here, :]
-    out_q[...] = op[aligned(place[1] * out_q.shape[0], out_q.shape[0]), :]
-    halo[...] = rows[rows.shape[0] - HALO :, :]
+def pack_body(place, rows, cot, xp, bcp, dtp, gp, op, packed, edge, dt_wide, halves, sems):
+    n = packed.shape[0]
+    here = aligned(place[1] * n, n)
+    inner, both = xp.shape[1], xp.shape[1] + bcp.shape[1]
+    wide = both + LANES
+    span = op.shape[1]
+    blocks = inner // span
+    base = place[1] * n * blocks
+    half = aligned(place[2] * halves.shape[1], halves.shape[1])
+    moves = [
+        (rows.at[rows.shape[0] - HALO :], edge),
+        (xp.at[here], packed.at[:, :inner]),
+        (bcp.at[here], packed.at[:, inner:both]),
+        (gp.at[here], packed.at[:, wide : wide + inner]),
+        (rows.at[half], halves.at[0]),
+        (cot.at[half], halves.at[1]),
+    ]
+    for i in range(blocks):
+        put = wide + inner + i * span
+        moves.append((op.at[aligned(base + i * n, n)], packed.at[:, put : put + span]))
+    copies = [pltpu.make_async_copy(a, b, sems.at[i]) for i, (a, b) in enumerate(moves)]
+    for copy in copies:
+        copy.start()
+    turned = dtp[...].astype(F32).T
+    blank = jnp.zeros((turned.shape[0], LANES - turned.shape[1]), F32)
+    dt_wide[...] = jnp.concatenate([turned, blank], axis=1).astype(LOW)
+    packed[:, both:wide] = dt_wide[here, :]
+    for copy in copies:
+        copy.wait()
+
+
+def copy_body(place, source, out):
+    out[...] = source[...]
 
 
 def norm_rows(v, gain):
@@ -119,17 +160,46 @@
     return v * lax.rsqrt(jnp.mean(v * v, axis=-1, keepdims=True) + EPSILON) * gain
 
 
-def norm_body(place, rows, halo, gain, normed):
-    normed[:HALO] = norm_rows(halo[...], gain[...]).astype(LOW)
+def lay_sequence(place, own, near, halves, which, out):
+    length = own.shape[0]
+    half = length // 2
+    for k, piece in enumerate((own, near)):
+        out[aligned((place[1] ^ k) * length, length), :] = piece[...]
+    for i, piece in enumerate(halves):
+        k, side = 2 + i // 2, i % 2
+        at = (place[1] ^ k) * length + (place[2] ^ side) * half
+        out[aligned(at, half), :] = piece[which]
+
+
+def norm_body(place, rows, edge, gain, normed):
+    normed[:HALO] = norm_rows(edge[...], gain[...]).astype(LOW)
     for at in range(0, rows.shape[0], 64):
         normed[HALO + at : HALO + at + 64] = norm_rows(rows[at : at + 64], gain[...]).astype(LOW)
 
 
+def sequence_body(place, gain, rows, near_rows, cot, near_cot, *rest):
+    *halves, normed_seq, cot_seq, raw = rest
+    normed_seq[:HALO] = jnp.zeros((HALO, raw.shape[1]), LOW)
+    lay_sequence(place, rows, near_rows, halves, 0, raw)
+    lay_sequence(place, cot, near_cot, halves, 1, cot_seq)
+
+    @pl.loop(0, raw.shape[0] // 64)
+    def _(i):
+        at = pl.ds(pl.multiple_of(i * 64, 64), 64)
+        put = pl.ds(pl.multiple_of(HALO + i * 64, HALO), 64)
+        normed_seq[put, :] = norm_rows(raw[at, :], gain[...]).astype(LOW)
+
+
+def padded(row):
+    return jnp.concatenate([row, jnp.zeros((1, LANES - row.shape[1]), F32)], axis=1)
+
+
 def front_body(fsdp, ctx, taps, heads, size):
     def body(place, normed, xp, bcp, dtp, *rest):
-        parts = rest[:ctx]
-        x_conv, bc_conv, dt_bias, a_log = rest[ctx : ctx + 4]
-        w_all, proj, conv_out, act, within, state, scalars, w_x = rest[ctx + 4 :]
+        count = ctx * (fsdp - 1)
+        parts = rest[:count]
+        x_conv, bc_conv, dt_bias, a_log = rest[count : count + 4]
+        w_all, proj, conv_out, act, within, state, scalars, decay, w_x = rest[count + 4 :]
         z, c = place[0], place[1]
         shard, inner = xp.shape
         both = inner + bcp.shape[1]
@@ -141,7 +211,8 @@
         n = shard // ctx
         for j in range(ctx):
             for k in range(1, fsdp):
-                w_all[aligned((z ^ k) * shard + (c ^ j) * n, n), :] = parts[j][k - 1]
+                put = aligned((z ^ k) * shard + (c ^ j) * n, n)
+                w_all[put, :] = parts[j * (fsdp - 1) + k - 1][:, : w_all.shape[1]]
         proj[...] = jnp.dot(normed[...], w_all[...], preferred_element_type=F32)
         length = conv_out.shape[0]
         start = HALO - taps + 1
@@ -156,15 +227,17 @@
                 total = total + tap[k : k + 1] * proj[start + k : start + k + length, cols]
             conv_out[:, cols] = total
             act[:, cols] = total * sigmoid(total)
-        pre = proj[HALO:, both:] + dt_bias[...]
+        pre = proj[HALO:, both:] + padded(dt_bias[...])
         step = jnp.maximum(pre, 0.0) + jnp.log1p(jnp.exp(-jnp.abs(pre)))
-        log_decay = -jnp.exp(a_log[...]) * step
+        log_decay = -jnp.exp(padded(a_log[...])) * step
         lower = iota((length, length), 0) >= iota((length, length), 1)
         cum = fine(jnp.where(lower, 1.0, 0.0), log_decay)
         cum_t = cum.T
         scalars[0] = step
         scalars[1] = cum
-        scalars[2] = jnp.exp(cum)
+        grow = jnp.exp(cum)
+        scalars[2] = grow
+        decay[...] = jnp.broadcast_to(grow[length - 1 :], decay.shape)
         tail = jnp.exp(cum[length - 1 :] - cum)
         scalars[3] = tail
         b_low = act[:, inner : inner + half_bc].astype(LOW)
@@ -223,7 +296,7 @@
     return body
 
 
-def run_scan(place, state, decay, reverse, size):
+def run_scan(place, state, decay, reverse, size, deps=()):
     bits = bits_of("ctx")
     kept = ()
     for bit in bits[:-1]:
@@ -238,7 +311,8 @@
             decay,
             other_decay,
             *kept,
-            mib=16,
+            mib=8,
+            deps=deps,
         )
     return swap(state, "ctx", bits[-1]), kept[0], kept[1]
 
@@ -251,18 +325,24 @@
 
 def gate_body(fsdp, ctx):
     def body(place, normed, cot, gp, op, *rest):
-        g_parts, o_parts = rest[:ctx], rest[ctx : 2 * ctx]
-        gate_in, d_normed_out, w_gate, w_out = rest[2 * ctx :]
+        parts = rest[: ctx * (fsdp - 1)]
+        gate_in, d_normed_out, w_gate, w_out = rest[ctx * (fsdp - 1) :]
         z, c = place[0], place[1]
         shard = gp.shape[0]
+        span, inner = op.shape[1], gp.shape[1]
         w_gate[aligned(z * shard, shard), :] = gp[...]
-        span = op.shape[1]
         w_out[:, aligned(z * span, span)] = op[...]
         n, m = shard // ctx, op.shape[0] // ctx
+        wide = parts[0].shape[1] - inner - span * (m // n)
         for j in range(ctx):
             for k in range(1, fsdp):
-                w_gate[aligned((z ^ k) * shard + (c ^ j) * n, n), :] = g_parts[j][k - 1]
-                w_out[aligned((c ^ j) * m, m), aligned((z ^ k) * span, span)] = o_parts[j][k - 1]
+                part = parts[j * (fsdp - 1) + k - 1]
+                w_gate[aligned((z ^ k) * shard + (c ^ j) * n, n), :] = part[:, wide : wide + inner]
+                for i in range(m // n):
+                    put = wide + inner + i * span
+                    w_out[aligned((c ^ j) * m + i * n, n), aligned((z ^ k) * span, span)] = part[
+                        :, put : put + span
+                    ]
         gate_in[...] = jnp.dot(normed[HALO:], w_gate[...], preferred_element_type=F32)
         d_normed_out[...] = mm(cot[...], w_out[...], NT).astype(LOW)
 
@@ -288,7 +368,7 @@
             carried = mm(c_low, state_in[cols, :], NT)
             flow = within[:, cols] + pair_wide(grow, i, per) * carried
             swept[:, cols] = flow
-            mixed = flow + skip[:, cols] * act[:, cols]
+            mixed = flow + pair_wide(skip[...], i, per) * act[:, cols]
             gate = gate_in[:, cols]
             gated = mixed * gate * sigmoid(gate)
             squares = squares + gated * gated
@@ -304,10 +384,10 @@
     return body
 
 
-def turn_body(size, full_inner):
+def turn_body(size, full_inner, ctx):
     def body(
         place, mine, theirs, act, swept, scalars, gate_in, d_no, skip, gain,
-        normed_out, d_gate, d_mixed, d_scaled, state_grad, rows_out,
+        normed_out, d_gate, d_mixed, d_scaled, state_grad, rows_out, *rest,
     ):
         length, inner = swept.shape
         half_bc = (act.shape[1] - inner) // 2
@@ -320,7 +400,7 @@
         for i in range(inner // LANES):
             cols = slice(LANES * i, LANES * i + LANES)
             x_act = act[:, cols]
-            mixed = swept[:, cols] + skip[:, cols] * x_act
+            mixed = swept[:, cols] + pair_wide(skip[...], i, per) * x_act
             gate = gate_in[:, cols]
             s = sigmoid(gate)
             gated = mixed * gate * s
@@ -336,14 +416,8 @@
             d_scaled[:, cols] = (dm * pair_wide(grow, i, per)).astype(LOW)
         c_low = act[:, inner + half_bc :].astype(LOW)
         state_grad[...] = mm(d_scaled[...], c_low, TN).astype(LOW)
-
-    return body
-
-
-def deal_body(ctx):
-    def body(place, d_gate, normed_out, *rest):
-        sends, stage = rest[:ctx], rest[ctx]
-        w = sends[0].shape[2]
+        *sends, stage = rest
+        w = inner // ctx
         for q in range(ctx):
             stage[q, 0] = d_gate[:, q * w : q * w + w]
             stage[q, 1] = normed_out[:, q * w : q * w + w]
@@ -430,7 +504,7 @@
             sweeps[:, cols] = grad * swept[:, cols]
             v = conv_out[:, cols]
             spaced[HALO : HALO + length, cols] = (
-                wide_step * whole + skip[:, cols] * grad
+                wide_step * whole + pair_wide(skip[...], i, per) * grad
             ) * silu_slope(v, sigmoid(v))
         pair = pair_t[...]
         d_b = mm(pair, c_low) + mm(tails[...], later)
@@ -470,8 +544,8 @@
         ends = tail_row + jnp.exp(cum[length - 1 :]) * decay_grad
         upper = jnp.where(iota((length, length), 0) <= iota((length, length), 1), 1.0, 0.0)
         d_log = fine(upper, row_sum - step * d_step) + ends
-        rates = jnp.exp(a_log[...])
-        pre = proj[HALO:, both:] + dt_bias[...]
+        rates = jnp.exp(padded(a_log[...]))
+        pre = proj[HALO:, both:] + padded(dt_bias[...])
         d_pre = (d_step - rates * d_log) * sigmoid(pre)
         d_pre = jnp.where(iota(d_pre.shape, 1) < heads, d_pre, 0.0)
         d_first[:HALO, both:] = jnp.zeros((HALO, LANES), LOW)
@@ -517,48 +591,127 @@
 
 def weights_body(fsdp, ctx, stacked):
     def body(place, *rest):
-        pieces, normeds = rest[:ctx], rest[ctx : 2 * ctx]
-        rest = rest[2 * ctx :]
-        cots = rest[: ctx if stacked else 0]
-        own, *sends, part = rest[len(cots) :]
+        pieces = rest[:ctx]
+        normed_seq = rest[ctx]
+        other = rest[ctx + 1] if stacked else None
+        keep, send, part = rest[ctx + 2 if stacked else ctx + 1 :]
+        length = pieces[0].shape[1] if stacked else pieces[0].shape[0] - HALO
         for j in range(2 if stacked else 1):
             total = None
             for k in range(ctx):
-                if stacked:
-                    big = cots[k][...] if j else normeds[k][HALO:]
+                start = (place[1] ^ k) * length
+                if not stacked:
+                    big = normed_seq[pl.ds(pl.multiple_of(start, HALO), HALO + length), :]
+                    term = mm(pieces[k][...], big, TN)
+                else:
+                    if j:
+                        big = other[pl.ds(pl.multiple_of(start, HALO), length), :]
+                    else:
+                        big = normed_seq[pl.ds(pl.multiple_of(start + HALO, HALO), length), :]
                     term = mm(pieces[k][j], big, TN)
-                else:
-                    term = mm(pieces[k][...], normeds[k][...], TN)
                 total = term if total is None else total + term
             part[j] = total
-        span = own.shape[2]
-        own[...] = part[:, :, aligned(place[0] * span, span)]
-        for k in range(1, fsdp):
-            sends[k - 1][...] = part[:, :, aligned((place[0] ^ k) * span, span)].astype(LOW)
+        span = keep.shape[3]
+        for k in range(fsdp):
+            block = part[:, :, aligned((place[0] ^ k) * span, span)]
+            if k % 2:
+                send[k // 2] = block.astype(LOW)
+            else:
+                keep[k // 2] = block
 
     return body
 
 
-def close_body(ctx, inner, states, heads):
+def add_body(place, mine, theirs, keep, send):
+    for k in range(mine.shape[0]):
+        total = mine[k] + theirs[k].astype(F32)
+        if k % 2:
+            send[k // 2] = total.astype(LOW)
+        else:
+            keep[k // 2] = total
+
+
+def last_add_body(place, mine, theirs, *outs):
+    total = mine[0] + theirs[0].astype(F32)
+    at = 0
+    for out in outs:
+        out[...] = total[:, at : at + out.shape[1]].astype(LOW)
+        at += out.shape[1]
+
+
+def join_body(states):
+    def body(place, mine, theirs, out):
+        r = mine.shape[1]
+        row = iota(mine.shape, 1) + place[1] * r
+        total = mine[...].astype(F32) + jnp.where(row < states, theirs[...].astype(F32), 0.0)
+        out[...] = total.astype(LOW)
+
+    return body
+
+
+def with_tally(body, count, shared=False):
+    def run(place, mine, theirs, *rest):
+        tally_body(shared)(place, mine, theirs, rest[count])
+        body(place, *rest[:count], *rest[count + 1 :])
+
+    return run
+
+
+def tally_body(shared):
+    def body(place, mine, theirs, out):
+        if shared:
+            row = iota(mine.shape, 0) < 2
+            out[...] = mine[...] + jnp.where(row, theirs[...], 0.0)
+        else:
+            out[...] = mine[...] + theirs[...]
+
+    return body
+
+
+def small_body(place, mine, theirs, gain, bc_taps, x_taps, gated, bias, decay, skip):
+    total = mine[...] + theirs[...]
+    gain[...] = total[0:1]
+    taps, states = bc_taps.shape
+    for k in range(taps):
+        bc_taps[k : k + 1] = total[1:2, k * states : k * states + states]
+    x_taps[...] = total[2 : 2 + taps]
+    gated[...] = total[6:7]
+    for i, out in enumerate((bias, decay, skip)):
+        out[...] = total[7:8, i * LANES : i * LANES + out.shape[1]]
+
+
+def output_body(place, half_out, branch, out):
+    out[...] = (half_out[...] + branch[...].astype(F32)).astype(LOW)
+
+
+def close_pair_body(ctx):
     def body(place, *rest):
-        pairs, firsts, peers = rest[:ctx], rest[ctx : 2 * ctx], rest[2 * ctx : 3 * ctx]
-        grad_gate, grad_out, grad_x, grad_bc, grad_dt, g_stage, x_stage, r_stage = rest[3 * ctx :]
-        c = place[1]
+        pairs = rest[:ctx]
+        grad_gate, grad_out, stage = rest[ctx:]
         w = pairs[0].shape[1]
-        r = peers[0].shape[1]
         for k in range(ctx):
-            q = c ^ k
-            g_stage[q] = pairs[k][0].astype(F32)
+            q = place[1] ^ k
+            stage[q] = pairs[k][0].astype(F32)
             grad_out[aligned(q * w, w), :] = pairs[k][1].astype(F32)
-            x_stage[q] = firsts[k][0, :w].astype(F32)
-            mine = firsts[k][0, w:].astype(F32)
-            r_stage[0, aligned(q * r, r), :] = mine
-            r_stage[1, aligned(q * r, r), :] = mine + peers[k][0].astype(F32)
         for q in range(ctx):
-            grad_gate[:, q * w : q * w + w] = g_stage[q].T
+            grad_gate[:, q * w : q * w + w] = stage[q].T
+
+    return body
+
+
+def close_body(ctx, states, heads):
+    def body(place, *rest):
+        firsts, lasts = rest[:ctx], rest[ctx : 2 * ctx]
+        grad_x, grad_bc, grad_dt, x_stage, r_stage = rest[2 * ctx :]
+        r, w = lasts[0].shape[1], firsts[0].shape[1]
+        for k in range(ctx):
+            q = place[1] ^ k
+            x_stage[q] = firsts[k][0].astype(F32)
+            r_stage[aligned(q * r, r), :] = lasts[k][0].astype(F32)
+        for q in range(ctx):
             grad_x[:, q * w : q * w + w] = x_stage[q].T
-        grad_bc[...] = r_stage[1, :states].T
-        grad_dt[...] = r_stage[0, states : states + LANES].T[:, :heads]
+        grad_bc[...] = r_stage[:states].T
+        grad_dt[...] = r_stage[states : states + heads]
 
     return body
 
@@ -612,47 +765,60 @@
     ext = HALO + length
     last_bit = bits_of("ctx")[-1]
 
-    first_q, gate_q, out_q, edge_rows, dt_wide = launch(
+    gain = input_gain[None]
+    wide = both + LANES
+    packed, edge_rows, dt_wide, halves = launch(
         pack_body,
         [
-            ((shard // ctx, both + LANES), LOW),
-            ((shard // ctx, inner), LOW),
-            ((inner // ctx, out_proj.shape[1]), LOW),
+            ((shard // ctx, wide + 2 * inner), LOW),
             ((HALO, width), LOW),
             ((shard, LANES), LOW),
+            ((2, length // 2, width), LOW),
         ],
         place,
         rows,
+        cot,
         x_proj,
         bc_proj,
-        dt_proj,
+        dt_proj.T,
         gate_proj,
         out_proj,
-        mib=16,
-    )
+        scratch=[((6 + inner // out_proj.shape[1],), None)],
+        mib=58,
+        hbm=(0, 1, 2, 3, 5, 6),
+    )
+    halves_far = far_halves(halves)
     halo = lax.ppermute(edge_rows, "ctx", [(i, i + 1) for i in range(ctx - 1)])
-    gain = input_gain[None]
-    [normed] = launch(norm_body, [((ext, width), LOW)], place, rows, halo, gain, mib=16)
-
-    def across(block):
-        return [swap(block, "fsdp", k) for k in range(1, fsdp)]
-
-    first_far = jnp.stack(across(first_q))
-    first_parts = spread(first_far, "ctx")
-    gate_q, out_q = after((gate_q, out_q), first_far)
-    gate_far, out_far = jnp.stack(across(gate_q)), jnp.stack(across(out_q))
-    gate_far, out_far = after((gate_far, out_far), first_parts[1])
-    gate_parts, out_parts = spread(gate_far, "ctx"), spread(out_far, "ctx")
-    late = after((normed, cot), gate_parts[-1])
-    normed_all = [normed] + spread(late[0], "ctx")[1:]
-    cot_all = [cot] + spread(late[1], "ctx")[1:]
-
-    pad_heads = ((0, 0), (0, LANES - heads))
-    bias_row = jnp.pad(dt_bias[None], pad_heads)
-    a_row = jnp.pad(a_log[None], pad_heads)
-    skip_row = jnp.repeat(skip_gain, size)[None]
-    gained = gated_gain[None]
-    w_first, proj, conv_out, act, within, state, scalars = launch(
+    [normed] = launch(norm_body, [((ext, width), LOW)], place, rows, halo, gain, mib=8)
+    near = swap(packed, "fsdp", 1)
+    [near] = launch(
+        copy_body,
+        [(packed.shape, LOW)],
+        place,
+        near,
+        mib=4,
+        deps=[normed, *halves_far.values()],
+    )
+    near_y = swap(near, "ctx", bits_of("ctx")[-1])
+    found = {0: packed, 1: near}
+    for bit in reversed(bits_of("fsdp")[1:]):
+        for k in [k for k in found if k % 2 == 0]:
+            found[k ^ bit] = swap(found[k], "fsdp", bit)
+    for k in [k for k in found if k and k % 2 == 0]:
+        [on] = launch(copy_body, [(packed.shape, LOW)], place, found[k], mib=4, deps=[near_y])
+        found[k ^ 1] = swap(on, "fsdp", 1)
+    far = [found[k] for k in range(1, fsdp)]
+    by_distance = [spread(p, "ctx") for p in far]
+    parts = [by_distance[k][j] for j in range(ctx) for k in range(fsdp - 1)]
+    halves_all = across_tp(halves_far)
+
+    bias_row, a_row, skip_row, gained = (
+        dt_bias[None],
+        a_log[None],
+        skip_gain[None],
+        gated_gain[None],
+    )
+    w_first, proj, conv_out, act, within, state, scalars, decay = launch(
         front_body(fsdp, ctx, taps, heads, size),
         [
             ((width, both + LANES), LOW),
@@ -662,22 +828,21 @@
             ((length, inner), F32),
             ((inner, half_bc), LOW),
             ((4, length, LANES), F32),
+            ((8, LANES), F32),
         ],
         place,
         normed,
         x_proj,
         bc_proj,
         dt_wide,
-        *first_parts,
+        *parts,
         x_conv,
         bc_conv,
         bias_row,
         a_row,
         scratch=[((length, inner), LOW)],
-        flops=2 * ext * width * (both + LANES),
-    )
-    decay = scalars[2, length - 8 :][7:8] * jnp.ones((8, 1), F32)
-    other, kept, kept_decay = run_scan(place, state, decay, False, size)
+    )
+    other, kept, kept_decay = run_scan(place, state, decay, False, size, [halves_all[1]])
     gate_in, d_no, w_gate, w_out = launch(
         gate_body(fsdp, ctx),
         [
@@ -691,9 +856,20 @@
         cot,
         gate_proj,
         out_proj,
-        *gate_parts,
-        *out_parts,
-        flops=4 * length * width * inner,
+        *parts,
+    )
+    normed_seq, cot_seq = launch(
+        sequence_body,
+        [((HALO + ctx * length, width), LOW), ((ctx * length, width), LOW)],
+        place,
+        gain,
+        rows,
+        swap(rows, "ctx", 1),
+        cot,
+        swap(cot, "ctx", 1),
+        *halves_all,
+        scratch=[((ctx * length, width), LOW)],
+        mib=4 + 10 * ctx // 4,
     )
     state_in, swept, sums = launch(
         mix_body(last_bit, size),
@@ -709,11 +885,12 @@
         d_no,
         skip_row,
         gained,
-        flops=2 * length * inner * half_bc,
+        deps=[normed_seq],
     )
     others = swap(sums, "tp", 1)
-    normed_out, d_gate, d_mixed, d_scaled, state_grad, skip_rows = launch(
-        turn_body(size, full_inner),
+    w = inner // ctx
+    normed_out, d_gate, d_mixed, d_scaled, state_grad, skip_rows, *sends = launch(
+        turn_body(size, full_inner, ctx),
         [
             ((length, inner), LOW),
             ((length, inner), LOW),
@@ -721,7 +898,8 @@
             ((length, inner), LOW),
             ((inner, half_bc), LOW),
             ((8, inner), F32),
-        ],
+        ]
+        + [((2, length, w), LOW)] * ctx,
         place,
         sums,
         others,
@@ -732,20 +910,10 @@
         d_no,
         skip_row,
         gained,
-        flops=2 * length * inner * half_bc,
+        scratch=[((ctx, 2, length, w), LOW)],
     )
     other, kept, kept_decay = run_scan(place, state_grad, decay, True, size)
 
-    w = inner // ctx
-    sends = launch(
-        deal_body(ctx),
-        [((2, length, w), LOW)] * ctx,
-        place,
-        d_gate,
-        normed_out,
-        scratch=[((ctx, 2, length, w), LOW)],
-        mib=16,
-    )
     back, pair_t, half_out, branch = launch(
         local_body(heads, size),
         [
@@ -761,11 +929,36 @@
         rows,
         normed_out,
         w_out,
-        flops=2 * length * width * inner,
-    )
-    block_output = (half_out + swap(branch, "tp", 1).astype(F32)).astype(LOW)[None]
+    )
+    branch = swap(branch, "tp", 1)
     pieces = [sends[0]] + [swap(sends[k], "ctx", k) for k in range(1, ctx)]
 
+    def partial_sums(count, columns, *args, stacked, deps=()):
+        span = width // fsdp
+        block = (fsdp // 2, count, columns, span)
+        return launch(
+            weights_body(fsdp, ctx, stacked),
+            [(block, F32), (block, LOW)],
+            place,
+            *args,
+            scratch=[((count, columns, width), F32)],
+            mib=20,
+            deps=deps,
+        )
+
+    def halve(keep, received, deps=()):
+        block = (keep.shape[0] // 2, *keep.shape[1:])
+        return launch(
+            add_body, [(block, F32), (block, LOW)], place, keep, received, mib=10, deps=deps
+        )
+
+    pair_keep, pair_send = partial_sums(2, w, *pieces, normed_seq, cot_seq, stacked=True, deps=[other, back])
+    pair_send_first = pair_send
+    fsdp_bits = bits_of("fsdp")
+    received = swap(pair_send, "fsdp", 1)
+    for bit in fsdp_bits[1:]:
+        pair_keep, pair_send = halve(pair_keep, received)
+        received = swap(pair_send, "fsdp", bit)
     r = 4 * LANES // ctx
     d_first, small, *first_sends = launch(
         rear_body(last_bit, ctx, taps, heads, size),
@@ -797,7 +990,7 @@
             ((length, inner), F32),
             ((ctx, ext, w + r), LOW),
         ],
-        flops=2 * length * inner * half_bc * 4,
+        deps=[pair_send_first],
     )
     first_pieces = [first_sends[0]] + [swap(first_sends[k], "ctx", k) for k in range(1, ctx)]
     own_grad, send_grad, edge, tally = launch(
@@ -811,11 +1004,49 @@
         rows,
         halo,
         small,
-        flops=2 * ext * width * (both + LANES + inner),
+        deps=[pair_send, branch],
+    )
+
+    def add_tally(tally, axis, bit):
+        return launch(
+            tally_body(axis == "tp"),
+            [(tally.shape, F32)],
+            place,
+            tally,
+            swap(tally, axis, bit),
+            mib=2,
+        )[0]
+
+    high, fsdp_high = bits_of("ctx")[1:], bits_of("fsdp")[1:]
+    for hop in [("ctx", b) for b in high[:-1]] + [("fsdp", b) for b in fsdp_high[:-1]]:
+        tally = add_tally(tally, *hop)
+    [pair_own] = launch(
+        last_add_body, [((2, w, width // fsdp), LOW)], place, pair_keep, received, mib=10
+    )
+    tally, keep, send = launch(
+        with_tally(weights_body(fsdp, ctx, False), ctx + 1),
+        [
+            (tally.shape, F32),
+            ((fsdp // 2, 1, w + r, width // fsdp), F32),
+            ((fsdp // 2, 1, w + r, width // fsdp), LOW),
+        ],
+        place,
+        tally,
+        swap(tally, "ctx", 1),
+        *first_pieces,
+        normed_seq,
+        scratch=[((1, w + r, width), F32)],
+        mib=20,
     )
     back_one = [(i + 1, i) for i in range(ctx - 1)]
     edge_in = lax.ppermute(edge, "ctx", back_one)
     edge_peer = swap(edge_in, "tp", 1)
+    received = swap(send, "fsdp", 1)
+    tally = add_tally(tally, "ctx", high[-1])
+    tally_in = swap(tally, "tp", 1)
+    [block_output] = launch(
+        output_body, [((length, width), LOW)], place, half_out, branch, mib=8
+    )
     [input_grad] = launch(
         finish_body,
         [((length, width), F32)],
@@ -829,63 +1060,96 @@
         gain,
         mib=24,
     )
-
-    def reduce_parts(count, columns, *args, stacked):
-        span = width // fsdp
-        own, *outs = launch(
-            weights_body(fsdp, ctx, stacked),
-            [((count, columns, span), F32)] + [((count, columns, span), LOW)] * (fsdp - 1),
-            place,
-            *args,
-            scratch=[((count, columns, width), F32)],
-            flops=2 * count * columns * width * length * ctx,
-        )
-        for k in range(1, fsdp):
-            own = own + swap(outs[k - 1], "fsdp", k).astype(F32)
-        return own.astype(LOW)
-
-    pair_own = reduce_parts(2, w, *pieces, *normed_all, *cot_all, stacked=True)
+    block = (keep.shape[0] // 2, *keep.shape[1:])
+    tally, keep, send = launch(
+        with_tally(add_body, 2, True),
+        [(tally.shape, F32), (block, F32), (block, LOW)],
+        place,
+        tally,
+        tally_in,
+        keep,
+        received,
+        mib=10,
+        deps=[input_grad, block_output],
+    )
+    received = swap(send, "fsdp", fsdp_bits[1])
+    for bit in fsdp_bits[2:]:
+        keep, send = halve(keep, received)
+        received = swap(send, "fsdp", bit)
     pair_all = [pair_own] + [swap(pair_own, "ctx", k) for k in range(1, ctx)]
-    first_own = reduce_parts(1, w + r, *first_pieces, *normed_all, stacked=False)
-    first_all = [first_own] + [swap(first_own, "ctx", k) for k in range(1, ctx)]
-    peer_own = swap(first_own[:, w:], "tp", 1)
-    peer_all = [peer_own] + [swap(peer_own, "ctx", k) for k in range(1, ctx)]
-    grad_gate, grad_out, grad_x, grad_bc, grad_dt = launch(
-        close_body(ctx, inner, states, heads),
+    tally, first_own, last_own = launch(
+        with_tally(last_add_body, 2),
         [
-            ((shard, inner), F32),
-            ((inner, out_proj.shape[1]), F32),
-            ((shard, inner), F32),
-            ((shard, states), F32),
-            ((shard, heads), F32),
+            (tally.shape, F32),
+            ((1, w, width // fsdp), LOW),
+            ((1, r, width // fsdp), LOW),
         ],
         place,
+        tally,
+        swap(tally, "fsdp", 1),
+        keep,
+        received,
+        mib=10,
+    )
+    first_all = spread(first_own, "ctx")
+    [last_own] = launch(
+        join_body(states),
+        [(last_own.shape, LOW)],
+        place,
+        last_own,
+        swap(last_own, "tp", 1),
+        mib=2,
+        deps=[first_all[2]],
+    )
+    last_all = spread(last_own, "ctx")
+    grad_gate, grad_out = launch(
+        close_pair_body(ctx),
+        [((shard, inner), F32), ((inner, out_proj.shape[1]), F32)],
+        place,
         *pair_all,
+        scratch=[((ctx, w, shard), F32)],
+        mib=12,
+        deps=[last_all[2]],
+    )
+    smalls = launch(
+        small_body,
+        [
+            ((1, width), F32),
+            ((taps, states), F32),
+            ((taps, inner), F32),
+            ((1, inner), F32),
+            *[((1, heads), F32)] * 3,
+        ],
+        place,
+        tally,
+        swap(tally, "fsdp", fsdp_high[-1]),
+        mib=2,
+    )
+    grad_x, grad_bc, grad_dt = launch(
+        close_body(ctx, states, heads),
+        [((shard, inner), F32), ((shard, states), F32), ((heads, shard), F32)],
+        place,
         *first_all,
-        *peer_all,
-        scratch=[((ctx, w, shard), F32), ((ctx, w, shard), F32), ((2, r * ctx, shard), F32)],
-        mib=24,
-    )
-
-    shared = (jnp.arange(8) < 2)[:, None]
-    tally = tally + jnp.where(shared, swap(tally, "tp", 1), 0.0)
-    for axis in ("ctx", "fsdp"):
-        for bit in bits_of(axis):
-            tally = tally + swap(tally, axis, bit)
+        *last_all,
+        scratch=[((ctx, w, shard), F32), ((r * ctx, shard), F32)],
+        mib=12,
+    )
+
+    grad_gain, bc_taps, x_taps, grad_gated, grad_bias, grad_a, grad_skip = smalls
     return (
-        block_output,
+        block_output[None],
         input_grad[None],
-        tally[0],
+        grad_gain[0],
         grad_gate,
         grad_x,
         grad_bc,
-        grad_dt,
-        tally[2 : 2 + taps],
-        tally[1].reshape(taps, states),
-        tally[7, :heads],
-        tally[7, LANES : LANES + heads],
-        tally[7, 2 * LANES : 2 * LANES + heads],
-        tally[6],
+        grad_dt.T,
+        x_taps,
+        bc_taps,
+        grad_bias[0],
+        grad_a[0],
+        grad_skip[0],
+        grad_gated[0],
         grad_out,
     )
 

time: 250 us -> 183 us (0.73)
  starting transfers between devices: 83.5 us -> 48.5 us
  waiting for transfers between devices: 104 us -> 80.7 us
  local copies, waits for them, and re-layouts: 18.9 us -> 1.31 us
  Pallas kernels: 38.8 us -> 50.6 us
    ppermute x60 -> x52, starting transfers between devices: 80.6 us -> 46 us  [swap(): return lax.ppermute(block, axis, [(i, i ^ bits) for i in range(count)])]
    ppermute x60 -> x52, waiting for transfers between devices: 104 us -> 80.7 us  [swap(): return lax.ppermute(block, axis, [(i, i ^ bits) for i in range(count)])]
    unnamed x68 -> x34, local copies, waits for them, and re-layouts: 15.6 us -> 1.31 us
    pallas_call x16 -> x27, Pallas kernels: 38.8 us -> 50.6 us  [launch(): pl.pallas_call(run, out_shape=[jax.ShapeDtypeStruct(s, d) for s, d in out...]
  transfers between devices with their start and end apart: 62 -> 54, of which waited for: 25 -> 22; matrix products, arithmetic and copies ran while one was open for 2% -> 0% of each run, Pallas kernels for 12% -> 21%
where the time goes in v2:
time: 183 us
  waiting for transfers between devices  80.7 us (44%)
  Pallas kernels  50.6 us (28%)
  starting transfers between devices  48.5 us (27%)
    ppermute x52, waiting for transfers between devices, swap(): return lax.ppermute(block, axis, [(i, i ^ bits) for i in range(count)])  80.7 us
    pallas_call x27, Pallas kernels, launch(): pl.pallas_call(run, out_shape=[jax.ShapeDtypeStruct(s, d) for s, d in out...  50.6 us
    ppermute x52, starting transfers between devices, swap(): return lax.ppermute(block, axis, [(i, i ^ bits) for i in range(count)])  46 us
  transfers between devices with their start and end apart: 54, of which 22 were waited for; matrix products, arithmetic and copies ran while one was open for 0% of the time, Pallas kernels for 21%

profile of v2, /device:TPU:0, one launch (start us, length us, event | category | flops | bytes accessed | tf_op | source)
XLA Modules:
  0.0 182.8 jit_solution(10567553939805662036)
XLA Ops:
  1.3 3.0 %shard_map.245 = (bf16[64,3456]{1,0:T(8,128)(2,1)}, bf16[16,1024]{1,0:T(8,128)(2,1)}, bf16[256,128]{1,0:T(8,128)(2,1)}, bf16[2,128,1024]{2,1,0:T(8,128)(2,1)}) custom-call(s32[3]{0:T(128)} %pad_add_fusion.place_ref, bf16[256,1024]{1,0:T(8,128)(2,1)} %bitcast.19, bf16[256,1024]{1,0:T(8,128)(2,1)} %bitcast.26, bf16[256,1024]{1,0:T(8,128)(2,1)} %refs_1_.1, ...), custom_call_target="tpu_custom_call" | custom-call | flops 1 | bytes 1 | tf_op jit(solution)/shard_map/pallas_call | solution.py:52
  4.3 3.0 %collective-permute-start.2 = (bf16[2,128,1024]{2,1,0:T(8,128)(2,1)}, bf16[2,128,1024]{2,1,0:T(8,128)(2,1)S(1)}, u32[]{:S(2)}, u32[]{:S(2)}) collective-permute-start(bf16[2,128,1024]{2,1,0:T(8,128)(2,1)} %get-tuple-element.93), channel_id=1, source_target_pairs={{0,4},{2,6},{4,0},{6,2},{1,5},{3,7},{5,1},{7,3},{8,12},{10,14},{12... | collective-permute-start | bytes 1572872 | tf_op jit(solution)/shard_map/ppermute | solution.py:19
  7.4 1.6 collective-permute-start.1
  8.9 1.3 collective-permute-start
  10.2 2.7 %collective-permute-start.3 = (bf16[64,3456]{1,0:T(8,128)(2,1)}, bf16[64,3456]{1,0:T(8,128)(2,1)S(1)}, u32[]{:S(2)}, u32[]{:S(2)}) collective-permute-start(bf16[64,3456]{1,0:T(8,128)(2,1)} %get-tuple-element.92), channel_id=1, source_target_pairs={{0,16},{8,24},{16,0},{24,8},{1,17},{9,25},{17,1},{25,9},{2,18},{10... | collective-permute-start | bytes 1327112 | tf_op jit(solution)/shard_map/ppermute | solution.py:19
  13.0 0.8 shard_map.246.refs_1_.refs_0_
  13.7 11.8 %collective-permute-done.1.refs_0_ = bf16[64,3456]{1,0:T(8,128)(2,1)S(1)} collective-permute-done((bf16[64,3456]{1,0:T(8,128)(2,1)}, bf16[64,3456]{1,0:T(8,128)(2,1)S(1)}, u32[]{:S(2)}, u32[]{:S(2)}) %collective-permute-start.1) | collective-permute-done | bytes 442400 | tf_op jit(solution)/shard_map/ppermute | solution.py:19
  26.1 2.1 %collective-permute-start.4 = (bf16[64,3456]{1,0:T(8,128)(2,1)S(1)}, bf16[64,3456]{1,0:T(8,128)(2,1)S(1)}, u32[]{:S(2)}, u32[]{:S(2)}) collective-permute-start(bf16[64,3456]{1,0:T(8,128)(2,1)S(1)} %shard_map.247.refs_4_), channel_id=1, source_target_pairs={{0,4},{2,6},{4,0},{6,2},{1,5},{3,7},{5,1},{7,3},{8,12},{10,14},{12... | collective-permute-start | bytes 1327112 | tf_op jit(solution)/shard_map/ppermute | solution.py:19
  28.2 5.5 %collective-permute-done.3.refs_0_.refs_5_ = bf16[64,3456]{1,0:T(8,128)(2,1)S(1)} collective-permute-done((bf16[64,3456]{1,0:T(8,128)(2,1)}, bf16[64,3456]{1,0:T(8,128)(2,1)S(1)}, u32[]{:S(2)}, u32[]{:S(2)}) %collective-permute-start.3) | collective-permute-done | bytes 442400 | tf_op jit(solution)/shard_map/ppermute | solution.py:19
  33.7 3.8 %collective-permute-done.4.refs_1_.refs_10_ = bf16[64,3456]{1,0:T(8,128)(2,1)S(1)} collective-permute-done((bf16[64,3456]{1,0:T(8,128)(2,1)S(1)}, bf16[64,3456]{1,0:T(8,128)(2,1)S(1)}, u32[]{:S(2)}, u32[]{:S(2)}) %collective-permute-start.4) | collective-permute-done | bytes 442400 | tf_op jit(solution)/shard_map/ppermute | solution.py:19
  38.2 1.8 collective-permute-start.9
  40.5 8.1 %collective-permute-done.5.refs_6_ = bf16[64,3456]{1,0:T(8,128)(2,1)S(1)} collective-permute-done((bf16[64,3456]{1,0:T(8,128)(2,1)S(1)}, bf16[64,3456]{1,0:T(8,128)(2,1)S(1)}, u32[]{:S(2)}, u32[]{:S(2)}) %collective-permute-start.5) | collective-permute-done | bytes 442400 | tf_op jit(solution)/shard_map/ppermute | solution.py:19
  48.5 1.5 collective-permute-start.10
  50.0 1.0 collective-permute-start.16
  51.6 6.5 %collective-permute-done.10.refs_12_ = bf16[64,3456]{1,0:T(8,128)(2,1)S(1)} collective-permute-done((bf16[64,3456]{1,0:T(8,128)(2,1)S(1)}, bf16[64,3456]{1,0:T(8,128)(2,1)S(1)}, u32[]{:S(2)}, u32[]{:S(2)}) %collective-permute-start.10) | collective-permute-done | bytes 442400 | tf_op jit(solution)/shard_map/ppermute | solution.py:19
  58.1 1.8 collective-permute-done.13.refs_15_
  60.0 4.8 %shard_map.249 = (bf16[1024,1408]{1,0:T(8,128)(2,1)S(1)}, f32[272,1408]{1,0:T(8,128)S(1)}, f32[256,1280]{1,0:T(8,128)S(1)}, f32[256,1280]{1,0:T(8,128)S(1)}, f32...) custom-call(s32[3]{0:T(128)S(1)} %copy-done.8, ...), custom_call_target="tpu_custom_call" | custom-call | flops 1 | bytes 1 | tf_op jit(solution)/shard_map/pallas_call | solution.py:52
  66.4 2.4 %collective-permute-done.14.refs_1_ = bf16[1024,128]{1,0:T(8,128)(2,1)S(1)} collective-permute-done((bf16[1024,128]{1,0:T(8,128)(2,1)S(1)}, bf16[1024,128]{1,0:T(8,128)(2,1)S(1)}, u32[]{:S(2)}, u32[]{:S(2)}) %collective-permute-start.14) | collective-permute-done | bytes 262176 | tf_op jit(solution)/shard_map/ppermute | solution.py:19
  68.7 1.4 shard_map.250
  70.2 1.5 collective-permute-start.17
  71.7 3.0 %shard_map.252 = (bf16[1040,1024]{1,0:T(8,128)(2,1)S(1)}, bf16[1024,1024]{1,0:T(8,128)(2,1)S(1)}) custom-call(s32[3]{0:T(128)S(1)} %copy-done.8, f32[1,1024]{1,0:T(1,128)S(1)} %bitcast.34, bf16[256,1024]{1,0:T(8,128)(2,1)S(1)} %bitcast.22, bf16[256,1024]{1,0:T(8,128)(2,1)S(1)} %collective-permute-done.18.refs_2_, bf16[256,1024]{1,0:T(8,128)(2,1)S(1)} %bitcast.28, ...), custom_call_target="tpu_custom_call" | custom-call | flops 1 | bytes 1 | tf_op jit(solution)/shard_map/pallas_call | solution.py:52
  74.7 2.1 %shard_map.251 = (f32[256,1024]{1,0:T(8,128)S(1)}, bf16[256,1024]{1,0:T(8,128)(2,1)S(1)}, bf16[1024,1024]{1,0:T(8,128)(2,1)S(1)}, bf16[1024,1024]{1,0:T(8,128)(2,1)S(1)}) custom-call(s32[3]{0:T(128)S(1)} %copy-done.8, bf16[272,1024]{1,0:T(8,128)(2,1)S(1)} %shard_map.246.refs_1_.refs_0_, bf16[256,1024]{1,0:T(8,128)(2,1)S(1)} %bitcast.29, ...), custom_call_target="tpu_custom_call" | custom-call | flops 1 | bytes 1 | tf_op jit(solution)/shard_map/pallas_call | solution.py:52
  76.8 1.9 %collective-permute-done.17.refs_0_ = bf16[1024,128]{1,0:T(8,128)(2,1)S(1)} collective-permute-done((bf16[1024,128]{1,0:T(8,128)(2,1)S(1)}, bf16[1024,128]{1,0:T(8,128)(2,1)S(1)}, u32[]{:S(2)}, u32[]{:S(2)}) %collective-permute-start.17) | collective-permute-done | bytes 262176 | tf_op jit(solution)/shard_map/ppermute | solution.py:19
  78.8 2.0 %shard_map.253 = (bf16[1024,128]{1,0:T(8,128)(2,1)S(1)}, f32[256,1024]{1,0:T(8,128)S(1)}, f32[8,256]{1,0:T(8,128)S(1)}) custom-call(s32[3]{0:T(128)S(1)} %copy-done.8, bf16[1024,128]{1,0:T(8,128)(2,1)S(1)} %collective-permute-done.17.refs_0_, bf16[1024,128]{1,0:T(8,128)(2,1)S(1)} %get-tuple-element.97.refs_1_, f32[8,128]{1,0:T(8,128)S(1)} %get-tuple-element.98.refs_2_, ...), custom_call_target="tpu_custom_call" | custom-call | flops 1 | bytes 1 | tf_op jit(solution)/shard_map/pallas_call | solution.py:52
  80.7 1.0 collective-permute-start.22
  81.8 2.6 %collective-permute-done.22.refs_1_ = f32[8,256]{1,0:T(8,128)S(1)} collective-permute-done((f32[8,256]{1,0:T(8,128)S(1)}, f32[8,256]{1,0:T(8,128)S(1)}, u32[]{:S(2)}, u32[]{:S(2)}) %collective-permute-start.22) | collective-permute-done | bytes 8224 | tf_op jit(solution)/shard_map/ppermute | solution.py:19
  84.4 2.6 %shard_map.254 = (bf16[256,1024]{1,0:T(8,128)(2,1)S(1)}, bf16[256,1024]{1,0:T(8,128)(2,1)S(1)}, f32[256,1024]{1,0:T(8,128)S(1)}, bf16[256,1024]{1,0:T(8,128)(2,1...) custom-call(s32[3]{0:T(128)S(1)} %copy-done.8, ...), custom_call_target="tpu_custom_call" | custom-call | flops 1 | bytes 1 | tf_op jit(solution)/shard_map/pallas_call | solution.py:52
  87.6 1.5 collective-permute-start.27
  89.1 1.4 shard_map.257
  90.5 1.4 collective-permute-start.25
  92.0 3.0 %shard_map.255 = (f32[256,1024]{1,0:T(8,128)S(1)}, f32[256,256]{1,0:T(8,128)S(1)}, f32[256,1024]{1,0:T(8,128)S(1)}, bf16[256,1024]{1,0:T(8,128)(2,1)S(1)}) custom-call(s32[3]{0:T(128)S(1)} %copy-done.8, f32[256,1024]{1,0:T(8,128)S(1)} %get-tuple-element.107.refs_0_.refs_10_, f32[256,1280]{1,0:T(8,128)S(1)} %get-tuple-element.99.refs_3_.refs_2_.refs_1_.refs_5_, ...), custom_call_target="tpu_custom_call" | custom-call | flops 1 | bytes 1 | tf_op jit(solution)/shard_map/pallas_call | solution.py:52
  94.9 1.9 %collective-permute-done.27.refs_2_ = bf16[2,256,256]{2,1,0:T(8,128)(2,1)S(1)} collective-permute-done((bf16[2,256,256]{2,1,0:T(8,128)(2,1)S(1)}, bf16[2,256,256]{2,1,0:T(8,128)(2,1)S(1)}, u32[]{:S(2)}, u32[]{:S(2)}) %collective-permute-start.27) | collective-permute-done | bytes 262176 | tf_op jit(solution)/shard_map/ppermute | solution.py:19
  96.8 4.6 %collective-permute-done.28.refs_3_ = bf16[2,256,256]{2,1,0:T(8,128)(2,1)S(1)} collective-permute-done((bf16[2,256,256]{2,1,0:T(8,128)(2,1)S(1)}, bf16[2,256,256]{2,1,0:T(8,128)(2,1)S(1)}, u32[]{:S(2)}, u32[]{:S(2)}) %collective-permute-start.28) | collective-permute-done | bytes 262176 | tf_op jit(solution)/shard_map/ppermute | solution.py:19
  101.4 5.7 %collective-permute-done.25.refs_6_.refs_0_ = bf16[1024,128]{1,0:T(8,128)(2,1)S(1)} collective-permute-done((bf16[1024,128]{1,0:T(8,128)(2,1)S(1)}, bf16[1024,128]{1,0:T(8,128)(2,1)S(1)}, u32[]{:S(2)}, u32[]{:S(2)}) %collective-permute-start.25) | collective-permute-done | bytes 262176 | tf_op jit(solution)/shard_map/ppermute | solution.py:19
  107.2 2.0 %shard_map.258 = (f32[2,2,256,256]{3,2,1,0:T(8,128)S(1)}, bf16[2,2,256,256]{3,2,1,0:T(8,128)(2,1)S(1)}) custom-call(s32[3]{0:T(128)S(1)} %copy-done.8, bf16[2,256,256]{2,1,0:T(8,128)(2,1)S(1)} %get-tuple-element.123.refs_0_, bf16[2,256,256]{2,1,0:T(8,128)(2,1)S(1)} %collective-permute-done.26.refs_1_, ...), custom_call_target="tpu_custom_call" | custom-call | flops 1 | bytes 1 | tf_op jit(solution)/shard_map/pallas_call | solution.py:52
  109.1 1.7 collective-permute-start.29
  110.9 1.0 collective-permute-start.23
  111.9 6.2 %shard_map.259 = (bf16[272,1408]{1,0:T(8,128)(2,1)S(1)}, f32[8,1024]{1,0:T(8,128)S(1)}, bf16[272,384]{1,0:T(8,128)(2,1)S(1)}, bf16[272,384]{1,0:T(8,128)(2,1)S(1...) custom-call(s32[3]{0:T(128)S(1)} %copy-done.8, ...), custom_call_target="tpu_custom_call" | custom-call | flops 1 | bytes 1 | tf_op jit(solution)/shard_map/pallas_call | solution.py:52
  118.2 1.5 collective-permute-start.35
  120.0 2.2 %collective-permute-done.29.refs_1_ = bf16[2,2,256,256]{3,2,1,0:T(8,128)(2,1)S(1)} collective-permute-done((bf16[2,2,256,256]{3,2,1,0:T(8,128)(2,1)S(1)}, bf16[2,2,256,256]{3,2,1,0:T(8,128)(2,1)S(1)}, u32[]{:S(2)}, u32[]{:S(2)}) %collective-permute-start.29) | collective-permute-done | bytes 524320 | tf_op jit(solution)/shard_map/ppermute | solution.py:19
  123.7 2.2 %shard_map.261 = (f32[256,1024]{1,0:T(8,128)S(1)}, bf16[256,1024]{1,0:T(8,128)(2,1)S(1)}, bf16[16,1024]{1,0:T(8,128)(2,1)S(1)}, f32[8,1024]{1,0:T(8,128)S(1)}) custom-call(s32[3]{0:T(128)S(1)} %copy-done.8, bf16[272,1408]{1,0:T(8,128)(2,1)S(1)} %get-tuple-element.129.refs_0_, bf16[256,1024]{1,0:T(8,128)(2,1)S(1)} %get-tuple-element.130.refs_1_, ...), custom_call_target="tpu_custom_call" | custom-call | flops 1 | bytes 1 | tf_op jit(solution)/shard_map/pallas_call | solution.py:52
  125.9 1.1 collective-permute-start.30
  127.0 2.8 %collective-permute-done.36.refs_5_ = bf16[272,384]{1,0:T(8,128)(2,1)S(1)} collective-permute-done((bf16[272,384]{1,0:T(8,128)(2,1)S(1)}, bf16[272,384]{1,0:T(8,128)(2,1)S(1)}, u32[]{:S(2)}, u32[]{:S(2)}) %collective-permute-start.36) | collective-permute-done | bytes 208928 | tf_op jit(solution)/shard_map/ppermute | solution.py:19
  129.8 2.5 %shard_map.263 = (f32[8,1024]{1,0:T(8,128)S(1)}, f32[2,1,384,256]{3,2,1,0:T(8,128)S(1)}, bf16[2,1,384,256]{3,2,1,0:T(8,128)(2,1)S(1)}) custom-call(s32[3]{0:T(128)S(1)} %copy-done.8, f32[8,1024]{1,0:T(8,128)S(1)} %get-tuple-element.139.refs_0_, f32[8,1024]{1,0:T(8,128)S(1)} %collective-permute-done.33.refs_1_, ...), custom_call_target="tpu_custom_call" | custom-call | flops 1 | bytes 1 | tf_op jit(solution)/shard_map/pallas_call | solution.py:52
  132.7 2.7 %collective-permute-start.43 = (bf16[1,2,256,256]{3,2,1,0:T(8,128)(2,1)S(1)}, bf16[1,2,256,256]{3,2,1,0:T(8,128)(2,1)S(1)}, u32[]{:S(2)}, u32[]{:S(2)}) collective-permute-start(bf16[1,2,256,256]{3,2,1,0:T(8,128)(2,1)S(1)} %get-tuple-element.135.refs_7_), channel_id=1, source_target_pairs={{0,16},{8,24},{16,0},{24,8},{1,17},{9,25},{17,1},{25,9},{2,18},{10... | collective-permute-start | bytes 786440 | tf_op jit(solution)/shard_map/ppermute | solution.py:19
  135.3 1.3 collective-permute-start.31
  136.6 2.3 %collective-permute-start.37 = (f32[8,1024]{1,0:T(8,128)S(1)}, f32[8,1024]{1,0:T(8,128)S(1)}, u32[]{:S(2)}, u32[]{:S(2)}) collective-permute-start(f32[8,1024]{1,0:T(8,128)S(1)} %get-tuple-element.144.refs_0_), channel_id=1, source_target_pairs={{0,4},{2,6},{4,0},{6,2},{1,5},{3,7},{5,1},{7,3},{8,12},{10,14},{12... | collective-permute-start | bytes 98312 | tf_op jit(solution)/shard_map/ppermute | solution.py:19
  139.5 2.0 %collective-permute-done.37.refs_1_ = f32[8,1024]{1,0:T(8,128)S(1)} collective-permute-done((f32[8,1024]{1,0:T(8,128)S(1)}, f32[8,1024]{1,0:T(8,128)S(1)}, u32[]{:S(2)}, u32[]{:S(2)}) %collective-permute-start.37) | collective-permute-done | bytes 32800 | tf_op jit(solution)/shard_map/ppermute | solution.py:19
  142.6 1.4 shard_map.256.refs_5_
  144.1 2.0 %shard_map.262.refs_4_ = f32[256,1024]{1,0:T(8,128)} custom-call(s32[3]{0:T(128)S(1)} %copy-done.8, f32[256,1024]{1,0:T(8,128)S(1)} %get-tuple-element.136.refs_0_, bf16[256,1024]{1,0:T(8,128)(2,1)S(1)} %collective-permute-done.30.refs_1_, bf16[16,1024]{1,0:T(8,128)(2,1)S(1)} %collective-permute-done.31.refs_2_, ...), custom_call_target="tpu_custom_call" | custom-call | flops 1 | bytes 1 | tf_op jit(solution)/shard_map/pallas_call | solution.py:52
  146.1 3.4 %collective-permute-done.39.refs_3_ = bf16[2,1,384,256]{3,2,1,0:T(8,128)(2,1)S(1)} collective-permute-done((bf16[2,1,384,256]{3,2,1,0:T(8,128)(2,1)S(1)}, bf16[2,1,384,256]{3,2,1,0:T(8,128)(2,1)S(1)}, u32[]{:S(2)}, u32[]{:S(2)}) %collective-permute-start.39) | collective-permute-done | bytes 393248 | tf_op jit(solution)/shard_map/ppermute | solution.py:19
  149.5 1.2 copy-done.2
  152.7 1.5 collective-permute-start.45
  154.2 2.5 %collective-permute-start.40 = (f32[8,1024]{1,0:T(8,128)S(1)}, f32[8,1024]{1,0:T(8,128)S(1)}, u32[]{:S(2)}, u32[]{:S(2)}) collective-permute-start(f32[8,1024]{1,0:T(8,128)S(1)} %get-tuple-element.147.refs_0_), channel_id=1, source_target_pairs={{0,8},{8,0},{16,24},{24,16},{1,9},{9,1},{17,25},{25,17},{2,10},{10... | collective-permute-start | bytes 98312 | tf_op jit(solution)/shard_map/ppermute | solution.py:19
  156.7 1.8 %collective-permute-done.40.refs_1_ = f32[8,1024]{1,0:T(8,128)S(1)} collective-permute-done((f32[8,1024]{1,0:T(8,128)S(1)}, f32[8,1024]{1,0:T(8,128)S(1)}, u32[]{:S(2)}, u32[]{:S(2)}) %collective-permute-start.40) | collective-permute-done | bytes 32800 | tf_op jit(solution)/shard_map/ppermute | solution.py:19
  158.6 4.4 %collective-permute-done.41.refs_3_ = bf16[1,1,384,256]{3,2,1,0:T(8,128)(2,1)S(1)} collective-permute-done((bf16[1,1,384,256]{3,2,1,0:T(8,128)(2,1)S(1)}, bf16[1,1,384,256]{3,2,1,0:T(8,128)(2,1)S(1)}, u32[]{:S(2)}, u32[]{:S(2)}) %collective-permute-start.41) | collective-permute-done | bytes 196640 | tf_op jit(solution)/shard_map/ppermute | solution.py:19
  163.6 1.5 collective-permute-start.48
  165.6 3.7 %collective-permute-done.47.refs_1_ = bf16[1,128,256]{2,1,0:T(8,128)(2,1)S(1)} collective-permute-done((bf16[1,128,256]{2,1,0:T(8,128)(2,1)S(1)}, bf16[1,128,256]{2,1,0:T(8,128)(2,1)S(1)}, u32[]{:S(2)}, u32[]{:S(2)}) %collective-permute-start.47) | collective-permute-done | bytes 65568 | tf_op jit(solution)/shard_map/ppermute | solution.py:19
  170.4 1.5 collective-permute-start.49
  171.9 2.4 %collective-permute-start.42 = (f32[8,1024]{1,0:T(8,128)S(1)}, f32[8,1024]{1,0:T(8,128)S(1)}, u32[]{:S(2)}, u32[]{:S(2)}) collective-permute-start(f32[8,1024]{1,0:T(8,128)S(1)} %get-tuple-element.150.refs_0_), channel_id=1, source_target_pairs={{0,16},{8,24},{16,0},{24,8},{1,17},{9,25},{17,1},{25,9},{2,18},{10... | collective-permute-start | bytes 98312 | tf_op jit(solution)/shard_map/ppermute | solution.py:19
  174.4 2.4 %collective-permute-done.42.refs_1_ = f32[8,1024]{1,0:T(8,128)S(1)} collective-permute-done((f32[8,1024]{1,0:T(8,128)S(1)}, f32[8,1024]{1,0:T(8,128)S(1)}, u32[]{:S(2)}, u32[]{:S(2)}) %collective-permute-start.42) | collective-permute-done | bytes 32800 | tf_op jit(solution)/shard_map/ppermute | solution.py:19
  177.3 1.2 shard_map.267
  178.5 2.3 %shard_map.270 = (f32[256,1024]{1,0:T(8,128)}, f32[1024,256]{1,0:T(8,128)}) custom-call(s32[3]{0:T(128)S(1)} %copy-done.8, bf16[2,256,256]{2,1,0:T(8,128)(2,1)S(1)} %shard_map.268.refs_0_, bf16[2,256,256]{2,1,0:T(8,128)(2,1)S(1)} %collective-permute-done.44.refs_1_, bf16[2,256,256]{2,1,0:T(8,128)(2,1)S(1)} %collective-permute-done.45.refs_2_, ...), custom_call_target="tpu_custom_call" | custom-call | flops 1 | bytes 1 | tf_op jit(solution)/shard_map/pallas_call | solution.py:52
  180.8 2.0 %shard_map.271 = (f32[256,1024]{1,0:T(8,128)}, f32[256,256]{1,0:T(8,128)}, f32[16,256]{1,0:T(8,128)}) custom-call(s32[3]{0:T(128)S(1)} %copy-done.8, bf16[1,256,256]{2,1,0:T(8,128)(2,1)S(1)} %get-tuple-element.154.refs_0_, bf16[1,256,256]{2,1,0:T(8,128)(2,1)S(1)} %collective-permute-done.50.refs_1_, ...), custom_call_target="tpu_custom_call" | custom-call | flops 1 | bytes 1 | tf_op jit(solution)/shard_map/pallas_call | solution.py:52
  (106 shorter events, 13.7 us)
Async XLA Ops:
  0.6 12.2 %copy-start = (bf16[1,256,1024]{2,1,0:T(8,128)(2,1)S(1)}, bf16[1,256,1024]{2,1,0:T(8,128)(2,1)}, u32[]{:S(2)}) copy-start(bf16[1,256,1024]{2,1,0:T(8,128)(2,1)} %param.14) | copy-start | bytes 1572868
  0.7 12.2 %copy-start.11 = (f32[1024]{0:T(1024)S(1)}, f32[1024]{0:T(1024)}, u32[]{:S(2)}) copy-start(f32[1024]{0:T(1024)} %param.15) | copy-start | bytes 12292
  1.3 11.6 %copy-start.8 = (s32[3]{0:T(128)S(1)}, s32[3]{0:T(128)}, u32[]{:S(2)}) copy-start(s32[3]{0:T(128)} %pad_add_fusion.place_ref) | copy-start | bytes 40
  4.3 21.2 %collective-permute-start.2 = (bf16[2,128,1024]{2,1,0:T(8,128)(2,1)}, bf16[2,128,1024]{2,1,0:T(8,128)(2,1)S(1)}, u32[]{:S(2)}, u32[]{:S(2)}) collective-permute-start(bf16[2,128,1024]{2,1,0:T(8,128)(2,1)} %get-tuple-element.93), channel_id=1, source_target_pairs={{0,4},{2,6},{4,0},{6,2},{1,5},{3,7},{5,1},{7,3},{8,12},{10,14},{12... | collective-permute-start | bytes 1572872 | tf_op jit(solution)/shard_map/ppermute | solution.py:19
  7.4 18.2 %collective-permute-start.1 = (bf16[64,3456]{1,0:T(8,128)(2,1)}, bf16[64,3456]{1,0:T(8,128)(2,1)S(1)}, u32[]{:S(2)}, u32[]{:S(2)}) collective-permute-start(bf16[64,3456]{1,0:T(8,128)(2,1)} %get-tuple-element.92), channel_id=1, source_target_pairs={{0,8},{8,0},{16,24},{24,16},{1,9},{9,1},{17,25},{25,17},{2,10},{10... | collective-permute-start | bytes 1327112 | tf_op jit(solution)/shard_map/ppermute | solution.py:19
  8.9 3.9 %collective-permute-start = (bf16[16,1024]{1,0:T(8,128)(2,1)}, bf16[16,1024]{1,0:T(8,128)(2,1)S(1)}, u32[]{:S(2)}, u32[]{:S(2)}) collective-permute-start(bf16[16,1024]{1,0:T(8,128)(2,1)} %get-tuple-element.90), channel_id=1, source_target_pairs={{0,2},{2,4},{4,6},{1,3},{3,5},{5,7},{8,10},{10,12},{12,14},{9,11},... | collective-permute-start | bytes 98312 | tf_op jit(solution)/shard_map/ppermute | solution.py:791
  10.2 23.5 %collective-permute-start.3 = (bf16[64,3456]{1,0:T(8,128)(2,1)}, bf16[64,3456]{1,0:T(8,128)(2,1)S(1)}, u32[]{:S(2)}, u32[]{:S(2)}) collective-permute-start(bf16[64,3456]{1,0:T(8,128)(2,1)} %get-tuple-element.92), channel_id=1, source_target_pairs={{0,16},{8,24},{16,0},{24,8},{1,17},{9,25},{17,1},{25,9},{2,18},{10... | collective-permute-start | bytes 1327112 | tf_op jit(solution)/shard_map/ppermute | solution.py:19
  12.9 47.0 %copy-start.3 = (bf16[256,1024]{1,0:T(8,128)(2,1)S(1)}, bf16[256,1024]{1,0:T(8,128)(2,1)}, u32[]{:S(2)}) copy-start(bf16[256,1024]{1,0:T(8,128)(2,1)} %refs_1_.1) | copy-start | bytes 1572868
  12.9 47.0 %copy-start.7 = (bf16[256,256]{1,0:T(8,128)(2,1)S(1)}, bf16[256,256]{1,0:T(8,128)(2,1)}, u32[]{:S(2)}) copy-start(bf16[256,256]{1,0:T(8,128)(2,1)} %refs_2_.4) | copy-start | bytes 393220
  12.9 47.0 %copy-start.9 = (bf16[256,128]{1,0:T(8,128)(2,1)S(1)}, bf16[256,128]{1,0:T(8,128)(2,1)}, u32[]{:S(2)}) copy-start(bf16[256,128]{1,0:T(8,128)(2,1)} %get-tuple-element.91.refs_3_) | copy-start | bytes 196612
  12.9 47.0 %copy-start.10 = (f32[4,1024]{1,0:T(4,128)S(1)}, f32[4,1024]{1,0:T(4,128)}, u32[]{:S(2)}) copy-start(f32[4,1024]{1,0:T(4,128)} %refs_15_.1) | copy-start | bytes 49156
  12.9 47.0 %copy-start.12 = (f32[4,256]{1,0:T(4,128)S(1)}, f32[4,256]{1,0:T(4,128)}, u32[]{:S(2)}) copy-start(f32[4,256]{1,0:T(4,128)} %refs_16_.3) | copy-start | bytes 12292
  13.0 47.0 %copy-start.15 = (f32[16]{0:T(128)S(1)}, f32[16]{0:T(128)}, u32[]{:S(2)}) copy-start(f32[16]{0:T(128)} %param.22) | copy-start | bytes 196
  13.0 47.0 %copy-start.16 = (f32[16]{0:T(128)S(1)}, f32[16]{0:T(128)}, u32[]{:S(2)}) copy-start(f32[16]{0:T(128)} %param.23) | copy-start | bytes 196
  26.1 11.4 %collective-permute-start.4 = (bf16[64,3456]{1,0:T(8,128)(2,1)S(1)}, bf16[64,3456]{1,0:T(8,128)(2,1)S(1)}, u32[]{:S(2)}, u32[]{:S(2)}) collective-permute-start(bf16[64,3456]{1,0:T(8,128)(2,1)S(1)} %shard_map.247.refs_4_), channel_id=1, source_target_pairs={{0,4},{2,6},{4,0},{6,2},{1,5},{3,7},{5,1},{7,3},{8,12},{10,14},{12... | collective-permute-start | bytes 1327112 | tf_op jit(solution)/shard_map/ppermute | solution.py:19
  38.1 10.5 %collective-permute-start.5 = (bf16[64,3456]{1,0:T(8,128)(2,1)S(1)}, bf16[64,3456]{1,0:T(8,128)(2,1)S(1)}, u32[]{:S(2)}, u32[]{:S(2)}) collective-permute-start(bf16[64,3456]{1,0:T(8,128)(2,1)S(1)} %shard_map.248), channel_id=1, source_target_pairs={{0,8},{8,0},{16,24},{24,16},{1,9},{9,1},{17,25},{25,17},{2,10},{10... | collective-permute-start | bytes 1327112 | tf_op jit(solution)/shard_map/ppermute | solution.py:19
  38.2 12.8 %collective-permute-start.9 = (bf16[64,3456]{1,0:T(8,128)(2,1)S(1)}, bf16[64,3456]{1,0:T(8,128)(2,1)S(1)}, u32[]{:S(2)}, u32[]{:S(2)}) collective-permute-start(bf16[64,3456]{1,0:T(8,128)(2,1)S(1)} %collective-permute-done.3.refs_0_.refs_5_), channel_id=1, source_target_pairs={{0,4},{2,6},{4,0},{6,2},{1,5},{3,7},{5,1},{7,3},{8,12},{10,14},{12... | collective-permute-start | bytes 1327112 | tf_op jit(solution)/shard_map/ppermute | solution.py:19
  40.0 11.0 %collective-permute-start.7 = (bf16[64,3456]{1,0:T(8,128)(2,1)S(1)}, bf16[64,3456]{1,0:T(8,128)(2,1)S(1)}, u32[]{:S(2)}, u32[]{:S(2)}) collective-permute-start(bf16[64,3456]{1,0:T(8,128)(2,1)S(1)} %collective-permute-done.3.refs_0_.refs_5_), channel_id=1, source_target_pairs={{0,2},{2,0},{4,6},{6,4},{1,3},{3,1},{5,7},{7,5},{8,10},{10,8},{12,... | collective-permute-start | bytes 1327112 | tf_op jit(solution)/shard_map/ppermute | solution.py:19
  40.0 11.6 %collective-permute-start.6 = (bf16[64,3456]{1,0:T(8,128)(2,1)S(1)}, bf16[64,3456]{1,0:T(8,128)(2,1)S(1)}, u32[]{:S(2)}, u32[]{:S(2)}) collective-permute-start(bf16[64,3456]{1,0:T(8,128)(2,1)S(1)} %shard_map.247.refs_4_), channel_id=1, source_target_pairs={{0,2},{2,0},{4,6},{6,4},{1,3},{3,1},{5,7},{7,5},{8,10},{10,8},{12,... | collective-permute-start | bytes 1327112 | tf_op jit(solution)/shard_map/ppermute | solution.py:19
  48.5 9.6 %collective-permute-start.10 = (bf16[64,3456]{1,0:T(8,128)(2,1)S(1)}, bf16[64,3456]{1,0:T(8,128)(2,1)S(1)}, u32[]{:S(2)}, u32[]{:S(2)}) collective-permute-start(bf16[64,3456]{1,0:T(8,128)(2,1)S(1)} %collective-permute-done.5.refs_6_), channel_id=1, source_target_pairs={{0,4},{2,6},{4,0},{6,2},{1,5},{3,7},{5,1},{7,3},{8,12},{10,14},{12... | collective-permute-start | bytes 1327112 | tf_op jit(solution)/shard_map/ppermute | solution.py:19
  50.0 15.8 %collective-permute-start.16 = (bf16[2,128,1024]{2,1,0:T(8,128)(2,1)S(1)}, bf16[2,128,1024]{2,1,0:T(8,128)(2,1)S(1)}, u32[]{:S(2)}, u32[]{:S(2)}) collective-permute-start(bf16[2,128,1024]{2,1,0:T(8,128)(2,1)S(1)} %collective-permute-done.2.refs_2_.refs_5_), channel_id=1, source_target_pairs={{0,1},{1,0},{2,3},{3,2},{4,5},{5,4},{6,7},{7,6},{8,9},{9,8},{10,11... | collective-permute-start | bytes 1572872 | tf_op jit(solution)/shard_map/ppermute | solution.py:19
  51.0 7.1 %collective-permute-start.12 = (bf16[64,3456]{1,0:T(8,128)(2,1)S(1)}, bf16[64,3456]{1,0:T(8,128)(2,1)S(1)}, u32[]{:S(2)}, u32[]{:S(2)}) collective-permute-start(bf16[64,3456]{1,0:T(8,128)(2,1)S(1)} %collective-permute-done.9.refs_11_), channel_id=1, source_target_pairs={{0,2},{2,0},{4,6},{6,4},{1,3},{3,1},{5,7},{7,5},{8,10},{10,8},{12,... | collective-permute-start | bytes 1327112 | tf_op jit(solution)/shard_map/ppermute | solution.py:19
  51.0 7.1 %collective-permute-start.11 = (bf16[64,3456]{1,0:T(8,128)(2,1)S(1)}, bf16[64,3456]{1,0:T(8,128)(2,1)S(1)}, u32[]{:S(2)}, u32[]{:S(2)}) collective-permute-start(bf16[64,3456]{1,0:T(8,128)(2,1)S(1)} %collective-permute-done.4.refs_1_.refs_10_), channel_id=1, source_target_pairs={{0,2},{2,0},{4,6},{6,4},{1,3},{3,1},{5,7},{7,5},{8,10},{10,8},{12,... | collective-permute-start | bytes 1327112 | tf_op jit(solution)/shard_map/ppermute | solution.py:19
  51.5 6.6 %collective-permute-start.8 = (bf16[64,3456]{1,0:T(8,128)(2,1)S(1)}, bf16[64,3456]{1,0:T(8,128)(2,1)S(1)}, u32[]{:S(2)}, u32[]{:S(2)}) collective-permute-start(bf16[64,3456]{1,0:T(8,128)(2,1)S(1)} %collective-permute-done.5.refs_6_), channel_id=1, source_target_pairs={{0,2},{2,0},{4,6},{6,4},{1,3},{3,1},{5,7},{7,5},{8,10},{10,8},{12,... | collective-permute-start | bytes 1327112 | tf_op jit(solution)/shard_map/ppermute | solution.py:19
  58.1 1.8 collective-permute-start.13
  64.7 1.2 collective-permute-start.15
  64.9 6.7 %collective-permute-start.18 = (bf16[256,1024]{1,0:T(8,128)(2,1)S(1)}, bf16[256,1024]{1,0:T(8,128)(2,1)S(1)}, u32[]{:S(2)}, u32[]{:S(2)}) collective-permute-start(bf16[256,1024]{1,0:T(8,128)(2,1)S(1)} %bitcast.21), channel_id=1, source_target_pairs={{0,2},{2,0},{4,6},{6,4},{1,3},{3,1},{5,7},{7,5},{8,10},{10,8},{12,... | collective-permute-start | bytes 1572872 | tf_op jit(solution)/shard_map/ppermute | solution.py:19
  65.3 6.3 %collective-permute-start.19 = (bf16[256,1024]{1,0:T(8,128)(2,1)S(1)}, bf16[256,1024]{1,0:T(8,128)(2,1)S(1)}, u32[]{:S(2)}, u32[]{:S(2)}) collective-permute-start(bf16[256,1024]{1,0:T(8,128)(2,1)S(1)} %bitcast.27), channel_id=1, source_target_pairs={{0,2},{2,0},{4,6},{6,4},{1,3},{3,1},{5,7},{7,5},{8,10},{10,8},{12,... | collective-permute-start | bytes 1572872 | tf_op jit(solution)/shard_map/ppermute | solution.py:19
  65.5 6.2 %collective-permute-start.20 = (bf16[2,128,1024]{2,1,0:T(8,128)(2,1)S(1)}, bf16[2,128,1024]{2,1,0:T(8,128)(2,1)S(1)}, u32[]{:S(2)}, u32[]{:S(2)}) collective-permute-start(bf16[2,128,1024]{2,1,0:T(8,128)(2,1)S(1)} %collective-permute-done.2.refs_2_.refs_5_), channel_id=1, source_target_pairs={{0,2},{2,0},{4,6},{6,4},{1,3},{3,1},{5,7},{7,5},{8,10},{10,8},{12,... | collective-permute-start | bytes 1572872 | tf_op jit(solution)/shard_map/ppermute | solution.py:19
  65.8 2.9 %collective-permute-start.14 = (bf16[1024,128]{1,0:T(8,128)(2,1)S(1)}, bf16[1024,128]{1,0:T(8,128)(2,1)S(1)}, u32[]{:S(2)}, u32[]{:S(2)}) collective-permute-start(bf16[1024,128]{1,0:T(8,128)(2,1)S(1)} %get-tuple-element.94.refs_0_), channel_id=1, source_target_pairs={{0,2},{2,0},{4,6},{6,4},{1,3},{3,1},{5,7},{7,5},{8,10},{10,8},{12,... | collective-permute-start | bytes 786440 | tf_op jit(solution)/shard_map/ppermute | solution.py:19
  66.0 5.7 %collective-permute-start.21 = (bf16[2,128,1024]{2,1,0:T(8,128)(2,1)S(1)}, bf16[2,128,1024]{2,1,0:T(8,128)(2,1)S(1)}, u32[]{:S(2)}, u32[]{:S(2)}) collective-permute-start(bf16[2,128,1024]{2,1,0:T(8,128)(2,1)S(1)} %collective-permute-done.16.refs_4_.refs_6_), channel_id=1, source_target_pairs={{0,2},{2,0},{4,6},{6,4},{1,3},{3,1},{5,7},{7,5},{8,10},{10,8},{12,... | collective-permute-start | bytes 1572872 | tf_op jit(solution)/shard_map/ppermute | solution.py:19
  70.2 8.6 %collective-permute-start.17 = (bf16[1024,128]{1,0:T(8,128)(2,1)S(1)}, bf16[1024,128]{1,0:T(8,128)(2,1)S(1)}, u32[]{:S(2)}, u32[]{:S(2)}) collective-permute-start(bf16[1024,128]{1,0:T(8,128)(2,1)S(1)} %get-tuple-element.96), channel_id=1, source_target_pairs={{0,4},{2,6},{4,0},{6,2},{1,5},{3,7},{5,1},{7,3},{8,12},{10,14},{12... | collective-permute-start | bytes 786440 | tf_op jit(solution)/shard_map/ppermute | solution.py:19
  80.7 3.7 %collective-permute-start.22 = (f32[8,256]{1,0:T(8,128)S(1)}, f32[8,256]{1,0:T(8,128)S(1)}, u32[]{:S(2)}, u32[]{:S(2)}) collective-permute-start(f32[8,256]{1,0:T(8,128)S(1)} %get-tuple-element.105.refs_0_), channel_id=1, source_target_pairs={{0,1},{1,0},{2,3},{3,2},{4,5},{5,4},{6,7},{7,6},{8,9},{9,8},{10,11... | collective-permute-start | bytes 24584 | tf_op jit(solution)/shard_map/ppermute | solution.py:19
  87.1 2.1 %collective-permute-start.24 = (bf16[1024,128]{1,0:T(8,128)(2,1)S(1)}, bf16[1024,128]{1,0:T(8,128)(2,1)S(1)}, u32[]{:S(2)}, u32[]{:S(2)}) collective-permute-start(bf16[1024,128]{1,0:T(8,128)(2,1)S(1)} %get-tuple-element.112.refs_0_), channel_id=1, source_target_pairs={{0,2},{2,0},{4,6},{6,4},{1,3},{3,1},{5,7},{7,5},{8,10},{10,8},{12,... | collective-permute-start | bytes 786440 | tf_op jit(solution)/shard_map/ppermute | solution.py:19
  87.1 7.8 %collective-permute-start.26 = (bf16[2,256,256]{2,1,0:T(8,128)(2,1)S(1)}, bf16[2,256,256]{2,1,0:T(8,128)(2,1)S(1)}, u32[]{:S(2)}, u32[]{:S(2)}) collective-permute-start(bf16[2,256,256]{2,1,0:T(8,128)(2,1)S(1)} %get-tuple-element.124), channel_id=1, source_target_pairs={{0,2},{2,0},{4,6},{6,4},{1,3},{3,1},{5,7},{7,5},{8,10},{10,8},{12,... | collective-permute-start | bytes 786440 | tf_op jit(solution)/shard_map/ppermute | solution.py:19
  87.6 9.2 %collective-permute-start.27 = (bf16[2,256,256]{2,1,0:T(8,128)(2,1)S(1)}, bf16[2,256,256]{2,1,0:T(8,128)(2,1)S(1)}, u32[]{:S(2)}, u32[]{:S(2)}) collective-permute-start(bf16[2,256,256]{2,1,0:T(8,128)(2,1)S(1)} %get-tuple-element.125), channel_id=1, source_target_pairs={{0,4},{2,6},{4,0},{6,2},{1,5},{3,7},{5,1},{7,3},{8,12},{10,14},{12... | collective-permute-start | bytes 786440 | tf_op jit(solution)/shard_map/ppermute | solution.py:19
  89.1 12.3 %collective-permute-start.28 = (bf16[2,256,256]{2,1,0:T(8,128)(2,1)S(1)}, bf16[2,256,256]{2,1,0:T(8,128)(2,1)S(1)}, u32[]{:S(2)}, u32[]{:S(2)}) collective-permute-start(bf16[2,256,256]{2,1,0:T(8,128)(2,1)S(1)} %get-tuple-element.126), channel_id=1, source_target_pairs={{0,6},{2,4},{4,2},{6,0},{1,7},{3,5},{5,3},{7,1},{8,14},{10,12},{12... | collective-permute-start | bytes 786440 | tf_op jit(solution)/shard_map/ppermute | solution.py:19
  90.5 16.6 %collective-permute-start.25 = (bf16[1024,128]{1,0:T(8,128)(2,1)S(1)}, bf16[1024,128]{1,0:T(8,128)(2,1)S(1)}, u32[]{:S(2)}, u32[]{:S(2)}) collective-permute-start(bf16[1024,128]{1,0:T(8,128)(2,1)S(1)} %get-tuple-element.113), channel_id=1, source_target_pairs={{0,4},{2,6},{4,0},{6,2},{1,5},{3,7},{5,1},{7,3},{8,12},{10,14},{12... | collective-permute-start | bytes 786440 | tf_op jit(solution)/shard_map/ppermute | solution.py:19
  109.1 13.1 %collective-permute-start.29 = (bf16[2,2,256,256]{3,2,1,0:T(8,128)(2,1)S(1)}, bf16[2,2,256,256]{3,2,1,0:T(8,128)(2,1)S(1)}, u32[]{:S(2)}, u32[]{:S(2)}) collective-permute-start(bf16[2,2,256,256]{3,2,1,0:T(8,128)(2,1)S(1)} %get-tuple-element.128.refs_19_), channel_id=1, source_target_pairs={{0,8},{8,0},{16,24},{24,16},{1,9},{9,1},{17,25},{25,17},{2,10},{10... | collective-permute-start | bytes 1572872 | tf_op jit(solution)/shard_map/ppermute | solution.py:19
  110.9 12.8 %collective-permute-start.23 = (bf16[256,1024]{1,0:T(8,128)(2,1)S(1)}, bf16[256,1024]{1,0:T(8,128)(2,1)S(1)}, u32[]{:S(2)}, u32[]{:S(2)}) collective-permute-start(bf16[256,1024]{1,0:T(8,128)(2,1)S(1)} %get-tuple-element.111), channel_id=1, source_target_pairs={{0,1},{1,0},{2,3},{3,2},{4,5},{5,4},{6,7},{7,6},{8,9},{9,8},{10,11... | collective-permute-start | bytes 1572872 | tf_op jit(solution)/shard_map/ppermute | solution.py:19
  118.1 8.9 %collective-permute-start.34 = (bf16[272,384]{1,0:T(8,128)(2,1)S(1)}, bf16[272,384]{1,0:T(8,128)(2,1)S(1)}, u32[]{:S(2)}, u32[]{:S(2)}) collective-permute-start(bf16[272,384]{1,0:T(8,128)(2,1)S(1)} %get-tuple-element.141), channel_id=1, source_target_pairs={{0,2},{2,0},{4,6},{6,4},{1,3},{3,1},{5,7},{7,5},{8,10},{10,8},{12,... | collective-permute-start | bytes 626696 | tf_op jit(solution)/shard_map/ppermute | solution.py:19
  118.2 8.8 %collective-permute-start.35 = (bf16[272,384]{1,0:T(8,128)(2,1)S(1)}, bf16[272,384]{1,0:T(8,128)(2,1)S(1)}, u32[]{:S(2)}, u32[]{:S(2)}) collective-permute-start(bf16[272,384]{1,0:T(8,128)(2,1)S(1)} %get-tuple-element.142), channel_id=1, source_target_pairs={{0,4},{2,6},{4,0},{6,2},{1,5},{3,7},{5,1},{7,3},{8,12},{10,14},{12... | collective-permute-start | bytes 626696 | tf_op jit(solution)/shard_map/ppermute | solution.py:19
  119.7 10.1 %collective-permute-start.36 = (bf16[272,384]{1,0:T(8,128)(2,1)S(1)}, bf16[272,384]{1,0:T(8,128)(2,1)S(1)}, u32[]{:S(2)}, u32[]{:S(2)}) collective-permute-start(bf16[272,384]{1,0:T(8,128)(2,1)S(1)} %get-tuple-element.143), channel_id=1, source_target_pairs={{0,6},{2,4},{4,2},{6,0},{1,7},{3,5},{5,3},{7,1},{8,14},{10,12},{12... | collective-permute-start | bytes 626696 | tf_op jit(solution)/shard_map/ppermute | solution.py:19
  125.9 18.2 %collective-permute-start.30 = (bf16[256,1024]{1,0:T(8,128)(2,1)S(1)}, bf16[256,1024]{1,0:T(8,128)(2,1)S(1)}, u32[]{:S(2)}, u32[]{:S(2)}) collective-permute-start(bf16[256,1024]{1,0:T(8,128)(2,1)S(1)} %get-tuple-element.137), channel_id=1, source_target_pairs={{0,1},{1,0},{2,3},{3,2},{4,5},{5,4},{6,7},{7,6},{8,9},{9,8},{10,11... | collective-permute-start | bytes 1572872 | tf_op jit(solution)/shard_map/ppermute | solution.py:19
  126.9 2.8 %collective-permute-start.33 = (f32[8,1024]{1,0:T(8,128)S(1)}, f32[8,1024]{1,0:T(8,128)S(1)}, u32[]{:S(2)}, u32[]{:S(2)}) collective-permute-start(f32[8,1024]{1,0:T(8,128)S(1)} %get-tuple-element.139.refs_0_), channel_id=1, source_target_pairs={{0,2},{2,0},{4,6},{6,4},{1,3},{3,1},{5,7},{7,5},{8,10},{10,8},{12,... | collective-permute-start | bytes 98312 | tf_op jit(solution)/shard_map/ppermute | solution.py:19
  132.2 17.3 %collective-permute-start.39 = (bf16[2,1,384,256]{3,2,1,0:T(8,128)(2,1)S(1)}, bf16[2,1,384,256]{3,2,1,0:T(8,128)(2,1)S(1)}, u32[]{:S(2)}, u32[]{:S(2)}) collective-permute-start(bf16[2,1,384,256]{3,2,1,0:T(8,128)(2,1)S(1)} %get-tuple-element.146), channel_id=1, source_target_pairs={{0,8},{8,0},{16,24},{24,16},{1,9},{9,1},{17,25},{25,17},{2,10},{10... | collective-permute-start | bytes 1179656 | tf_op jit(solution)/shard_map/ppermute | solution.py:19
  132.7 19.3 %collective-permute-start.43 = (bf16[1,2,256,256]{3,2,1,0:T(8,128)(2,1)S(1)}, bf16[1,2,256,256]{3,2,1,0:T(8,128)(2,1)S(1)}, u32[]{:S(2)}, u32[]{:S(2)}) collective-permute-start(bf16[1,2,256,256]{3,2,1,0:T(8,128)(2,1)S(1)} %get-tuple-element.135.refs_7_), channel_id=1, source_target_pairs={{0,16},{8,24},{16,0},{24,8},{1,17},{9,25},{17,1},{25,9},{2,18},{10... | collective-permute-start | bytes 786440 | tf_op jit(solution)/shard_map/ppermute | solution.py:19
  135.3 3.6 %collective-permute-start.31 = (bf16[16,1024]{1,0:T(8,128)(2,1)S(1)}, bf16[16,1024]{1,0:T(8,128)(2,1)S(1)}, u32[]{:S(2)}, u32[]{:S(2)}) collective-permute-start(bf16[16,1024]{1,0:T(8,128)(2,1)S(1)} %get-tuple-element.138), channel_id=1, source_target_pairs={{2,0},{4,2},{6,4},{3,1},{5,3},{7,5},{10,8},{12,10},{14,12},{11,9},... | collective-permute-start | bytes 98312 | tf_op jit(solution)/shard_map/ppermute | solution.py:1042
  136.6 4.8 %collective-permute-start.37 = (f32[8,1024]{1,0:T(8,128)S(1)}, f32[8,1024]{1,0:T(8,128)S(1)}, u32[]{:S(2)}, u32[]{:S(2)}) collective-permute-start(f32[8,1024]{1,0:T(8,128)S(1)} %get-tuple-element.144.refs_0_), channel_id=1, source_target_pairs={{0,4},{2,6},{4,0},{6,2},{1,5},{3,7},{5,1},{7,3},{8,12},{10,14},{12... | collective-permute-start | bytes 98312 | tf_op jit(solution)/shard_map/ppermute | solution.py:19
  139.0 5.1 %collective-permute-start.32 = (bf16[16,1024]{1,0:T(8,128)(2,1)S(1)}, bf16[16,1024]{1,0:T(8,128)(2,1)S(1)}, u32[]{:S(2)}, u32[]{:S(2)}) collective-permute-start(bf16[16,1024]{1,0:T(8,128)(2,1)S(1)} %collective-permute-done.31.refs_2_), channel_id=1, source_target_pairs={{0,1},{1,0},{2,3},{3,2},{4,5},{5,4},{6,7},{7,6},{8,9},{9,8},{10,11... | collective-permute-start | bytes 98312 | tf_op jit(solution)/shard_map/ppermute | solution.py:19
  142.0 4.1 %collective-permute-start.38 = (f32[8,1024]{1,0:T(8,128)S(1)}, f32[8,1024]{1,0:T(8,128)S(1)}, u32[]{:S(2)}, u32[]{:S(2)}) collective-permute-start(f32[8,1024]{1,0:T(8,128)S(1)} %shard_map.264.refs_0_), channel_id=1, source_target_pairs={{0,1},{1,0},{2,3},{3,2},{4,5},{5,4},{6,7},{7,6},{8,9},{9,8},{10,11... | collective-permute-start | bytes 98312 | tf_op jit(solution)/shard_map/ppermute | solution.py:19
  151.4 11.6 %collective-permute-start.41 = (bf16[1,1,384,256]{3,2,1,0:T(8,128)(2,1)S(1)}, bf16[1,1,384,256]{3,2,1,0:T(8,128)(2,1)S(1)}, u32[]{:S(2)}, u32[]{:S(2)}) collective-permute-start(bf16[1,1,384,256]{3,2,1,0:T(8,128)(2,1)S(1)} %get-tuple-element.149), channel_id=1, source_target_pairs={{0,16},{8,24},{16,0},{24,8},{1,17},{9,25},{17,1},{25,9},{2,18},{10... | collective-permute-start | bytes 589832 | tf_op jit(solution)/shard_map/ppermute | solution.py:19
  152.6 19.3 %collective-permute-start.44 = (bf16[2,256,256]{2,1,0:T(8,128)(2,1)S(1)}, bf16[2,256,256]{2,1,0:T(8,128)(2,1)S(1)}, u32[]{:S(2)}, u32[]{:S(2)}) collective-permute-start(bf16[2,256,256]{2,1,0:T(8,128)(2,1)S(1)} %shard_map.268.refs_0_), channel_id=1, source_target_pairs={{0,2},{2,0},{4,6},{6,4},{1,3},{3,1},{5,7},{7,5},{8,10},{10,8},{12,... | collective-permute-start | bytes 786440 | tf_op jit(solution)/shard_map/ppermute | solution.py:19
  152.7 19.3 %collective-permute-start.45 = (bf16[2,256,256]{2,1,0:T(8,128)(2,1)S(1)}, bf16[2,256,256]{2,1,0:T(8,128)(2,1)S(1)}, u32[]{:S(2)}, u32[]{:S(2)}) collective-permute-start(bf16[2,256,256]{2,1,0:T(8,128)(2,1)S(1)} %shard_map.268.refs_0_), channel_id=1, source_target_pairs={{0,4},{2,6},{4,0},{6,2},{1,5},{3,7},{5,1},{7,3},{8,12},{10,14},{12... | collective-permute-start | bytes 786440 | tf_op jit(solution)/shard_map/ppermute | solution.py:19
  154.2 4.4 %collective-permute-start.40 = (f32[8,1024]{1,0:T(8,128)S(1)}, f32[8,1024]{1,0:T(8,128)S(1)}, u32[]{:S(2)}, u32[]{:S(2)}) collective-permute-start(f32[8,1024]{1,0:T(8,128)S(1)} %get-tuple-element.147.refs_0_), channel_id=1, source_target_pairs={{0,8},{8,0},{16,24},{24,16},{1,9},{9,1},{17,25},{25,17},{2,10},{10... | collective-permute-start | bytes 98312 | tf_op jit(solution)/shard_map/ppermute | solution.py:19
  156.7 21.8 %collective-permute-start.46 = (bf16[2,256,256]{2,1,0:T(8,128)(2,1)S(1)}, bf16[2,256,256]{2,1,0:T(8,128)(2,1)S(1)}, u32[]{:S(2)}, u32[]{:S(2)}) collective-permute-start(bf16[2,256,256]{2,1,0:T(8,128)(2,1)S(1)} %shard_map.268.refs_0_), channel_id=1, source_target_pairs={{0,6},{2,4},{4,2},{6,0},{1,7},{3,5},{5,3},{7,1},{8,14},{10,12},{12... | collective-permute-start | bytes 786440 | tf_op jit(solution)/shard_map/ppermute | solution.py:19
  163.6 6.2 %collective-permute-start.48 = (bf16[1,256,256]{2,1,0:T(8,128)(2,1)S(1)}, bf16[1,256,256]{2,1,0:T(8,128)(2,1)S(1)}, u32[]{:S(2)}, u32[]{:S(2)}) collective-permute-start(bf16[1,256,256]{2,1,0:T(8,128)(2,1)S(1)} %get-tuple-element.154.refs_0_), channel_id=1, source_target_pairs={{0,4},{2,6},{4,0},{6,2},{1,5},{3,7},{5,1},{7,3},{8,12},{10,14},{12... | collective-permute-start | bytes 393224 | tf_op jit(solution)/shard_map/ppermute | solution.py:19
  165.1 4.3 %collective-permute-start.47 = (bf16[1,128,256]{2,1,0:T(8,128)(2,1)S(1)}, bf16[1,128,256]{2,1,0:T(8,128)(2,1)S(1)}, u32[]{:S(2)}, u32[]{:S(2)}) collective-permute-start(bf16[1,128,256]{2,1,0:T(8,128)(2,1)S(1)} %get-tuple-element.153.refs_0_), channel_id=1, source_target_pairs={{0,1},{1,0},{2,3},{3,2},{4,5},{5,4},{6,7},{7,6},{8,9},{9,8},{10,11... | collective-permute-start | bytes 196616 | tf_op jit(solution)/shard_map/ppermute | solution.py:19
  169.4 11.4 %collective-permute-start.50 = (bf16[1,256,256]{2,1,0:T(8,128)(2,1)S(1)}, bf16[1,256,256]{2,1,0:T(8,128)(2,1)S(1)}, u32[]{:S(2)}, u32[]{:S(2)}) collective-permute-start(bf16[1,256,256]{2,1,0:T(8,128)(2,1)S(1)} %get-tuple-element.154.refs_0_), channel_id=1, source_target_pairs={{0,2},{2,0},{4,6},{6,4},{1,3},{3,1},{5,7},{7,5},{8,10},{10,8},{12,... | collective-permute-start | bytes 393224 | tf_op jit(solution)/shard_map/ppermute | solution.py:19
  170.4 6.4 %collective-permute-start.49 = (bf16[1,128,256]{2,1,0:T(8,128)(2,1)S(1)}, bf16[1,128,256]{2,1,0:T(8,128)(2,1)S(1)}, u32[]{:S(2)}, u32[]{:S(2)}) collective-permute-start(bf16[1,128,256]{2,1,0:T(8,128)(2,1)S(1)} %shard_map.269.refs_4_), channel_id=1, source_target_pairs={{0,4},{2,6},{4,0},{6,2},{1,5},{3,7},{5,1},{7,3},{8,12},{10,14},{12... | collective-permute-start | bytes 196616 | tf_op jit(solution)/shard_map/ppermute | solution.py:19
  171.9 8.9 %collective-permute-start.51 = (bf16[1,256,256]{2,1,0:T(8,128)(2,1)S(1)}, bf16[1,256,256]{2,1,0:T(8,128)(2,1)S(1)}, u32[]{:S(2)}, u32[]{:S(2)}) collective-permute-start(bf16[1,256,256]{2,1,0:T(8,128)(2,1)S(1)} %collective-permute-done.48.refs_2_), channel_id=1, source_target_pairs={{0,2},{2,0},{4,6},{6,4},{1,3},{3,1},{5,7},{7,5},{8,10},{10,8},{12,... | collective-permute-start | bytes 393224 | tf_op jit(solution)/shard_map/ppermute | solution.py:19
  171.9 4.9 %collective-permute-start.42 = (f32[8,1024]{1,0:T(8,128)S(1)}, f32[8,1024]{1,0:T(8,128)S(1)}, u32[]{:S(2)}, u32[]{:S(2)}) collective-permute-start(f32[8,1024]{1,0:T(8,128)S(1)} %get-tuple-element.150.refs_0_), channel_id=1, source_target_pairs={{0,16},{8,24},{16,0},{24,8},{1,17},{9,25},{17,1},{25,9},{2,18},{10... | collective-permute-start | bytes 98312 | tf_op jit(solution)/shard_map/ppermute | solution.py:19
  176.8 4.0 %collective-permute-start.52 = (bf16[1,128,256]{2,1,0:T(8,128)(2,1)S(1)}, bf16[1,128,256]{2,1,0:T(8,128)(2,1)S(1)}, u32[]{:S(2)}, u32[]{:S(2)}) collective-permute-start(bf16[1,128,256]{2,1,0:T(8,128)(2,1)S(1)} %shard_map.269.refs_4_), channel_id=1, source_target_pairs={{0,2},{2,0},{4,6},{6,4},{1,3},{3,1},{5,7},{7,5},{8,10},{10,8},{12,... | collective-permute-start | bytes 196616 | tf_op jit(solution)/shard_map/ppermute | solution.py:19
  176.8 4.0 %collective-permute-start.53 = (bf16[1,128,256]{2,1,0:T(8,128)(2,1)S(1)}, bf16[1,128,256]{2,1,0:T(8,128)(2,1)S(1)}, u32[]{:S(2)}, u32[]{:S(2)}) collective-permute-start(bf16[1,128,256]{2,1,0:T(8,128)(2,1)S(1)} %collective-permute-done.49.refs_4_.refs_6_), channel_id=1, source_target_pairs={{0,2},{2,0},{4,6},{6,4},{1,3},{3,1},{5,7},{7,5},{8,10},{10,8},{12,... | collective-permute-start | bytes 196616 | tf_op jit(solution)/shard_map/ppermute | solution.py:19
  (7 other events, 29.2 us)

commit v3 on v2

--- a/solution.py
+++ b/solution.py
@@ -680,6 +680,17 @@
         out[...] = total[7:8, i * LANES : i * LANES + out.shape[1]]
 
 
+def end_body(ctx, states, heads):
+    def body(place, *rest):
+        ins, rest = rest[: 3 * ctx + 2], rest[3 * ctx + 2 :]
+        outs, stages = rest[:12], rest[12:]
+        close_pair_body(ctx)(place, *ins[:ctx], *outs[:2], stages[0])
+        close_body(ctx, states, heads)(place, *ins[ctx : 3 * ctx], *outs[2:5], *stages[1:])
+        small_body(place, *ins[3 * ctx :], *outs[5:])
+
+    return body
+
+
 def output_body(place, half_out, branch, out):
     out[...] = (half_out[...] + branch[...].astype(F32)).astype(LOW)
 
@@ -1111,30 +1122,26 @@
         mib=12,
         deps=[last_all[2]],
     )
-    smalls = launch(
-        small_body,
-        [
-            ((1, width), F32),
-            ((taps, states), F32),
-            ((taps, inner), F32),
-            ((1, inner), F32),
-            *[((1, heads), F32)] * 3,
-        ],
-        place,
+    pair_outs = [((shard, inner), F32), ((inner, out_proj.shape[1]), F32)]
+    first_outs = [((shard, inner), F32), ((shard, states), F32), ((heads, shard), F32)]
+    small_outs = [((1, width), F32), ((taps, states), F32), ((taps, inner), F32), ((1, inner), F32)]
+    small_outs += [((1, heads), F32)] * 3
+    grad_gate, grad_out, grad_x, grad_bc, grad_dt, *smalls = launch(
+        end_body(ctx, states, heads),
+        pair_outs + first_outs + small_outs,
+        place,
+        *pair_all,
+        *first_all,
+        *last_all,
         tally,
         swap(tally, "fsdp", fsdp_high[-1]),
-        mib=2,
-    )
-    grad_x, grad_bc, grad_dt = launch(
-        close_body(ctx, states, heads),
-        [((shard, inner), F32), ((shard, states), F32), ((heads, shard), F32)],
-        place,
-        *first_all,
-        *last_all,
-        scratch=[((ctx, w, shard), F32), ((r * ctx, shard), F32)],
-        mib=12,
-    )
-
+        scratch=[
+            ((ctx, w, shard), F32),
+            ((ctx, w, shard), F32),
+            ((r * ctx, shard), F32),
+        ],
+        mib=24,
+    )
     grad_gain, bc_taps, x_taps, grad_gated, grad_bias, grad_a, grad_skip = smalls
     return (
         block_output[None],

time: 183 us -> 183 us (level)
  Pallas kernels: 50.6 us -> 48.1 us
  waiting for transfers between devices: 80.7 us -> 83 us
    pallas_call x27 -> x25, Pallas kernels: 50.6 us -> 48.1 us  [launch(): pl.pallas_call(run, out_shape=[jax.ShapeDtypeStruct(s, d) for s, d in out...]
    ppermute x52, waiting for transfers between devices: 80.7 us -> 83 us  [swap(): return lax.ppermute(block, axis, [(i, i ^ bits) for i in range(count)])]
  transfers between devices with their start and end apart: 54 -> 54, of which waited for: 22 -> 23; matrix products, arithmetic and copies ran while one was open for 0% -> 0% of each run, Pallas kernels for 21% -> 19%
where the time goes in v3:
time: 183 us
  waiting for transfers between devices  83 us (45%)
  starting transfers between devices  48.5 us (27%)
  Pallas kernels  48.1 us (26%)
    ppermute x52, waiting for transfers between devices, swap(): return lax.ppermute(block, axis, [(i, i ^ bits) for i in range(count)])  83 us
    pallas_call x25, Pallas kernels, launch(): pl.pallas_call(run, out_shape=[jax.ShapeDtypeStruct(s, d) for s, d in out...  48.1 us
    ppermute x52, starting transfers between devices, swap(): return lax.ppermute(block, axis, [(i, i ^ bits) for i in range(count)])  45.9 us
  transfers between devices with their start and end apart: 54, of which 23 were waited for; matrix products, arithmetic and copies ran while one was open for 0% of the time, Pallas kernels for 19%

profile of v3, /device:TPU:0, one launch (start us, length us, event | category | flops | bytes accessed | tf_op | source)
XLA Modules:
  0.0 182.7 jit_solution(11960124148116712082)
XLA Ops:
  1.3 3.0 %shard_map.245 = (bf16[64,3456]{1,0:T(8,128)(2,1)}, bf16[16,1024]{1,0:T(8,128)(2,1)}, bf16[256,128]{1,0:T(8,128)(2,1)}, bf16[2,128,1024]{2,1,0:T(8,128)(2,1)}) custom-call(s32[3]{0:T(128)} %pad_add_fusion.place_ref, bf16[256,1024]{1,0:T(8,128)(2,1)} %bitcast.19, bf16[256,1024]{1,0:T(8,128)(2,1)} %bitcast.26, bf16[256,1024]{1,0:T(8,128)(2,1)} %refs_1_.1, ...), custom_call_target="tpu_custom_call" | custom-call | flops 1 | bytes 1 | tf_op jit(solution)/shard_map/pallas_call | solution.py:52
  4.3 3.0 %collective-permute-start.2 = (bf16[2,128,1024]{2,1,0:T(8,128)(2,1)}, bf16[2,128,1024]{2,1,0:T(8,128)(2,1)S(1)}, u32[]{:S(2)}, u32[]{:S(2)}) collective-permute-start(bf16[2,128,1024]{2,1,0:T(8,128)(2,1)} %get-tuple-element.93), channel_id=1, source_target_pairs={{0,4},{2,6},{4,0},{6,2},{1,5},{3,7},{5,1},{7,3},{8,12},{10,14},{12... | collective-permute-start | bytes 1572872 | tf_op jit(solution)/shard_map/ppermute | solution.py:19
  7.4 1.6 collective-permute-start.1
  8.9 1.3 collective-permute-start
  10.2 2.7 %collective-permute-start.3 = (bf16[64,3456]{1,0:T(8,128)(2,1)}, bf16[64,3456]{1,0:T(8,128)(2,1)S(1)}, u32[]{:S(2)}, u32[]{:S(2)}) collective-permute-start(bf16[64,3456]{1,0:T(8,128)(2,1)} %get-tuple-element.92), channel_id=1, source_target_pairs={{0,16},{8,24},{16,0},{24,8},{1,17},{9,25},{17,1},{25,9},{2,18},{10... | collective-permute-start | bytes 1327112 | tf_op jit(solution)/shard_map/ppermute | solution.py:19
  13.0 0.8 shard_map.246.refs_1_.refs_0_
  13.7 11.8 %collective-permute-done.1.refs_0_ = bf16[64,3456]{1,0:T(8,128)(2,1)S(1)} collective-permute-done((bf16[64,3456]{1,0:T(8,128)(2,1)}, bf16[64,3456]{1,0:T(8,128)(2,1)S(1)}, u32[]{:S(2)}, u32[]{:S(2)}) %collective-permute-start.1) | collective-permute-done | bytes 442400 | tf_op jit(solution)/shard_map/ppermute | solution.py:19
  26.1 2.1 %collective-permute-start.4 = (bf16[64,3456]{1,0:T(8,128)(2,1)S(1)}, bf16[64,3456]{1,0:T(8,128)(2,1)S(1)}, u32[]{:S(2)}, u32[]{:S(2)}) collective-permute-start(bf16[64,3456]{1,0:T(8,128)(2,1)S(1)} %shard_map.247.refs_4_), channel_id=1, source_target_pairs={{0,4},{2,6},{4,0},{6,2},{1,5},{3,7},{5,1},{7,3},{8,12},{10,14},{12... | collective-permute-start | bytes 1327112 | tf_op jit(solution)/shard_map/ppermute | solution.py:19
  28.2 5.5 %collective-permute-done.3.refs_0_.refs_5_ = bf16[64,3456]{1,0:T(8,128)(2,1)S(1)} collective-permute-done((bf16[64,3456]{1,0:T(8,128)(2,1)}, bf16[64,3456]{1,0:T(8,128)(2,1)S(1)}, u32[]{:S(2)}, u32[]{:S(2)}) %collective-permute-start.3) | collective-permute-done | bytes 442400 | tf_op jit(solution)/shard_map/ppermute | solution.py:19
  33.7 3.8 %collective-permute-done.4.refs_1_.refs_10_ = bf16[64,3456]{1,0:T(8,128)(2,1)S(1)} collective-permute-done((bf16[64,3456]{1,0:T(8,128)(2,1)S(1)}, bf16[64,3456]{1,0:T(8,128)(2,1)S(1)}, u32[]{:S(2)}, u32[]{:S(2)}) %collective-permute-start.4) | collective-permute-done | bytes 442400 | tf_op jit(solution)/shard_map/ppermute | solution.py:19
  38.2 1.8 collective-permute-start.9
  40.5 8.1 %collective-permute-done.5.refs_6_ = bf16[64,3456]{1,0:T(8,128)(2,1)S(1)} collective-permute-done((bf16[64,3456]{1,0:T(8,128)(2,1)S(1)}, bf16[64,3456]{1,0:T(8,128)(2,1)S(1)}, u32[]{:S(2)}, u32[]{:S(2)}) %collective-permute-start.5) | collective-permute-done | bytes 442400 | tf_op jit(solution)/shard_map/ppermute | solution.py:19
  48.5 1.5 collective-permute-start.10
  50.0 1.0 collective-permute-start.16
  51.6 6.5 %collective-permute-done.10.refs_12_ = bf16[64,3456]{1,0:T(8,128)(2,1)S(1)} collective-permute-done((bf16[64,3456]{1,0:T(8,128)(2,1)S(1)}, bf16[64,3456]{1,0:T(8,128)(2,1)S(1)}, u32[]{:S(2)}, u32[]{:S(2)}) %collective-permute-start.10) | collective-permute-done | bytes 442400 | tf_op jit(solution)/shard_map/ppermute | solution.py:19
  58.1 1.8 collective-permute-done.13.refs_15_
  60.0 4.8 %shard_map.249 = (bf16[1024,1408]{1,0:T(8,128)(2,1)S(1)}, f32[272,1408]{1,0:T(8,128)S(1)}, f32[256,1280]{1,0:T(8,128)S(1)}, f32[256,1280]{1,0:T(8,128)S(1)}, f32...) custom-call(s32[3]{0:T(128)S(1)} %copy-done.8, ...), custom_call_target="tpu_custom_call" | custom-call | flops 1 | bytes 1 | tf_op jit(solution)/shard_map/pallas_call | solution.py:52
  66.4 2.4 %collective-permute-done.14.refs_1_ = bf16[1024,128]{1,0:T(8,128)(2,1)S(1)} collective-permute-done((bf16[1024,128]{1,0:T(8,128)(2,1)S(1)}, bf16[1024,128]{1,0:T(8,128)(2,1)S(1)}, u32[]{:S(2)}, u32[]{:S(2)}) %collective-permute-start.14) | collective-permute-done | bytes 262176 | tf_op jit(solution)/shard_map/ppermute | solution.py:19
  68.7 1.4 shard_map.250
  70.2 1.5 collective-permute-start.17
  71.7 3.0 %shard_map.252 = (bf16[1040,1024]{1,0:T(8,128)(2,1)S(1)}, bf16[1024,1024]{1,0:T(8,128)(2,1)S(1)}) custom-call(s32[3]{0:T(128)S(1)} %copy-done.8, f32[1,1024]{1,0:T(1,128)S(1)} %bitcast.34, bf16[256,1024]{1,0:T(8,128)(2,1)S(1)} %bitcast.22, bf16[256,1024]{1,0:T(8,128)(2,1)S(1)} %collective-permute-done.18.refs_2_, bf16[256,1024]{1,0:T(8,128)(2,1)S(1)} %bitcast.28, ...), custom_call_target="tpu_custom_call" | custom-call | flops 1 | bytes 1 | tf_op jit(solution)/shard_map/pallas_call | solution.py:52
  74.7 2.1 %shard_map.251 = (f32[256,1024]{1,0:T(8,128)S(1)}, bf16[256,1024]{1,0:T(8,128)(2,1)S(1)}, bf16[1024,1024]{1,0:T(8,128)(2,1)S(1)}, bf16[1024,1024]{1,0:T(8,128)(2,1)S(1)}) custom-call(s32[3]{0:T(128)S(1)} %copy-done.8, bf16[272,1024]{1,0:T(8,128)(2,1)S(1)} %shard_map.246.refs_1_.refs_0_, bf16[256,1024]{1,0:T(8,128)(2,1)S(1)} %bitcast.29, ...), custom_call_target="tpu_custom_call" | custom-call | flops 1 | bytes 1 | tf_op jit(solution)/shard_map/pallas_call | solution.py:52
  76.8 1.9 %collective-permute-done.17.refs_0_ = bf16[1024,128]{1,0:T(8,128)(2,1)S(1)} collective-permute-done((bf16[1024,128]{1,0:T(8,128)(2,1)S(1)}, bf16[1024,128]{1,0:T(8,128)(2,1)S(1)}, u32[]{:S(2)}, u32[]{:S(2)}) %collective-permute-start.17) | collective-permute-done | bytes 262176 | tf_op jit(solution)/shard_map/ppermute | solution.py:19
  78.8 2.0 %shard_map.253 = (bf16[1024,128]{1,0:T(8,128)(2,1)S(1)}, f32[256,1024]{1,0:T(8,128)S(1)}, f32[8,256]{1,0:T(8,128)S(1)}) custom-call(s32[3]{0:T(128)S(1)} %copy-done.8, bf16[1024,128]{1,0:T(8,128)(2,1)S(1)} %collective-permute-done.17.refs_0_, bf16[1024,128]{1,0:T(8,128)(2,1)S(1)} %get-tuple-element.97.refs_1_, f32[8,128]{1,0:T(8,128)S(1)} %get-tuple-element.98.refs_2_, ...), custom_call_target="tpu_custom_call" | custom-call | flops 1 | bytes 1 | tf_op jit(solution)/shard_map/pallas_call | solution.py:52
  80.7 1.0 collective-permute-start.22
  81.8 2.7 %collective-permute-done.22.refs_1_ = f32[8,256]{1,0:T(8,128)S(1)} collective-permute-done((f32[8,256]{1,0:T(8,128)S(1)}, f32[8,256]{1,0:T(8,128)S(1)}, u32[]{:S(2)}, u32[]{:S(2)}) %collective-permute-start.22) | collective-permute-done | bytes 8224 | tf_op jit(solution)/shard_map/ppermute | solution.py:19
  84.4 2.6 %shard_map.254 = (bf16[256,1024]{1,0:T(8,128)(2,1)S(1)}, bf16[256,1024]{1,0:T(8,128)(2,1)S(1)}, f32[256,1024]{1,0:T(8,128)S(1)}, bf16[256,1024]{1,0:T(8,128)(2,1...) custom-call(s32[3]{0:T(128)S(1)} %copy-done.8, ...), custom_call_target="tpu_custom_call" | custom-call | flops 1 | bytes 1 | tf_op jit(solution)/shard_map/pallas_call | solution.py:52
  87.6 1.5 collective-permute-start.27
  89.1 1.4 shard_map.257
  90.5 1.4 collective-permute-start.25
  92.0 3.0 %shard_map.255 = (f32[256,1024]{1,0:T(8,128)S(1)}, f32[256,256]{1,0:T(8,128)S(1)}, f32[256,1024]{1,0:T(8,128)S(1)}, bf16[256,1024]{1,0:T(8,128)(2,1)S(1)}) custom-call(s32[3]{0:T(128)S(1)} %copy-done.8, f32[256,1024]{1,0:T(8,128)S(1)} %get-tuple-element.107.refs_0_.refs_10_, f32[256,1280]{1,0:T(8,128)S(1)} %get-tuple-element.99.refs_3_.refs_2_.refs_1_.refs_5_, ...), custom_call_target="tpu_custom_call" | custom-call | flops 1 | bytes 1 | tf_op jit(solution)/shard_map/pallas_call | solution.py:52
  94.9 1.9 %collective-permute-done.27.refs_2_ = bf16[2,256,256]{2,1,0:T(8,128)(2,1)S(1)} collective-permute-done((bf16[2,256,256]{2,1,0:T(8,128)(2,1)S(1)}, bf16[2,256,256]{2,1,0:T(8,128)(2,1)S(1)}, u32[]{:S(2)}, u32[]{:S(2)}) %collective-permute-start.27) | collective-permute-done | bytes 262176 | tf_op jit(solution)/shard_map/ppermute | solution.py:19
  96.8 4.6 %collective-permute-done.28.refs_3_ = bf16[2,256,256]{2,1,0:T(8,128)(2,1)S(1)} collective-permute-done((bf16[2,256,256]{2,1,0:T(8,128)(2,1)S(1)}, bf16[2,256,256]{2,1,0:T(8,128)(2,1)S(1)}, u32[]{:S(2)}, u32[]{:S(2)}) %collective-permute-start.28) | collective-permute-done | bytes 262176 | tf_op jit(solution)/shard_map/ppermute | solution.py:19
  101.4 5.8 %collective-permute-done.25.refs_6_.refs_0_ = bf16[1024,128]{1,0:T(8,128)(2,1)S(1)} collective-permute-done((bf16[1024,128]{1,0:T(8,128)(2,1)S(1)}, bf16[1024,128]{1,0:T(8,128)(2,1)S(1)}, u32[]{:S(2)}, u32[]{:S(2)}) %collective-permute-start.25) | collective-permute-done | bytes 262176 | tf_op jit(solution)/shard_map/ppermute | solution.py:19
  107.2 2.0 %shard_map.258 = (f32[2,2,256,256]{3,2,1,0:T(8,128)S(1)}, bf16[2,2,256,256]{3,2,1,0:T(8,128)(2,1)S(1)}) custom-call(s32[3]{0:T(128)S(1)} %copy-done.8, bf16[2,256,256]{2,1,0:T(8,128)(2,1)S(1)} %get-tuple-element.123.refs_0_, bf16[2,256,256]{2,1,0:T(8,128)(2,1)S(1)} %collective-permute-done.26.refs_1_, ...), custom_call_target="tpu_custom_call" | custom-call | flops 1 | bytes 1 | tf_op jit(solution)/shard_map/pallas_call | solution.py:52
  109.1 1.7 collective-permute-start.29
  110.9 1.0 collective-permute-start.23
  111.9 6.2 %shard_map.259 = (bf16[272,1408]{1,0:T(8,128)(2,1)S(1)}, f32[8,1024]{1,0:T(8,128)S(1)}, bf16[272,384]{1,0:T(8,128)(2,1)S(1)}, bf16[272,384]{1,0:T(8,128)(2,1)S(1...) custom-call(s32[3]{0:T(128)S(1)} %copy-done.8, ...), custom_call_target="tpu_custom_call" | custom-call | flops 1 | bytes 1 | tf_op jit(solution)/shard_map/pallas_call | solution.py:52
  118.2 1.5 collective-permute-start.39
  120.0 2.2 %collective-permute-done.29.refs_1_ = bf16[2,2,256,256]{3,2,1,0:T(8,128)(2,1)S(1)} collective-permute-done((bf16[2,2,256,256]{3,2,1,0:T(8,128)(2,1)S(1)}, bf16[2,2,256,256]{3,2,1,0:T(8,128)(2,1)S(1)}, u32[]{:S(2)}, u32[]{:S(2)}) %collective-permute-start.29) | collective-permute-done | bytes 524320 | tf_op jit(solution)/shard_map/ppermute | solution.py:19
  122.9 0.7 collective-permute-done.23.refs_1_.refs_8_
  123.7 2.2 %shard_map.261 = (f32[256,1024]{1,0:T(8,128)S(1)}, bf16[256,1024]{1,0:T(8,128)(2,1)S(1)}, bf16[16,1024]{1,0:T(8,128)(2,1)S(1)}, f32[8,1024]{1,0:T(8,128)S(1)}) custom-call(s32[3]{0:T(128)S(1)} %copy-done.8, bf16[272,1408]{1,0:T(8,128)(2,1)S(1)} %get-tuple-element.129.refs_0_, bf16[256,1024]{1,0:T(8,128)(2,1)S(1)} %get-tuple-element.130.refs_1_, ...), custom_call_target="tpu_custom_call" | custom-call | flops 1 | bytes 1 | tf_op jit(solution)/shard_map/pallas_call | solution.py:52
  125.9 1.1 collective-permute-start.30
  127.0 2.8 %collective-permute-done.40.refs_5_ = bf16[272,384]{1,0:T(8,128)(2,1)S(1)} collective-permute-done((bf16[272,384]{1,0:T(8,128)(2,1)S(1)}, bf16[272,384]{1,0:T(8,128)(2,1)S(1)}, u32[]{:S(2)}, u32[]{:S(2)}) %collective-permute-start.40) | collective-permute-done | bytes 208928 | tf_op jit(solution)/shard_map/ppermute | solution.py:19
  129.8 2.5 %shard_map.264 = (f32[8,1024]{1,0:T(8,128)S(1)}, f32[2,1,384,256]{3,2,1,0:T(8,128)S(1)}, bf16[2,1,384,256]{3,2,1,0:T(8,128)(2,1)S(1)}) custom-call(s32[3]{0:T(128)S(1)} %copy-done.8, f32[8,1024]{1,0:T(8,128)S(1)} %get-tuple-element.140.refs_0_, f32[8,1024]{1,0:T(8,128)S(1)} %collective-permute-done.37.refs_1_, ...), custom_call_target="tpu_custom_call" | custom-call | flops 1 | bytes 1 | tf_op jit(solution)/shard_map/pallas_call | solution.py:52
  132.7 2.7 %collective-permute-start.33 = (bf16[1,2,256,256]{3,2,1,0:T(8,128)(2,1)S(1)}, bf16[1,2,256,256]{3,2,1,0:T(8,128)(2,1)S(1)}, u32[]{:S(2)}, u32[]{:S(2)}) collective-permute-start(bf16[1,2,256,256]{3,2,1,0:T(8,128)(2,1)S(1)} %get-tuple-element.135.refs_7_), channel_id=1, source_target_pairs={{0,16},{8,24},{16,0},{24,8},{1,17},{9,25},{17,1},{25,9},{2,18},{10... | collective-permute-start | bytes 786440 | tf_op jit(solution)/shard_map/ppermute | solution.py:19
  135.3 1.3 collective-permute-start.31
  136.6 2.3 %collective-permute-start.41 = (f32[8,1024]{1,0:T(8,128)S(1)}, f32[8,1024]{1,0:T(8,128)S(1)}, u32[]{:S(2)}, u32[]{:S(2)}) collective-permute-start(f32[8,1024]{1,0:T(8,128)S(1)} %get-tuple-element.145.refs_0_), channel_id=1, source_target_pairs={{0,4},{2,6},{4,0},{6,2},{1,5},{3,7},{5,1},{7,3},{8,12},{10,14},{12... | collective-permute-start | bytes 98312 | tf_op jit(solution)/shard_map/ppermute | solution.py:19
  139.5 2.0 %collective-permute-done.41.refs_1_ = f32[8,1024]{1,0:T(8,128)S(1)} collective-permute-done((f32[8,1024]{1,0:T(8,128)S(1)}, f32[8,1024]{1,0:T(8,128)S(1)}, u32[]{:S(2)}, u32[]{:S(2)}) %collective-permute-start.41) | collective-permute-done | bytes 32800 | tf_op jit(solution)/shard_map/ppermute | solution.py:19
  142.6 1.4 shard_map.256.refs_5_
  144.1 2.0 %shard_map.262.refs_4_ = f32[256,1024]{1,0:T(8,128)} custom-call(s32[3]{0:T(128)S(1)} %copy-done.8, f32[256,1024]{1,0:T(8,128)S(1)} %get-tuple-element.136.refs_0_, bf16[256,1024]{1,0:T(8,128)(2,1)S(1)} %collective-permute-done.30.refs_1_, bf16[16,1024]{1,0:T(8,128)(2,1)S(1)} %collective-permute-done.31.refs_2_, ...), custom_call_target="tpu_custom_call" | custom-call | flops 1 | bytes 1 | tf_op jit(solution)/shard_map/pallas_call | solution.py:52
  146.1 3.4 %collective-permute-done.43.refs_3_ = bf16[2,1,384,256]{3,2,1,0:T(8,128)(2,1)S(1)} collective-permute-done((bf16[2,1,384,256]{3,2,1,0:T(8,128)(2,1)S(1)}, bf16[2,1,384,256]{3,2,1,0:T(8,128)(2,1)S(1)}, u32[]{:S(2)}, u32[]{:S(2)}) %collective-permute-start.43) | collective-permute-done | bytes 393248 | tf_op jit(solution)/shard_map/ppermute | solution.py:19
  149.5 1.2 copy-done.2
  152.7 1.5 collective-permute-start.35
  154.2 2.5 %collective-permute-start.44 = (f32[8,1024]{1,0:T(8,128)S(1)}, f32[8,1024]{1,0:T(8,128)S(1)}, u32[]{:S(2)}, u32[]{:S(2)}) collective-permute-start(f32[8,1024]{1,0:T(8,128)S(1)} %get-tuple-element.148.refs_0_), channel_id=1, source_target_pairs={{0,8},{8,0},{16,24},{24,16},{1,9},{9,1},{17,25},{25,17},{2,10},{10... | collective-permute-start | bytes 98312 | tf_op jit(solution)/shard_map/ppermute | solution.py:19
  156.7 1.8 %collective-permute-done.44.refs_1_ = f32[8,1024]{1,0:T(8,128)S(1)} collective-permute-done((f32[8,1024]{1,0:T(8,128)S(1)}, f32[8,1024]{1,0:T(8,128)S(1)}, u32[]{:S(2)}, u32[]{:S(2)}) %collective-permute-start.44) | collective-permute-done | bytes 32800 | tf_op jit(solution)/shard_map/ppermute | solution.py:19
  158.6 4.4 %collective-permute-done.45.refs_3_ = bf16[1,1,384,256]{3,2,1,0:T(8,128)(2,1)S(1)} collective-permute-done((bf16[1,1,384,256]{3,2,1,0:T(8,128)(2,1)S(1)}, bf16[1,1,384,256]{3,2,1,0:T(8,128)(2,1)S(1)}, u32[]{:S(2)}, u32[]{:S(2)}) %collective-permute-start.45) | collective-permute-done | bytes 196640 | tf_op jit(solution)/shard_map/ppermute | solution.py:19
  163.6 1.5 collective-permute-start.47
  165.6 3.7 %collective-permute-done.49.refs_1_ = bf16[1,128,256]{2,1,0:T(8,128)(2,1)S(1)} collective-permute-done((bf16[1,128,256]{2,1,0:T(8,128)(2,1)S(1)}, bf16[1,128,256]{2,1,0:T(8,128)(2,1)S(1)}, u32[]{:S(2)}, u32[]{:S(2)}) %collective-permute-start.49) | collective-permute-done | bytes 65568 | tf_op jit(solution)/shard_map/ppermute | solution.py:19
  170.4 1.5 collective-permute-start.51
  172.5 2.3 %collective-permute-done.51.refs_10_ = bf16[1,128,256]{2,1,0:T(8,128)(2,1)S(1)} collective-permute-done((bf16[1,128,256]{2,1,0:T(8,128)(2,1)S(1)}, bf16[1,128,256]{2,1,0:T(8,128)(2,1)S(1)}, u32[]{:S(2)}, u32[]{:S(2)}) %collective-permute-start.51) | collective-permute-done | bytes 65568 | tf_op jit(solution)/shard_map/ppermute | solution.py:19
  174.7 2.4 %collective-permute-start.53 = (f32[8,1024]{1,0:T(8,128)S(1)}, f32[8,1024]{1,0:T(8,128)S(1)}, u32[]{:S(2)}, u32[]{:S(2)}) collective-permute-start(f32[8,1024]{1,0:T(8,128)S(1)} %get-tuple-element.153.refs_12_), channel_id=1, source_target_pairs={{0,16},{8,24},{16,0},{24,8},{1,17},{9,25},{17,1},{25,9},{2,18},{10... | collective-permute-start | bytes 98312 | tf_op jit(solution)/shard_map/ppermute | solution.py:19
  177.1 2.4 %collective-permute-done.53.refs_13_ = f32[8,1024]{1,0:T(8,128)S(1)} collective-permute-done((f32[8,1024]{1,0:T(8,128)S(1)}, f32[8,1024]{1,0:T(8,128)S(1)}, u32[]{:S(2)}, u32[]{:S(2)}) %collective-permute-start.53) | collective-permute-done | bytes 32800 | tf_op jit(solution)/shard_map/ppermute | solution.py:19
  179.6 2.9 %shard_map.269 = (f32[256,1024]{1,0:T(8,128)}, f32[1024,256]{1,0:T(8,128)}, f32[256,1024]{1,0:T(8,128)}, f32[256,256]{1,0:T(8,128)}, f32[16,256]{1,0:T(8,128)}, ...) custom-call(s32[3]{0:T(128)S(1)} %copy-done.8, ...), custom_call_target="tpu_custom_call" | custom-call | flops 1 | bytes 1 | tf_op jit(solution)/shard_map/pallas_call | solution.py:52
  (104 shorter events, 13.0 us)
Async XLA Ops:
  0.6 12.2 %copy-start = (bf16[1,256,1024]{2,1,0:T(8,128)(2,1)S(1)}, bf16[1,256,1024]{2,1,0:T(8,128)(2,1)}, u32[]{:S(2)}) copy-start(bf16[1,256,1024]{2,1,0:T(8,128)(2,1)} %param.14) | copy-start | bytes 1572868
  0.7 12.2 %copy-start.11 = (f32[1024]{0:T(1024)S(1)}, f32[1024]{0:T(1024)}, u32[]{:S(2)}) copy-start(f32[1024]{0:T(1024)} %param.15) | copy-start | bytes 12292
  1.3 11.6 %copy-start.8 = (s32[3]{0:T(128)S(1)}, s32[3]{0:T(128)}, u32[]{:S(2)}) copy-start(s32[3]{0:T(128)} %pad_add_fusion.place_ref) | copy-start | bytes 40
  4.3 21.2 %collective-permute-start.2 = (bf16[2,128,1024]{2,1,0:T(8,128)(2,1)}, bf16[2,128,1024]{2,1,0:T(8,128)(2,1)S(1)}, u32[]{:S(2)}, u32[]{:S(2)}) collective-permute-start(bf16[2,128,1024]{2,1,0:T(8,128)(2,1)} %get-tuple-element.93), channel_id=1, source_target_pairs={{0,4},{2,6},{4,0},{6,2},{1,5},{3,7},{5,1},{7,3},{8,12},{10,14},{12... | collective-permute-start | bytes 1572872 | tf_op jit(solution)/shard_map/ppermute | solution.py:19
  7.4 18.2 %collective-permute-start.1 = (bf16[64,3456]{1,0:T(8,128)(2,1)}, bf16[64,3456]{1,0:T(8,128)(2,1)S(1)}, u32[]{:S(2)}, u32[]{:S(2)}) collective-permute-start(bf16[64,3456]{1,0:T(8,128)(2,1)} %get-tuple-element.92), channel_id=1, source_target_pairs={{0,8},{8,0},{16,24},{24,16},{1,9},{9,1},{17,25},{25,17},{2,10},{10... | collective-permute-start | bytes 1327112 | tf_op jit(solution)/shard_map/ppermute | solution.py:19
  8.9 3.9 %collective-permute-start = (bf16[16,1024]{1,0:T(8,128)(2,1)}, bf16[16,1024]{1,0:T(8,128)(2,1)S(1)}, u32[]{:S(2)}, u32[]{:S(2)}) collective-permute-start(bf16[16,1024]{1,0:T(8,128)(2,1)} %get-tuple-element.90), channel_id=1, source_target_pairs={{0,2},{2,4},{4,6},{1,3},{3,5},{5,7},{8,10},{10,12},{12,14},{9,11},... | collective-permute-start | bytes 98312 | tf_op jit(solution)/shard_map/ppermute | solution.py:802
  10.2 23.5 %collective-permute-start.3 = (bf16[64,3456]{1,0:T(8,128)(2,1)}, bf16[64,3456]{1,0:T(8,128)(2,1)S(1)}, u32[]{:S(2)}, u32[]{:S(2)}) collective-permute-start(bf16[64,3456]{1,0:T(8,128)(2,1)} %get-tuple-element.92), channel_id=1, source_target_pairs={{0,16},{8,24},{16,0},{24,8},{1,17},{9,25},{17,1},{25,9},{2,18},{10... | collective-permute-start | bytes 1327112 | tf_op jit(solution)/shard_map/ppermute | solution.py:19
  12.9 47.0 %copy-start.3 = (bf16[256,1024]{1,0:T(8,128)(2,1)S(1)}, bf16[256,1024]{1,0:T(8,128)(2,1)}, u32[]{:S(2)}) copy-start(bf16[256,1024]{1,0:T(8,128)(2,1)} %refs_1_.1) | copy-start | bytes 1572868
  12.9 47.0 %copy-start.7 = (bf16[256,256]{1,0:T(8,128)(2,1)S(1)}, bf16[256,256]{1,0:T(8,128)(2,1)}, u32[]{:S(2)}) copy-start(bf16[256,256]{1,0:T(8,128)(2,1)} %refs_2_.4) | copy-start | bytes 393220
  12.9 47.0 %copy-start.9 = (bf16[256,128]{1,0:T(8,128)(2,1)S(1)}, bf16[256,128]{1,0:T(8,128)(2,1)}, u32[]{:S(2)}) copy-start(bf16[256,128]{1,0:T(8,128)(2,1)} %get-tuple-element.91.refs_3_) | copy-start | bytes 196612
  12.9 47.0 %copy-start.10 = (f32[4,1024]{1,0:T(4,128)S(1)}, f32[4,1024]{1,0:T(4,128)}, u32[]{:S(2)}) copy-start(f32[4,1024]{1,0:T(4,128)} %refs_15_.1) | copy-start | bytes 49156
  12.9 47.0 %copy-start.12 = (f32[4,256]{1,0:T(4,128)S(1)}, f32[4,256]{1,0:T(4,128)}, u32[]{:S(2)}) copy-start(f32[4,256]{1,0:T(4,128)} %refs_16_.3) | copy-start | bytes 12292
  13.0 47.0 %copy-start.15 = (f32[16]{0:T(128)S(1)}, f32[16]{0:T(128)}, u32[]{:S(2)}) copy-start(f32[16]{0:T(128)} %param.22) | copy-start | bytes 196
  13.0 47.0 %copy-start.16 = (f32[16]{0:T(128)S(1)}, f32[16]{0:T(128)}, u32[]{:S(2)}) copy-start(f32[16]{0:T(128)} %param.23) | copy-start | bytes 196
  26.1 11.4 %collective-permute-start.4 = (bf16[64,3456]{1,0:T(8,128)(2,1)S(1)}, bf16[64,3456]{1,0:T(8,128)(2,1)S(1)}, u32[]{:S(2)}, u32[]{:S(2)}) collective-permute-start(bf16[64,3456]{1,0:T(8,128)(2,1)S(1)} %shard_map.247.refs_4_), channel_id=1, source_target_pairs={{0,4},{2,6},{4,0},{6,2},{1,5},{3,7},{5,1},{7,3},{8,12},{10,14},{12... | collective-permute-start | bytes 1327112 | tf_op jit(solution)/shard_map/ppermute | solution.py:19
  38.1 10.5 %collective-permute-start.5 = (bf16[64,3456]{1,0:T(8,128)(2,1)S(1)}, bf16[64,3456]{1,0:T(8,128)(2,1)S(1)}, u32[]{:S(2)}, u32[]{:S(2)}) collective-permute-start(bf16[64,3456]{1,0:T(8,128)(2,1)S(1)} %shard_map.248), channel_id=1, source_target_pairs={{0,8},{8,0},{16,24},{24,16},{1,9},{9,1},{17,25},{25,17},{2,10},{10... | collective-permute-start | bytes 1327112 | tf_op jit(solution)/shard_map/ppermute | solution.py:19
  38.2 12.8 %collective-permute-start.9 = (bf16[64,3456]{1,0:T(8,128)(2,1)S(1)}, bf16[64,3456]{1,0:T(8,128)(2,1)S(1)}, u32[]{:S(2)}, u32[]{:S(2)}) collective-permute-start(bf16[64,3456]{1,0:T(8,128)(2,1)S(1)} %collective-permute-done.3.refs_0_.refs_5_), channel_id=1, source_target_pairs={{0,4},{2,6},{4,0},{6,2},{1,5},{3,7},{5,1},{7,3},{8,12},{10,14},{12... | collective-permute-start | bytes 1327112 | tf_op jit(solution)/shard_map/ppermute | solution.py:19
  40.0 11.0 %collective-permute-start.7 = (bf16[64,3456]{1,0:T(8,128)(2,1)S(1)}, bf16[64,3456]{1,0:T(8,128)(2,1)S(1)}, u32[]{:S(2)}, u32[]{:S(2)}) collective-permute-start(bf16[64,3456]{1,0:T(8,128)(2,1)S(1)} %collective-permute-done.3.refs_0_.refs_5_), channel_id=1, source_target_pairs={{0,2},{2,0},{4,6},{6,4},{1,3},{3,1},{5,7},{7,5},{8,10},{10,8},{12,... | collective-permute-start | bytes 1327112 | tf_op jit(solution)/shard_map/ppermute | solution.py:19
  40.0 11.6 %collective-permute-start.6 = (bf16[64,3456]{1,0:T(8,128)(2,1)S(1)}, bf16[64,3456]{1,0:T(8,128)(2,1)S(1)}, u32[]{:S(2)}, u32[]{:S(2)}) collective-permute-start(bf16[64,3456]{1,0:T(8,128)(2,1)S(1)} %shard_map.247.refs_4_), channel_id=1, source_target_pairs={{0,2},{2,0},{4,6},{6,4},{1,3},{3,1},{5,7},{7,5},{8,10},{10,8},{12,... | collective-permute-start | bytes 1327112 | tf_op jit(solution)/shard_map/ppermute | solution.py:19
  48.5 9.6 %collective-permute-start.10 = (bf16[64,3456]{1,0:T(8,128)(2,1)S(1)}, bf16[64,3456]{1,0:T(8,128)(2,1)S(1)}, u32[]{:S(2)}, u32[]{:S(2)}) collective-permute-start(bf16[64,3456]{1,0:T(8,128)(2,1)S(1)} %collective-permute-done.5.refs_6_), channel_id=1, source_target_pairs={{0,4},{2,6},{4,0},{6,2},{1,5},{3,7},{5,1},{7,3},{8,12},{10,14},{12... | collective-permute-start | bytes 1327112 | tf_op jit(solution)/shard_map/ppermute | solution.py:19
  50.0 15.8 %collective-permute-start.16 = (bf16[2,128,1024]{2,1,0:T(8,128)(2,1)S(1)}, bf16[2,128,1024]{2,1,0:T(8,128)(2,1)S(1)}, u32[]{:S(2)}, u32[]{:S(2)}) collective-permute-start(bf16[2,128,1024]{2,1,0:T(8,128)(2,1)S(1)} %collective-permute-done.2.refs_2_.refs_5_), channel_id=1, source_target_pairs={{0,1},{1,0},{2,3},{3,2},{4,5},{5,4},{6,7},{7,6},{8,9},{9,8},{10,11... | collective-permute-start | bytes 1572872 | tf_op jit(solution)/shard_map/ppermute | solution.py:19
  51.0 7.1 %collective-permute-start.12 = (bf16[64,3456]{1,0:T(8,128)(2,1)S(1)}, bf16[64,3456]{1,0:T(8,128)(2,1)S(1)}, u32[]{:S(2)}, u32[]{:S(2)}) collective-permute-start(bf16[64,3456]{1,0:T(8,128)(2,1)S(1)} %collective-permute-done.9.refs_11_), channel_id=1, source_target_pairs={{0,2},{2,0},{4,6},{6,4},{1,3},{3,1},{5,7},{7,5},{8,10},{10,8},{12,... | collective-permute-start | bytes 1327112 | tf_op jit(solution)/shard_map/ppermute | solution.py:19
  51.0 7.1 %collective-permute-start.11 = (bf16[64,3456]{1,0:T(8,128)(2,1)S(1)}, bf16[64,3456]{1,0:T(8,128)(2,1)S(1)}, u32[]{:S(2)}, u32[]{:S(2)}) collective-permute-start(bf16[64,3456]{1,0:T(8,128)(2,1)S(1)} %collective-permute-done.4.refs_1_.refs_10_), channel_id=1, source_target_pairs={{0,2},{2,0},{4,6},{6,4},{1,3},{3,1},{5,7},{7,5},{8,10},{10,8},{12,... | collective-permute-start | bytes 1327112 | tf_op jit(solution)/shard_map/ppermute | solution.py:19
  51.5 6.6 %collective-permute-start.8 = (bf16[64,3456]{1,0:T(8,128)(2,1)S(1)}, bf16[64,3456]{1,0:T(8,128)(2,1)S(1)}, u32[]{:S(2)}, u32[]{:S(2)}) collective-permute-start(bf16[64,3456]{1,0:T(8,128)(2,1)S(1)} %collective-permute-done.5.refs_6_), channel_id=1, source_target_pairs={{0,2},{2,0},{4,6},{6,4},{1,3},{3,1},{5,7},{7,5},{8,10},{10,8},{12,... | collective-permute-start | bytes 1327112 | tf_op jit(solution)/shard_map/ppermute | solution.py:19
  58.1 1.8 collective-permute-start.13
  64.7 1.2 collective-permute-start.15
  64.9 6.7 %collective-permute-start.18 = (bf16[256,1024]{1,0:T(8,128)(2,1)S(1)}, bf16[256,1024]{1,0:T(8,128)(2,1)S(1)}, u32[]{:S(2)}, u32[]{:S(2)}) collective-permute-start(bf16[256,1024]{1,0:T(8,128)(2,1)S(1)} %bitcast.21), channel_id=1, source_target_pairs={{0,2},{2,0},{4,6},{6,4},{1,3},{3,1},{5,7},{7,5},{8,10},{10,8},{12,... | collective-permute-start | bytes 1572872 | tf_op jit(solution)/shard_map/ppermute | solution.py:19
  65.3 6.3 %collective-permute-start.19 = (bf16[256,1024]{1,0:T(8,128)(2,1)S(1)}, bf16[256,1024]{1,0:T(8,128)(2,1)S(1)}, u32[]{:S(2)}, u32[]{:S(2)}) collective-permute-start(bf16[256,1024]{1,0:T(8,128)(2,1)S(1)} %bitcast.27), channel_id=1, source_target_pairs={{0,2},{2,0},{4,6},{6,4},{1,3},{3,1},{5,7},{7,5},{8,10},{10,8},{12,... | collective-permute-start | bytes 1572872 | tf_op jit(solution)/shard_map/ppermute | solution.py:19
  65.5 6.2 %collective-permute-start.20 = (bf16[2,128,1024]{2,1,0:T(8,128)(2,1)S(1)}, bf16[2,128,1024]{2,1,0:T(8,128)(2,1)S(1)}, u32[]{:S(2)}, u32[]{:S(2)}) collective-permute-start(bf16[2,128,1024]{2,1,0:T(8,128)(2,1)S(1)} %collective-permute-done.2.refs_2_.refs_5_), channel_id=1, source_target_pairs={{0,2},{2,0},{4,6},{6,4},{1,3},{3,1},{5,7},{7,5},{8,10},{10,8},{12,... | collective-permute-start | bytes 1572872 | tf_op jit(solution)/shard_map/ppermute | solution.py:19
  65.8 2.9 %collective-permute-start.14 = (bf16[1024,128]{1,0:T(8,128)(2,1)S(1)}, bf16[1024,128]{1,0:T(8,128)(2,1)S(1)}, u32[]{:S(2)}, u32[]{:S(2)}) collective-permute-start(bf16[1024,128]{1,0:T(8,128)(2,1)S(1)} %get-tuple-element.94.refs_0_), channel_id=1, source_target_pairs={{0,2},{2,0},{4,6},{6,4},{1,3},{3,1},{5,7},{7,5},{8,10},{10,8},{12,... | collective-permute-start | bytes 786440 | tf_op jit(solution)/shard_map/ppermute | solution.py:19
  66.0 5.7 %collective-permute-start.21 = (bf16[2,128,1024]{2,1,0:T(8,128)(2,1)S(1)}, bf16[2,128,1024]{2,1,0:T(8,128)(2,1)S(1)}, u32[]{:S(2)}, u32[]{:S(2)}) collective-permute-start(bf16[2,128,1024]{2,1,0:T(8,128)(2,1)S(1)} %collective-permute-done.16.refs_4_.refs_6_), channel_id=1, source_target_pairs={{0,2},{2,0},{4,6},{6,4},{1,3},{3,1},{5,7},{7,5},{8,10},{10,8},{12,... | collective-permute-start | bytes 1572872 | tf_op jit(solution)/shard_map/ppermute | solution.py:19
  70.2 8.6 %collective-permute-start.17 = (bf16[1024,128]{1,0:T(8,128)(2,1)S(1)}, bf16[1024,128]{1,0:T(8,128)(2,1)S(1)}, u32[]{:S(2)}, u32[]{:S(2)}) collective-permute-start(bf16[1024,128]{1,0:T(8,128)(2,1)S(1)} %get-tuple-element.96), channel_id=1, source_target_pairs={{0,4},{2,6},{4,0},{6,2},{1,5},{3,7},{5,1},{7,3},{8,12},{10,14},{12... | collective-permute-start | bytes 786440 | tf_op jit(solution)/shard_map/ppermute | solution.py:19
  80.7 3.7 %collective-permute-start.22 = (f32[8,256]{1,0:T(8,128)S(1)}, f32[8,256]{1,0:T(8,128)S(1)}, u32[]{:S(2)}, u32[]{:S(2)}) collective-permute-start(f32[8,256]{1,0:T(8,128)S(1)} %get-tuple-element.105.refs_0_), channel_id=1, source_target_pairs={{0,1},{1,0},{2,3},{3,2},{4,5},{5,4},{6,7},{7,6},{8,9},{9,8},{10,11... | collective-permute-start | bytes 24584 | tf_op jit(solution)/shard_map/ppermute | solution.py:19
  87.1 2.1 %collective-permute-start.24 = (bf16[1024,128]{1,0:T(8,128)(2,1)S(1)}, bf16[1024,128]{1,0:T(8,128)(2,1)S(1)}, u32[]{:S(2)}, u32[]{:S(2)}) collective-permute-start(bf16[1024,128]{1,0:T(8,128)(2,1)S(1)} %get-tuple-element.112.refs_0_), channel_id=1, source_target_pairs={{0,2},{2,0},{4,6},{6,4},{1,3},{3,1},{5,7},{7,5},{8,10},{10,8},{12,... | collective-permute-start | bytes 786440 | tf_op jit(solution)/shard_map/ppermute | solution.py:19
  87.1 7.8 %collective-permute-start.26 = (bf16[2,256,256]{2,1,0:T(8,128)(2,1)S(1)}, bf16[2,256,256]{2,1,0:T(8,128)(2,1)S(1)}, u32[]{:S(2)}, u32[]{:S(2)}) collective-permute-start(bf16[2,256,256]{2,1,0:T(8,128)(2,1)S(1)} %get-tuple-element.124), channel_id=1, source_target_pairs={{0,2},{2,0},{4,6},{6,4},{1,3},{3,1},{5,7},{7,5},{8,10},{10,8},{12,... | collective-permute-start | bytes 786440 | tf_op jit(solution)/shard_map/ppermute | solution.py:19
  87.6 9.2 %collective-permute-start.27 = (bf16[2,256,256]{2,1,0:T(8,128)(2,1)S(1)}, bf16[2,256,256]{2,1,0:T(8,128)(2,1)S(1)}, u32[]{:S(2)}, u32[]{:S(2)}) collective-permute-start(bf16[2,256,256]{2,1,0:T(8,128)(2,1)S(1)} %get-tuple-element.125), channel_id=1, source_target_pairs={{0,4},{2,6},{4,0},{6,2},{1,5},{3,7},{5,1},{7,3},{8,12},{10,14},{12... | collective-permute-start | bytes 786440 | tf_op jit(solution)/shard_map/ppermute | solution.py:19
  89.1 12.3 %collective-permute-start.28 = (bf16[2,256,256]{2,1,0:T(8,128)(2,1)S(1)}, bf16[2,256,256]{2,1,0:T(8,128)(2,1)S(1)}, u32[]{:S(2)}, u32[]{:S(2)}) collective-permute-start(bf16[2,256,256]{2,1,0:T(8,128)(2,1)S(1)} %get-tuple-element.126), channel_id=1, source_target_pairs={{0,6},{2,4},{4,2},{6,0},{1,7},{3,5},{5,3},{7,1},{8,14},{10,12},{12... | collective-permute-start | bytes 786440 | tf_op jit(solution)/shard_map/ppermute | solution.py:19
  90.5 16.6 %collective-permute-start.25 = (bf16[1024,128]{1,0:T(8,128)(2,1)S(1)}, bf16[1024,128]{1,0:T(8,128)(2,1)S(1)}, u32[]{:S(2)}, u32[]{:S(2)}) collective-permute-start(bf16[1024,128]{1,0:T(8,128)(2,1)S(1)} %get-tuple-element.113), channel_id=1, source_target_pairs={{0,4},{2,6},{4,0},{6,2},{1,5},{3,7},{5,1},{7,3},{8,12},{10,14},{12... | collective-permute-start | bytes 786440 | tf_op jit(solution)/shard_map/ppermute | solution.py:19
  109.1 13.1 %collective-permute-start.29 = (bf16[2,2,256,256]{3,2,1,0:T(8,128)(2,1)S(1)}, bf16[2,2,256,256]{3,2,1,0:T(8,128)(2,1)S(1)}, u32[]{:S(2)}, u32[]{:S(2)}) collective-permute-start(bf16[2,2,256,256]{3,2,1,0:T(8,128)(2,1)S(1)} %get-tuple-element.128.refs_19_), channel_id=1, source_target_pairs={{0,8},{8,0},{16,24},{24,16},{1,9},{9,1},{17,25},{25,17},{2,10},{10... | collective-permute-start | bytes 1572872 | tf_op jit(solution)/shard_map/ppermute | solution.py:19
  110.9 12.8 %collective-permute-start.23 = (bf16[256,1024]{1,0:T(8,128)(2,1)S(1)}, bf16[256,1024]{1,0:T(8,128)(2,1)S(1)}, u32[]{:S(2)}, u32[]{:S(2)}) collective-permute-start(bf16[256,1024]{1,0:T(8,128)(2,1)S(1)} %get-tuple-element.111), channel_id=1, source_target_pairs={{0,1},{1,0},{2,3},{3,2},{4,5},{5,4},{6,7},{7,6},{8,9},{9,8},{10,11... | collective-permute-start | bytes 1572872 | tf_op jit(solution)/shard_map/ppermute | solution.py:19
  118.1 8.9 %collective-permute-start.38 = (bf16[272,384]{1,0:T(8,128)(2,1)S(1)}, bf16[272,384]{1,0:T(8,128)(2,1)S(1)}, u32[]{:S(2)}, u32[]{:S(2)}) collective-permute-start(bf16[272,384]{1,0:T(8,128)(2,1)S(1)} %get-tuple-element.142), channel_id=1, source_target_pairs={{0,2},{2,0},{4,6},{6,4},{1,3},{3,1},{5,7},{7,5},{8,10},{10,8},{12,... | collective-permute-start | bytes 626696 | tf_op jit(solution)/shard_map/ppermute | solution.py:19
  118.2 8.8 %collective-permute-start.39 = (bf16[272,384]{1,0:T(8,128)(2,1)S(1)}, bf16[272,384]{1,0:T(8,128)(2,1)S(1)}, u32[]{:S(2)}, u32[]{:S(2)}) collective-permute-start(bf16[272,384]{1,0:T(8,128)(2,1)S(1)} %get-tuple-element.143), channel_id=1, source_target_pairs={{0,4},{2,6},{4,0},{6,2},{1,5},{3,7},{5,1},{7,3},{8,12},{10,14},{12... | collective-permute-start | bytes 626696 | tf_op jit(solution)/shard_map/ppermute | solution.py:19
  119.7 10.1 %collective-permute-start.40 = (bf16[272,384]{1,0:T(8,128)(2,1)S(1)}, bf16[272,384]{1,0:T(8,128)(2,1)S(1)}, u32[]{:S(2)}, u32[]{:S(2)}) collective-permute-start(bf16[272,384]{1,0:T(8,128)(2,1)S(1)} %get-tuple-element.144), channel_id=1, source_target_pairs={{0,6},{2,4},{4,2},{6,0},{1,7},{3,5},{5,3},{7,1},{8,14},{10,12},{12... | collective-permute-start | bytes 626696 | tf_op jit(solution)/shard_map/ppermute | solution.py:19
  125.9 18.2 %collective-permute-start.30 = (bf16[256,1024]{1,0:T(8,128)(2,1)S(1)}, bf16[256,1024]{1,0:T(8,128)(2,1)S(1)}, u32[]{:S(2)}, u32[]{:S(2)}) collective-permute-start(bf16[256,1024]{1,0:T(8,128)(2,1)S(1)} %get-tuple-element.137), channel_id=1, source_target_pairs={{0,1},{1,0},{2,3},{3,2},{4,5},{5,4},{6,7},{7,6},{8,9},{9,8},{10,11... | collective-permute-start | bytes 1572872 | tf_op jit(solution)/shard_map/ppermute | solution.py:19
  126.9 2.8 %collective-permute-start.37 = (f32[8,1024]{1,0:T(8,128)S(1)}, f32[8,1024]{1,0:T(8,128)S(1)}, u32[]{:S(2)}, u32[]{:S(2)}) collective-permute-start(f32[8,1024]{1,0:T(8,128)S(1)} %get-tuple-element.140.refs_0_), channel_id=1, source_target_pairs={{0,2},{2,0},{4,6},{6,4},{1,3},{3,1},{5,7},{7,5},{8,10},{10,8},{12,... | collective-permute-start | bytes 98312 | tf_op jit(solution)/shard_map/ppermute | solution.py:19
  132.2 17.3 %collective-permute-start.43 = (bf16[2,1,384,256]{3,2,1,0:T(8,128)(2,1)S(1)}, bf16[2,1,384,256]{3,2,1,0:T(8,128)(2,1)S(1)}, u32[]{:S(2)}, u32[]{:S(2)}) collective-permute-start(bf16[2,1,384,256]{3,2,1,0:T(8,128)(2,1)S(1)} %get-tuple-element.147), channel_id=1, source_target_pairs={{0,8},{8,0},{16,24},{24,16},{1,9},{9,1},{17,25},{25,17},{2,10},{10... | collective-permute-start | bytes 1179656 | tf_op jit(solution)/shard_map/ppermute | solution.py:19
  132.7 19.3 %collective-permute-start.33 = (bf16[1,2,256,256]{3,2,1,0:T(8,128)(2,1)S(1)}, bf16[1,2,256,256]{3,2,1,0:T(8,128)(2,1)S(1)}, u32[]{:S(2)}, u32[]{:S(2)}) collective-permute-start(bf16[1,2,256,256]{3,2,1,0:T(8,128)(2,1)S(1)} %get-tuple-element.135.refs_7_), channel_id=1, source_target_pairs={{0,16},{8,24},{16,0},{24,8},{1,17},{9,25},{17,1},{25,9},{2,18},{10... | collective-permute-start | bytes 786440 | tf_op jit(solution)/shard_map/ppermute | solution.py:19
  135.3 3.6 %collective-permute-start.31 = (bf16[16,1024]{1,0:T(8,128)(2,1)S(1)}, bf16[16,1024]{1,0:T(8,128)(2,1)S(1)}, u32[]{:S(2)}, u32[]{:S(2)}) collective-permute-start(bf16[16,1024]{1,0:T(8,128)(2,1)S(1)} %get-tuple-element.138), channel_id=1, source_target_pairs={{2,0},{4,2},{6,4},{3,1},{5,3},{7,5},{10,8},{12,10},{14,12},{11,9},... | collective-permute-start | bytes 98312 | tf_op jit(solution)/shard_map/ppermute | solution.py:1053
  136.6 4.8 %collective-permute-start.41 = (f32[8,1024]{1,0:T(8,128)S(1)}, f32[8,1024]{1,0:T(8,128)S(1)}, u32[]{:S(2)}, u32[]{:S(2)}) collective-permute-start(f32[8,1024]{1,0:T(8,128)S(1)} %get-tuple-element.145.refs_0_), channel_id=1, source_target_pairs={{0,4},{2,6},{4,0},{6,2},{1,5},{3,7},{5,1},{7,3},{8,12},{10,14},{12... | collective-permute-start | bytes 98312 | tf_op jit(solution)/shard_map/ppermute | solution.py:19
  139.0 5.1 %collective-permute-start.32 = (bf16[16,1024]{1,0:T(8,128)(2,1)S(1)}, bf16[16,1024]{1,0:T(8,128)(2,1)S(1)}, u32[]{:S(2)}, u32[]{:S(2)}) collective-permute-start(bf16[16,1024]{1,0:T(8,128)(2,1)S(1)} %collective-permute-done.31.refs_2_), channel_id=1, source_target_pairs={{0,1},{1,0},{2,3},{3,2},{4,5},{5,4},{6,7},{7,6},{8,9},{9,8},{10,11... | collective-permute-start | bytes 98312 | tf_op jit(solution)/shard_map/ppermute | solution.py:19
  142.0 4.1 %collective-permute-start.42 = (f32[8,1024]{1,0:T(8,128)S(1)}, f32[8,1024]{1,0:T(8,128)S(1)}, u32[]{:S(2)}, u32[]{:S(2)}) collective-permute-start(f32[8,1024]{1,0:T(8,128)S(1)} %shard_map.265.refs_0_), channel_id=1, source_target_pairs={{0,1},{1,0},{2,3},{3,2},{4,5},{5,4},{6,7},{7,6},{8,9},{9,8},{10,11... | collective-permute-start | bytes 98312 | tf_op jit(solution)/shard_map/ppermute | solution.py:19
  151.4 11.6 %collective-permute-start.45 = (bf16[1,1,384,256]{3,2,1,0:T(8,128)(2,1)S(1)}, bf16[1,1,384,256]{3,2,1,0:T(8,128)(2,1)S(1)}, u32[]{:S(2)}, u32[]{:S(2)}) collective-permute-start(bf16[1,1,384,256]{3,2,1,0:T(8,128)(2,1)S(1)} %get-tuple-element.150), channel_id=1, source_target_pairs={{0,16},{8,24},{16,0},{24,8},{1,17},{9,25},{17,1},{25,9},{2,18},{10... | collective-permute-start | bytes 589832 | tf_op jit(solution)/shard_map/ppermute | solution.py:19
  152.6 19.3 %collective-permute-start.34 = (bf16[2,256,256]{2,1,0:T(8,128)(2,1)S(1)}, bf16[2,256,256]{2,1,0:T(8,128)(2,1)S(1)}, u32[]{:S(2)}, u32[]{:S(2)}) collective-permute-start(bf16[2,256,256]{2,1,0:T(8,128)(2,1)S(1)} %shard_map.263.refs_0_), channel_id=1, source_target_pairs={{0,2},{2,0},{4,6},{6,4},{1,3},{3,1},{5,7},{7,5},{8,10},{10,8},{12,... | collective-permute-start | bytes 786440 | tf_op jit(solution)/shard_map/ppermute | solution.py:19
  152.7 19.3 %collective-permute-start.35 = (bf16[2,256,256]{2,1,0:T(8,128)(2,1)S(1)}, bf16[2,256,256]{2,1,0:T(8,128)(2,1)S(1)}, u32[]{:S(2)}, u32[]{:S(2)}) collective-permute-start(bf16[2,256,256]{2,1,0:T(8,128)(2,1)S(1)} %shard_map.263.refs_0_), channel_id=1, source_target_pairs={{0,4},{2,6},{4,0},{6,2},{1,5},{3,7},{5,1},{7,3},{8,12},{10,14},{12... | collective-permute-start | bytes 786440 | tf_op jit(solution)/shard_map/ppermute | solution.py:19
  154.2 4.4 %collective-permute-start.44 = (f32[8,1024]{1,0:T(8,128)S(1)}, f32[8,1024]{1,0:T(8,128)S(1)}, u32[]{:S(2)}, u32[]{:S(2)}) collective-permute-start(f32[8,1024]{1,0:T(8,128)S(1)} %get-tuple-element.148.refs_0_), channel_id=1, source_target_pairs={{0,8},{8,0},{16,24},{24,16},{1,9},{9,1},{17,25},{25,17},{2,10},{10... | collective-permute-start | bytes 98312 | tf_op jit(solution)/shard_map/ppermute | solution.py:19
  156.7 18.0 %collective-permute-start.36 = (bf16[2,256,256]{2,1,0:T(8,128)(2,1)S(1)}, bf16[2,256,256]{2,1,0:T(8,128)(2,1)S(1)}, u32[]{:S(2)}, u32[]{:S(2)}) collective-permute-start(bf16[2,256,256]{2,1,0:T(8,128)(2,1)S(1)} %shard_map.263.refs_0_), channel_id=1, source_target_pairs={{0,6},{2,4},{4,2},{6,0},{1,7},{3,5},{5,3},{7,1},{8,14},{10,12},{12... | collective-permute-start | bytes 786440 | tf_op jit(solution)/shard_map/ppermute | solution.py:19
  163.6 6.3 %collective-permute-start.47 = (bf16[1,256,256]{2,1,0:T(8,128)(2,1)S(1)}, bf16[1,256,256]{2,1,0:T(8,128)(2,1)S(1)}, u32[]{:S(2)}, u32[]{:S(2)}) collective-permute-start(bf16[1,256,256]{2,1,0:T(8,128)(2,1)S(1)} %get-tuple-element.151.refs_4_), channel_id=1, source_target_pairs={{0,4},{2,6},{4,0},{6,2},{1,5},{3,7},{5,1},{7,3},{8,12},{10,14},{12... | collective-permute-start | bytes 393224 | tf_op jit(solution)/shard_map/ppermute | solution.py:19
  165.1 4.3 %collective-permute-start.49 = (bf16[1,128,256]{2,1,0:T(8,128)(2,1)S(1)}, bf16[1,128,256]{2,1,0:T(8,128)(2,1)S(1)}, u32[]{:S(2)}, u32[]{:S(2)}) collective-permute-start(bf16[1,128,256]{2,1,0:T(8,128)(2,1)S(1)} %get-tuple-element.152.refs_0_), channel_id=1, source_target_pairs={{0,1},{1,0},{2,3},{3,2},{4,5},{5,4},{6,7},{7,6},{8,9},{9,8},{10,11... | collective-permute-start | bytes 196616 | tf_op jit(solution)/shard_map/ppermute | solution.py:19
  169.4 10.2 %collective-permute-start.46 = (bf16[1,256,256]{2,1,0:T(8,128)(2,1)S(1)}, bf16[1,256,256]{2,1,0:T(8,128)(2,1)S(1)}, u32[]{:S(2)}, u32[]{:S(2)}) collective-permute-start(bf16[1,256,256]{2,1,0:T(8,128)(2,1)S(1)} %get-tuple-element.151.refs_4_), channel_id=1, source_target_pairs={{0,2},{2,0},{4,6},{6,4},{1,3},{3,1},{5,7},{7,5},{8,10},{10,8},{12,... | collective-permute-start | bytes 393224 | tf_op jit(solution)/shard_map/ppermute | solution.py:19
  170.4 4.3 %collective-permute-start.51 = (bf16[1,128,256]{2,1,0:T(8,128)(2,1)S(1)}, bf16[1,128,256]{2,1,0:T(8,128)(2,1)S(1)}, u32[]{:S(2)}, u32[]{:S(2)}) collective-permute-start(bf16[1,128,256]{2,1,0:T(8,128)(2,1)S(1)} %shard_map.268.refs_8_), channel_id=1, source_target_pairs={{0,4},{2,6},{4,0},{6,2},{1,5},{3,7},{5,1},{7,3},{8,12},{10,14},{12... | collective-permute-start | bytes 196616 | tf_op jit(solution)/shard_map/ppermute | solution.py:19
  171.9 7.6 %collective-permute-start.48 = (bf16[1,256,256]{2,1,0:T(8,128)(2,1)S(1)}, bf16[1,256,256]{2,1,0:T(8,128)(2,1)S(1)}, u32[]{:S(2)}, u32[]{:S(2)}) collective-permute-start(bf16[1,256,256]{2,1,0:T(8,128)(2,1)S(1)} %collective-permute-done.47.refs_2_.refs_6_), channel_id=1, source_target_pairs={{0,2},{2,0},{4,6},{6,4},{1,3},{3,1},{5,7},{7,5},{8,10},{10,8},{12,... | collective-permute-start | bytes 393224 | tf_op jit(solution)/shard_map/ppermute | solution.py:19
  171.9 7.6 %collective-permute-start.50 = (bf16[1,128,256]{2,1,0:T(8,128)(2,1)S(1)}, bf16[1,128,256]{2,1,0:T(8,128)(2,1)S(1)}, u32[]{:S(2)}, u32[]{:S(2)}) collective-permute-start(bf16[1,128,256]{2,1,0:T(8,128)(2,1)S(1)} %shard_map.268.refs_8_), channel_id=1, source_target_pairs={{0,2},{2,0},{4,6},{6,4},{1,3},{3,1},{5,7},{7,5},{8,10},{10,8},{12,... | collective-permute-start | bytes 196616 | tf_op jit(solution)/shard_map/ppermute | solution.py:19
  174.7 4.8 %collective-permute-start.52 = (bf16[1,128,256]{2,1,0:T(8,128)(2,1)S(1)}, bf16[1,128,256]{2,1,0:T(8,128)(2,1)S(1)}, u32[]{:S(2)}, u32[]{:S(2)}) collective-permute-start(bf16[1,128,256]{2,1,0:T(8,128)(2,1)S(1)} %collective-permute-done.51.refs_10_), channel_id=1, source_target_pairs={{0,2},{2,0},{4,6},{6,4},{1,3},{3,1},{5,7},{7,5},{8,10},{10,8},{12,... | collective-permute-start | bytes 196616 | tf_op jit(solution)/shard_map/ppermute | solution.py:19
  174.7 4.8 %collective-permute-start.53 = (f32[8,1024]{1,0:T(8,128)S(1)}, f32[8,1024]{1,0:T(8,128)S(1)}, u32[]{:S(2)}, u32[]{:S(2)}) collective-permute-start(f32[8,1024]{1,0:T(8,128)S(1)} %get-tuple-element.153.refs_12_), channel_id=1, source_target_pairs={{0,16},{8,24},{16,0},{24,8},{1,17},{9,25},{17,1},{25,9},{2,18},{10... | collective-permute-start | bytes 98312 | tf_op jit(solution)/shard_map/ppermute | solution.py:19
  (7 other events, 29.2 us)
